TPU v7x, 32 devices: a whole 2x2x4 slice. The times are simulated.
32 devices in a mesh: dp: 16 (over z, y, core), tensor: 2 (over x).
Axes of the slice: x: 2, y: 2, z: 4, core: 2. Of those that a mesh axis runs over, the one named last changes fastest.
Arguments:
- tokens: bfloat16 [9216, 768], P('dp'), may hold values from -6 to 6
- cont_lengths: int32 [16, 2], P('dp'), may hold values from 1 to 320, 512 in all within a row
- routes: int32 [9216, 2], P('dp'), may hold values from 0 to 15, all different within a row; in each aligned block of 576 rows (0 to 575, 576 to 1151, ...) at most 92 rows name the same one
- route_gates: float32 [9216, 2], P('dp'), may hold values from 0.25 to 0.75
- w_qkv: bfloat16 [3, 768, 768], P(None, None, 'tensor'), may hold values from -0.21875 to 0.21875
- w_attn_out: bfloat16 [768, 768], P('tensor'), may hold values from -0.875 to 0.875
- norm_attn: float32 [768], replicated, may hold values from 0.5 to 1.5
- norm_ffn: float32 [768], replicated, may hold values from 0.5 to 1.5
- shared_in: bfloat16 [2, 768, 2048], P(None, None, 'tensor'), may hold values from -0.21875 to 0.21875
- shared_out: bfloat16 [2048, 768], P('tensor'), may hold values from -0.125 to 0.125
- expert_in: bfloat16 [2, 768, 32768], P(None, None, ('dp', 'tensor')), may hold values from -0.21875 to 0.21875
- expert_out: bfloat16 [32768, 768], P(('dp', 'tensor')), may hold values from -0.125 to 0.125
- cotangent: bfloat16 [9216, 768], P('dp'), may hold values from -6 to 6
Outputs:
- output: bfloat16 [9216, 768], P('dp')
- grad_tokens: bfloat16 [9216, 768], P('dp')
- grad_qkv: float32 [3, 768, 768], P(None, 'dp', 'tensor')
- grad_attn_out: float32 [768, 768], P('tensor', 'dp')
- grad_norm_attn: float32 [768], P('dp')
- grad_norm_ffn: float32 [768], P('dp')
- grad_shared_in: float32 [2, 768, 2048], P(None, 'dp', 'tensor')
- grad_shared_out: float32 [2048, 768], P('tensor', 'dp')
- grad_expert_in: float32 [2, 768, 32768], P(None, None, ('dp', 'tensor'))
- grad_expert_out: float32 [32768, 768], P(('dp', 'tensor'))
Inputs may be any that keep to these rules, and one draw needn't show every extreme that they name: `routes`: each row names 2 different experts. Among the 576 rows of one group no expert is named more than 92 times; in some groups one is named exactly 92 times. `cont_lengths`: the lengths of a group's continuations sum to 512; none has more than 320 tokens.
All inputs are finite; a program needn't handle non-finite values.
Results may differ from a plain program's by a relative error of at most 0.02.
Values may be sent and summed in bfloat16 or wider, within the bound.
A program may use at most 320 MiB of HBM per device.

v0:
```python
import jax
import jax.numpy as jnp
from jax import lax
from jax.sharding import PartitionSpec as P

HD = 64
EXPERTS = 16
TOP = 2
PROMPT = 64
CAP = 92


epsilon = 1e-06


def rms_parts(values, gain):
    factor = lax.rsqrt(jnp.mean(values * values, axis=-1, keepdims=True) + epsilon)
    return (values * factor * gain, factor)


def rms_back(values, factor, gain, incoming):
    weighted = incoming * gain
    inner = jnp.mean(weighted * values, axis=-1, keepdims=True)
    return (
        factor * weighted - values * factor * factor * factor * inner,
        jnp.sum(incoming * values * factor, axis=0),
    )


def silu_act(values):
    return values * jax.nn.sigmoid(values)


def swiglu_back(gate_up, d_act):
    sigma = jax.nn.sigmoid(gate_up[0])
    d_gate = d_act * gate_up[1] * sigma * (1.0 + gate_up[0] * (1.0 - sigma))
    d_upper = d_act * gate_up[0] * sigma
    return jnp.stack([d_gate, d_upper]).astype(jnp.bfloat16)


def group_layout(lengths, rows_here):
    row_index = jnp.arange(rows_here, dtype=jnp.int32)
    cont_ends = PROMPT + jnp.cumsum(lengths, dtype=jnp.int32)
    begins = cont_ends - lengths
    later = jnp.sum(
        (row_index[:, None] >= cont_ends[None, :]).astype(jnp.int32), axis=1, dtype=jnp.int32
    )
    segment = jnp.where(row_index < PROMPT, 0, 1 + later)
    member = (
        segment[:, None] == jnp.arange(1, lengths.shape[0] + 1, dtype=jnp.int32)[None, :]
    ).astype(jnp.int32)
    offset = jnp.sum(member * begins[None, :], axis=1, dtype=jnp.int32)
    position = jnp.where(segment == 0, row_index, PROMPT + row_index - offset)
    allowed = (row_index[None, :] <= row_index[:, None]) & (
        (segment[None, :] == 0) | (segment[None, :] == segment[:, None])
    )
    return (position, allowed)


def rope_tables(position):
    half_size = HD // 2
    inv_freq = 10000.0 ** (-jnp.arange(half_size, dtype=jnp.float32) / half_size)
    angles = position.astype(jnp.float32)[:, None] * inv_freq[None, :]
    return (jnp.cos(angles)[:, None, :], jnp.sin(angles)[:, None, :])


def rotate_pairs(values, cosine, sine):
    half_size = values.shape[-1] // 2
    front_half = values[..., :half_size]
    back_half = values[..., half_size:]
    return jnp.concatenate(
        [front_half * cosine - back_half * sine, front_half * sine + back_half * cosine], axis=-1
    )


def dispatch_plan(routes):
    flat_routes = routes.reshape(-1)
    one_hot = (flat_routes[:, None] == jnp.arange(EXPERTS, dtype=jnp.int32)[None, :]).astype(
        jnp.int32
    )
    earlier = jnp.cumsum(one_hot, axis=0, dtype=jnp.int32) - one_hot
    place_in = jnp.sum(earlier * one_hot, axis=1, dtype=jnp.int32)
    target = flat_routes * CAP + place_in
    pair_count = flat_routes.shape[0]
    slot_table = (
        jnp.full((EXPERTS * CAP,), pair_count, jnp.int32)
        .at[target]
        .set(jnp.arange(pair_count, dtype=jnp.int32))
    )
    return (target, slot_table)


def spread_rows(padded, indices, copies):
    model_width = padded.shape[1]
    picked = jnp.take(padded, indices, axis=0).reshape(EXPERTS, 1, CAP, model_width)
    return jnp.broadcast_to(picked, (EXPERTS, copies, CAP, model_width)).reshape(
        EXPERTS * copies, CAP, model_width
    )


def collect_rows(returned, target, copies, rows_here):
    model_width = returned.shape[2]
    summed = jnp.sum(returned.reshape(EXPERTS, copies, CAP, model_width), axis=1, dtype=jnp.float32)
    summed = summed.reshape(EXPERTS * CAP, model_width)
    return jnp.take(summed, target, axis=0).reshape(rows_here, TOP, model_width)


def local(
    tokens,
    cont_lengths,
    routes,
    route_gates,
    w_qkv,
    w_attn_out,
    norm_attn,
    norm_ffn,
    shared_in,
    shared_out,
    expert_in,
    expert_out,
    cotangent,
):
    rows_here = tokens.shape[0]
    model_width = tokens.shape[1]
    groups = lax.axis_size("dp")
    copies = groups // EXPERTS
    head_count = w_qkv.shape[2] // HD
    score_scale = HD ** (-0.5)
    inputs = tokens.astype(jnp.float32)
    position, allowed = group_layout(cont_lengths[0], rows_here)
    cosine, sine = rope_tables(position)
    normed_a, factor_a = rms_parts(inputs, norm_attn)
    normed_attn = normed_a.astype(jnp.bfloat16)
    projected = jnp.einsum("td,sdf->stf", normed_attn, w_qkv, preferred_element_type=jnp.float32)
    query = rotate_pairs(projected[0].reshape(rows_here, head_count, HD), cosine, sine).astype(
        jnp.bfloat16
    )
    key_rows = rotate_pairs(projected[1].reshape(rows_here, head_count, HD), cosine, sine).astype(
        jnp.bfloat16
    )
    value_rows = projected[2].reshape(rows_here, head_count, HD).astype(jnp.bfloat16)
    score = (
        jnp.einsum("qhd,khd->hqk", query, key_rows, preferred_element_type=jnp.float32)
        * score_scale
    )
    score = jnp.where(allowed[None], score, -1000000000.0)
    row_max = jnp.max(score, axis=-1, keepdims=True)
    exponent = jnp.exp(score - row_max)
    row_total = jnp.sum(exponent, axis=-1, keepdims=True)
    log_total = row_max + jnp.log(row_total)
    weights_b = (exponent / row_total).astype(jnp.bfloat16)
    attended = jnp.einsum("hqk,khd->qhd", weights_b, value_rows, preferred_element_type=jnp.float32)
    attended = attended.reshape(rows_here, head_count * HD).astype(jnp.bfloat16)
    attn_part = jnp.dot(attended, w_attn_out, preferred_element_type=jnp.float32)
    resid = inputs + lax.psum(attn_part.astype(jnp.bfloat16), "tensor").astype(jnp.float32)
    normed_f, factor_f = rms_parts(resid, norm_ffn)
    normed_ffn = normed_f.astype(jnp.bfloat16)
    gate_up = jnp.einsum("td,sdf->stf", normed_ffn, shared_in, preferred_element_type=jnp.float32)
    shared_act = (silu_act(gate_up[0]) * gate_up[1]).astype(jnp.bfloat16)
    shared_part = jnp.dot(shared_act, shared_out, preferred_element_type=jnp.float32)
    target, slot_table = dispatch_plan(routes)
    padded_rows = jnp.concatenate([normed_ffn, jnp.zeros((1, model_width), jnp.bfloat16)], axis=0)
    send_rows = spread_rows(padded_rows, slot_table // TOP, copies)
    arrived = lax.all_to_all(send_rows, "dp", split_axis=0, concat_axis=0, tiled=True)
    expert_input = arrived.reshape(groups * CAP, model_width)
    expert_gu = jnp.einsum(
        "rd,sdf->srf", expert_input, expert_in, preferred_element_type=jnp.float32
    )
    expert_act = (silu_act(expert_gu[0]) * expert_gu[1]).astype(jnp.bfloat16)
    expert_part = jnp.dot(expert_act, expert_out, preferred_element_type=jnp.float32).astype(
        jnp.bfloat16
    )
    returned = lax.all_to_all(
        expert_part.reshape(groups, CAP, model_width), "dp", split_axis=0, concat_axis=0, tiled=True
    )
    picked = collect_rows(returned, target, copies, rows_here)
    mixed = jnp.sum(route_gates[:, :, None] * picked, axis=1)
    ffn_total = lax.psum((shared_part + mixed).astype(jnp.bfloat16), "tensor").astype(jnp.float32)
    output = (resid + ffn_total).astype(jnp.bfloat16)
    upstream = cotangent.astype(jnp.float32)
    d_shared_act = jnp.einsum(
        "td,fd->tf", cotangent, shared_out, preferred_element_type=jnp.float32
    )
    d_shared_gu = swiglu_back(gate_up, d_shared_act)
    d_normed = jnp.einsum("stf,sdf->td", d_shared_gu, shared_in, preferred_element_type=jnp.float32)
    g_shared_in = jnp.einsum(
        "td,stf->sdf", normed_ffn, d_shared_gu, preferred_element_type=jnp.float32
    )
    g_shared_out = jnp.einsum(
        "tf,td->fd", shared_act, cotangent, preferred_element_type=jnp.float32
    )
    pair_grad = (
        (route_gates[:, :, None] * upstream[:, None, :])
        .reshape(rows_here * TOP, model_width)
        .astype(jnp.bfloat16)
    )
    padded_grad = jnp.concatenate([pair_grad, jnp.zeros((1, model_width), jnp.bfloat16)], axis=0)
    send_grad = spread_rows(padded_grad, slot_table, copies)
    again_rows = spread_rows(padded_rows, slot_table // TOP, copies)
    grad_arrived, rows_arrived = (
        lax.all_to_all(send_grad, "dp", split_axis=0, concat_axis=0, tiled=True),
        lax.all_to_all(again_rows, "dp", split_axis=0, concat_axis=0, tiled=True),
    )
    rows_back = rows_arrived.reshape(groups * CAP, model_width)
    d_expert_rows = grad_arrived.reshape(groups * CAP, model_width)
    back_gu = jnp.einsum("rd,sdf->srf", rows_back, expert_in, preferred_element_type=jnp.float32)
    back_act = (silu_act(back_gu[0]) * back_gu[1]).astype(jnp.bfloat16)
    d_expert_act = jnp.einsum(
        "rd,fd->rf", d_expert_rows, expert_out, preferred_element_type=jnp.float32
    )
    d_expert_gu = swiglu_back(back_gu, d_expert_act)
    d_expert_in = jnp.einsum(
        "srf,sdf->rd", d_expert_gu, expert_in, preferred_element_type=jnp.float32
    ).astype(jnp.bfloat16)
    g_expert_in = jnp.einsum(
        "rd,srf->sdf", rows_back, d_expert_gu, preferred_element_type=jnp.float32
    )
    g_expert_out = jnp.einsum(
        "rf,rd->fd", back_act, d_expert_rows, preferred_element_type=jnp.float32
    )
    d_returned = lax.all_to_all(
        d_expert_in.reshape(groups, CAP, model_width), "dp", split_axis=0, concat_axis=0, tiled=True
    )
    d_normed = d_normed + jnp.sum(collect_rows(d_returned, target, copies, rows_here), axis=1)
    d_normed = lax.psum(d_normed.astype(jnp.bfloat16), "tensor").astype(jnp.float32)
    d_resid_norm, g_norm_ffn = rms_back(resid, factor_f, norm_ffn, d_normed)
    d_resid = upstream + d_resid_norm
    d_resid_b = d_resid.astype(jnp.bfloat16)
    g_attn_out = jnp.einsum("tf,td->fd", attended, d_resid_b, preferred_element_type=jnp.float32)
    d_attended = jnp.einsum("td,fd->tf", d_resid_b, w_attn_out, preferred_element_type=jnp.float32)
    d_attended = d_attended.astype(jnp.bfloat16).reshape(rows_here, head_count, HD)
    recomputed = (
        jnp.einsum("qhd,khd->hqk", query, key_rows, preferred_element_type=jnp.float32)
        * score_scale
    )
    recomputed = jnp.where(allowed[None], recomputed, -1000000000.0)
    probs = jnp.exp(recomputed - log_total)
    probs_b = probs.astype(jnp.bfloat16)
    d_probs = jnp.einsum("qhd,khd->hqk", d_attended, value_rows, preferred_element_type=jnp.float32)
    d_value = jnp.einsum("hqk,qhd->khd", probs_b, d_attended, preferred_element_type=jnp.float32)
    inner = jnp.sum(d_probs * probs, axis=-1, keepdims=True)
    d_score = (probs * (d_probs - inner)).astype(jnp.bfloat16)
    d_query = (
        jnp.einsum("hqk,khd->qhd", d_score, key_rows, preferred_element_type=jnp.float32)
        * score_scale
    )
    d_key = (
        jnp.einsum("hqk,qhd->khd", d_score, query, preferred_element_type=jnp.float32) * score_scale
    )
    d_query = rotate_pairs(d_query, cosine, -sine).reshape(rows_here, head_count * HD)
    d_key = rotate_pairs(d_key, cosine, -sine).reshape(rows_here, head_count * HD)
    d_qkv = jnp.stack([d_query, d_key, d_value.reshape(rows_here, head_count * HD)]).astype(
        jnp.bfloat16
    )
    g_qkv = jnp.einsum("td,stf->sdf", normed_attn, d_qkv, preferred_element_type=jnp.float32)
    d_normed_attn = jnp.einsum("stf,sdf->td", d_qkv, w_qkv, preferred_element_type=jnp.float32)
    d_normed_attn = lax.psum(d_normed_attn.astype(jnp.bfloat16), "tensor").astype(jnp.float32)
    d_input_norm, g_norm_attn = rms_back(inputs, factor_a, norm_attn, d_normed_attn)
    grad_tokens = (d_resid + d_input_norm).astype(jnp.bfloat16)
    summed_all = (
        lax.psum_scatter(g_qkv, "dp", scatter_dimension=1, tiled=True),
        lax.psum_scatter(g_attn_out, "dp", scatter_dimension=1, tiled=True),
        lax.psum_scatter(g_norm_attn, "dp", scatter_dimension=0, tiled=True),
        lax.psum_scatter(g_shared_in, "dp", scatter_dimension=1, tiled=True),
        lax.psum_scatter(g_shared_out, "dp", scatter_dimension=1, tiled=True),
        lax.psum_scatter(g_norm_ffn, "dp", scatter_dimension=0, tiled=True),
    )
    return (
        output,
        grad_tokens,
        summed_all[0],
        summed_all[1],
        summed_all[2],
        summed_all[5],
        summed_all[3],
        summed_all[4],
        g_expert_in,
        g_expert_out,
    )


def solution(mesh):
    placed = (
        P("dp", None),
        P("dp", None),
        P("dp", None),
        P("dp", None),
        P(None, None, "tensor"),
        P("tensor", None),
        P(),
        P(),
        P(None, None, "tensor"),
        P("tensor", None),
        P(None, None, ("dp", "tensor")),
        P(("dp", "tensor"), None),
        P("dp", None),
    )
    return jax.shard_map(
        local,
        mesh=mesh,
        in_specs=placed,
        out_specs=(
            P("dp", None),
            P("dp", None),
            P(None, "dp", "tensor"),
            P("tensor", "dp"),
            P("dp"),
            P("dp"),
            P(None, "dp", "tensor"),
            P("tensor", "dp"),
            P(None, None, ("dp", "tensor")),
            P(("dp", "tensor"), None),
        ),
        check_vma=False,
    )
```

profile of v0, /device:TPU:0, one launch (start us, length us, event | category | flops | bytes accessed | tf_op | source)
XLA Modules:
  0.0 852.7 jit_solution(6825377094220159334)
XLA Ops:
  48.2 26.3 %all-reduce.14.cloned.1.call-done = bf16[576,768]{1,0:T(8,128)(2,1)} async-done(((bf16[576,768]{1,0:T(8,128)(2,1)}), bf16[576,768]{1,0:T(8,128)(2,1)}) %all-reduce.14.cloned.1.call-update) | async-done | bytes 884752 | tf_op jit(solution)/shard_map/psum | solution.py:155
  78.7 8.0 gather_fusion.1
  113.1 8.4 gather_fusion
  128.9 16.6 %all-to-all-done = bf16[16,92,768]{2,1,0:T(8,128)(2,1)} async-done(((bf16[16,92,768]{2,1,0:T(8,128)(2,1)}), bf16[16,92,768]{2,1,0:T(8,128)(2,1)}, u32[]{:S(2)}, u32[]{:S(2)}) %all-to-all-start) | async-done | bytes 2261024 | tf_op jit(solution)/shard_map/all_to_all | solution.py:164
  145.5 12.5 %all-to-all-start.2 = ((bf16[16,92,768]{2,1,0:T(8,128)(2,1)}), bf16[16,92,768]{2,1,0:T(8,128)(2,1)}, u32[]{:S(2)}, u32[]{:S(2)}) async-start(bf16[16,92,768]{2,1,0:T(8,128)(2,1)} %broadcast_select_fusion), calls=%async_computation.2 | async-start | bytes 4718592 | tf_op jit(solution)/shard_map/all_to_all | solution.py:201
  162.0 6.8 convolution_bitcast_fusion
  181.8 21.9 %all-to-all-done.2 = bf16[16,92,768]{2,1,0:T(8,128)(2,1)} async-done(((bf16[16,92,768]{2,1,0:T(8,128)(2,1)}), bf16[16,92,768]{2,1,0:T(8,128)(2,1)}, u32[]{:S(2)}, u32[]{:S(2)}) %all-to-all-start.2) | async-done | bytes 2261024 | tf_op jit(solution)/shard_map/all_to_all | solution.py:201
  203.7 12.3 %all-to-all-start.1 = ((bf16[16,92,768]{2,1,0:T(8,128)(2,1)}), bf16[16,92,768]{2,1,0:T(8,128)(2,1)}, u32[]{:S(2)}, u32[]{:S(2)}) async-start(bf16[16,92,768]{2,1,0:T(8,128)(2,1)} %reshape.373), calls=%async_computation.1 | async-start | bytes 4718592 | tf_op jit(solution)/shard_map/all_to_all | solution.py:173
  220.1 9.2 %fusion.22 = (bf16[1,1472,1024]{2,1,0:T(8,128)(2,1)S(1)}, bf16[1,1472,1024]{2,1,0:T(8,128)(2,1)S(1)}) fusion(f32[2,1472,1024]{2,1,0:T(8,128)} %copy-done.45, bf16[1472,768]{1,0:T(8,128)(2,1)} %reshape.377, bf16[1024,768]{1,0:T(8,128)(2,1)} %param.28), kind=kOutput, calls=%fused_computation.49 | convolution fusion | flops 2334851072 | bytes 21921792 | tf_op jit(solution)/shard_map/rd,fd->rf/dot_general | solution.py:208
  242.1 19.7 %all-to-all-done.1 = bf16[16,92,768]{2,1,0:T(8,128)(2,1)} async-done(((bf16[16,92,768]{2,1,0:T(8,128)(2,1)}), bf16[16,92,768]{2,1,0:T(8,128)(2,1)}, u32[]{:S(2)}, u32[]{:S(2)}) %all-to-all-start.1) | async-done | bytes 2261024 | tf_op jit(solution)/shard_map/all_to_all | solution.py:173
  261.8 12.3 %all-to-all-start.3 = ((bf16[16,92,768]{2,1,0:T(8,128)(2,1)}), bf16[16,92,768]{2,1,0:T(8,128)(2,1)S(1)}, u32[]{:S(2)}, u32[]{:S(2)}) async-start(bf16[16,92,768]{2,1,0:T(8,128)(2,1)} %reshape.378), calls=%async_computation.3 | async-start | bytes 4718592 | tf_op jit(solution)/shard_map/all_to_all | solution.py:221
  286.9 8.0 gather_fusion.2
  295.0 24.8 %all-to-all-done.3 = bf16[16,92,768]{2,1,0:T(8,128)(2,1)S(1)} async-done(((bf16[16,92,768]{2,1,0:T(8,128)(2,1)}), bf16[16,92,768]{2,1,0:T(8,128)(2,1)S(1)}, u32[]{:S(2)}, u32[]{:S(2)}) %all-to-all-start.3) | async-done | bytes 2261024 | tf_op jit(solution)/shard_map/all_to_all | solution.py:221
  322.3 8.1 gather_fusion.3
  368.0 29.2 %all-reduce.16.cloned.1.call-done = bf16[576,768]{1,0:T(8,128)(2,1)} async-done(((bf16[576,768]{1,0:T(8,128)(2,1)}), bf16[576,768]{1,0:T(8,128)(2,1)}) %all-reduce.16.cloned.1.call-update) | async-done | bytes 884752 | tf_op jit(solution)/shard_map/psum | solution.py:225
  415.8 9.8 %multiply_convert_fusion = bf16[6,576,576]{1,2,0:T(8,128)(2,1)} fusion(f32[6,576,576]{1,2,0:T(8,128)} %get-tuple-element.98, f32[6,576,576]{1,2,0:T(8,128)} %copy-done.2, f32[6,576]{1,0:T(8,128)S(1)} %get-tuple-element.97, f32[6,576]{1,0:T(8,128)S(1)} %log_add_fusion), kind=kLoop, calls=%fused_computation.5 | loop fusion | flops 7962624 | bytes 19934208 | tf_op jit(solution)/shard_map/convert_element_type | solution.py:242
  443.1 7.3 convolution_bitcast_fusion.1
  450.4 10.4 %copy.99 = f32[2,768,1024]{2,0,1:T(2,128)} copy(f32[2,768,1024]{1,2,0:T(8,128)} %convolution_bitcast_fusion.1) | data formatting | bytes 12582912 | tf_op jit(solution)/shard_map/td,stf->sdf/transpose | solution.py:186
  478.4 10.3 %fusion.18 = f32[1024,768]{1,0:T(8,128)} fusion(bf16[1472,768]{1,0:T(8,128)(2,1)} %reshape.377, f32[2,1472,1024]{2,1,0:T(8,128)} %copy-done.45), kind=kOutput, calls=%fused_computation.46 | convolution fusion | flops 2324299776 | bytes 17465344 | tf_op jit(solution)/shard_map/rf,rd->fd/dot_general | solution.py:218
  490.5 9.7 %fusion.23 = f32[2,768,1024]{1,2,0:T(8,128)} fusion(bf16[1472,768,1]{1,0,2:T(8,128)(2,1)} %reshape.439, bf16[1,1472,1024]{2,1,0:T(8,128)(2,1)} %copy-done.47, bf16[1,1472,1024]{2,1,0:T(8,128)(2,1)} %copy-done.46), kind=kOutput, calls=%fused_computation.51 | convolution fusion | flops 4633526272 | bytes 14581760 | tf_op jit(solution)/shard_map/rd,srf->sdf/dot_general | solution.py:215
  508.8 36.2 %all-reduce.6 = (f32[768]{0:T(1024)S(1)}, f32[768]{0:T(1024)S(1)}) all-reduce(f32[768]{0:T(1024)S(1)} %get-tuple-element.54, f32[768]{0:T(1024)S(1)} %get-tuple-element.52), channel_id=4, replica_groups=mesh['dp'=16,'tensor'=2] {'dp'}, use_global_device_ids=true, to_apply=%region_23.26.clone | all-reduce | flops 1536 | bytes 12288
  551.1 161.8 %all-reduce.18.cloned.1.call-done = (f32[3,768,384]{2,0,1:T(4,128)}, f32[2,768,1024]{2,0,1:T(2,128)}) async-done(((f32[3,768,384]{2,0,1:T(4,128)}, f32[2,768,1024]{2,0,1:T(2,128)}), (f32[3,768,384]{2,0,1:T(4,128)}, f32[2,768,1024]{2,0,1:T(2,128)})) %all-reduce.18.cloned.1.call-update) | async-done | bytes 9830416
  716.5 67.4 %reduce-scatter.5.cloned.1.call-done = f32[1024,48]{0,1:T(8,128)} async-done(((f32[1024,768]{0,1:T(8,128)}), f32[1024,48]{0,1:T(8,128)}) %reduce-scatter.5.cloned.1.call-update) | async-done | bytes 196624 | tf_op jit(solution)/shard_map/reduce_scatter | solution.py:265
  783.9 61.6 %reduce-scatter.3.cloned.1.call-done = f32[384,48]{0,1:T(8,128)} async-done(((f32[384,768]{0,1:T(8,128)}), f32[384,48]{0,1:T(8,128)}) %reduce-scatter.3.cloned.1.call-update) | async-done | bytes 73744 | tf_op jit(solution)/shard_map/reduce_scatter | solution.py:262
  (218 shorter events, 238.3 us)
Async XLA Ops:
  7.2 154.9 %copy-start = (bf16[2,768,1024]{2,1,0:T(8,128)(2,1)S(1)}, bf16[2,768,1024]{2,1,0:T(8,128)(2,1)}, u32[]{:S(2)}) copy-start(bf16[2,768,1024]{2,1,0:T(8,128)(2,1)} %param.27) | copy-start | bytes 9437188
  7.2 67.3 %all-reduce.14.cloned.1.call-start = ((), (), s32[]{:S(2)}) async-start(), calls=%async_computation.6 | async-start | bytes 1769472 | tf_op jit(solution)/shard_map/psum | solution.py:155
  35.1 41.3 %copy-start.33 = (f32[768]{0:T(1024)S(1)}, f32[768]{0:T(1024)}, u32[]{:S(2)}) copy-start(f32[768]{0:T(1024)} %param.24) | copy-start | bytes 9220
  93.9 51.5 %all-to-all-start = ((bf16[16,92,768]{2,1,0:T(8,128)(2,1)}), bf16[16,92,768]{2,1,0:T(8,128)(2,1)}, u32[]{:S(2)}, u32[]{:S(2)}) async-start(bf16[16,92,768]{2,1,0:T(8,128)(2,1)} %reshape_reshape.2), calls=%async_computation | async-start | bytes 4718592 | tf_op jit(solution)/shard_map/all_to_all | solution.py:164
  145.5 58.3 %all-to-all-start.2 = ((bf16[16,92,768]{2,1,0:T(8,128)(2,1)}), bf16[16,92,768]{2,1,0:T(8,128)(2,1)}, u32[]{:S(2)}, u32[]{:S(2)}) async-start(bf16[16,92,768]{2,1,0:T(8,128)(2,1)} %broadcast_select_fusion), calls=%async_computation.2 | async-start | bytes 4718592 | tf_op jit(solution)/shard_map/all_to_all | solution.py:201
  162.0 11.2 %copy-start.39 = (bf16[1024,768]{1,0:T(8,128)(2,1)S(1)}, bf16[1024,768]{1,0:T(8,128)(2,1)}, u32[]{:S(2)}) copy-start(bf16[1024,768]{1,0:T(8,128)(2,1)} %param.28) | copy-start | bytes 4718596
  203.7 58.0 %all-to-all-start.1 = ((bf16[16,92,768]{2,1,0:T(8,128)(2,1)}), bf16[16,92,768]{2,1,0:T(8,128)(2,1)}, u32[]{:S(2)}, u32[]{:S(2)}) async-start(bf16[16,92,768]{2,1,0:T(8,128)(2,1)} %reshape.373), calls=%async_computation.1 | async-start | bytes 4718592 | tf_op jit(solution)/shard_map/all_to_all | solution.py:173
  261.8 57.9 %all-to-all-start.3 = ((bf16[16,92,768]{2,1,0:T(8,128)(2,1)}), bf16[16,92,768]{2,1,0:T(8,128)(2,1)S(1)}, u32[]{:S(2)}, u32[]{:S(2)}) async-start(bf16[16,92,768]{2,1,0:T(8,128)(2,1)} %reshape.378), calls=%async_computation.3 | async-start | bytes 4718592 | tf_op jit(solution)/shard_map/all_to_all | solution.py:221
  274.1 123.1 %all-reduce.16.cloned.1.call-start = ((), (), s32[]{:S(2)}) async-start(), calls=%async_computation.7 | async-start | bytes 1769472 | tf_op jit(solution)/shard_map/psum | solution.py:225
  353.9 152.9 %all-reduce.20.cloned.1.call-start = ((), (), s32[]{:S(2)}) async-start(), calls=%async_computation.11 | async-start | bytes 3538944 | tf_op jit(solution)/shard_map/psum | solution.py:178
  359.4 6.5 copy-start.43
  366.0 31.2 %copy-start.4 = (bf16[576,768]{1,0:T(8,128)(2,1)S(1)}, bf16[576,768]{1,0:T(8,128)(2,1)}, u32[]{:S(2)}) copy-start(bf16[576,768]{1,0:T(8,128)(2,1)} %param.17) | copy-start | bytes 2654212
  366.0 31.2 %copy-start.8 = (bf16[576,768]{1,0:T(8,128)(2,1)S(1)}, bf16[576,768]{1,0:T(8,128)(2,1)}, u32[]{:S(2)}) copy-start(bf16[576,768]{1,0:T(8,128)(2,1)} %all-reduce.14.cloned.1.call-done) | copy-start | bytes 2654212
  400.5 88.2 %copy-start.6 = (f32[576,768]{1,0:T(8,128)}, f32[576,768]{1,0:T(8,128)S(1)}, u32[]{:S(2)}) copy-start(f32[576,768]{1,0:T(8,128)S(1)} %fusion.36) | copy-start | bytes 5308420
  415.8 9.8 %copy-start.26 = (bf16[576,6,32]{0,2,1:T(8,128)(2,1)S(1)}, bf16[576,6,32]{0,2,1:T(8,128)(2,1)}, u32[]{:S(2)}) copy-start(bf16[576,6,32]{0,2,1:T(8,128)(2,1)} %copy-done.25) | copy-start | bytes 663556
  415.8 9.8 %copy-start.28 = (bf16[576,6,32]{0,2,1:T(8,128)(2,1)S(1)}, bf16[576,6,32]{0,2,1:T(8,128)(2,1)}, u32[]{:S(2)}) copy-start(bf16[576,6,32]{0,2,1:T(8,128)(2,1)} %copy-done.27) | copy-start | bytes 663556
  443.1 269.8 %all-reduce.18.cloned.1.call-start = ((), (), s32[]{:S(2)}) async-start(), calls=%async_computation.10 | async-start | bytes 22020096
  450.4 10.4 %copy-start.31 = (bf16[1,576,384]{2,1,0:T(8,128)(2,1)S(1)}, bf16[1,576,384]{2,1,0:T(8,128)(2,1)}, u32[]{:S(2)}) copy-start(bf16[1,576,384]{2,1,0:T(8,128)(2,1)} %copy.97) | copy-start | bytes 1327108
  450.4 10.4 %copy-start.35 = (f32[576]{0:T(1024)S(1)}, f32[576]{0:T(1024)}, u32[]{:S(2)}) copy-start(f32[576]{0:T(1024)} %copy-done.34) | copy-start | bytes 6916
  450.4 10.4 %copy-start.37 = (f32[768]{0:T(1024)S(1)}, f32[768]{0:T(1024)}, u32[]{:S(2)}) copy-start(f32[768]{0:T(1024)} %param.23) | copy-start | bytes 9220
  471.7 312.2 %reduce-scatter.5.cloned.1.call-start = ((), (), s32[]{:S(2)}) async-start(), calls=%async_computation.9 | async-start | bytes 3342336 | tf_op jit(solution)/shard_map/reduce_scatter | solution.py:265
  476.5 369.0 %reduce-scatter.3.cloned.1.call-start = ((), (), s32[]{:S(2)}) async-start(), calls=%async_computation.8 | async-start | bytes 1253376 | tf_op jit(solution)/shard_map/reduce_scatter | solution.py:262
  478.3 10.3 %copy-start.20 = (bf16[6,64,576]{2,1,0:T(8,128)(2,1)S(1)}, bf16[6,64,576]{2,1,0:T(8,128)(2,1)}, u32[]{:S(2)}) copy-start(bf16[6,64,576]{2,1,0:T(8,128)(2,1)} %copy-done.19) | copy-start | bytes 1327108
  546.2 299.2 %copy-start.1 = (bf16[2,768,1024]{2,1,0:T(8,128)(2,1)S(1)}, bf16[2,768,1024]{2,1,0:T(8,128)(2,1)}, u32[]{:S(2)}) copy-start(bf16[2,768,1024]{2,1,0:T(8,128)(2,1)} %param.27) | copy-start | bytes 9437188
  (34 other events, 101.6 us)
Sparse Core Ops, SparseCore 0:
  35.3 39.1 all-reduce.13
  354.0 43.1 all-reduce.15
  443.2 55.9 all-reduce.19
  503.2 209.6 all-reduce.17
  717.6 66.2 reduce-scatter.4
  788.4 57.0 reduce-scatter.2
where the time goes:
time: 863 us; the launch traced here: 853 us
  waiting for transfers between devices  429 us (50%)
  local copies, waits for them, and re-layouts  149 us (17%)
  matrix products  113 us (13%)
  other arithmetic  65.4 us (8%)
  starting transfers between devices  43.8 us (5%)
  blocking collectives  36.2 us (4%)
  between operations  16 us (2%)
    unnamed x7, waiting for transfers between devices  162 us
    reduce_scatter x1, waiting for transfers between devices, local(): lax.psum_scatter(g_shared_out, 'dp', scatter_dimension=1, tiled=True)  67.4 us
    reduce_scatter x1, waiting for transfers between devices, local(): lax.psum_scatter(g_attn_out, 'dp', scatter_dimension=1, tiled=True)  61.6 us
    unnamed x1, blocking collectives  36.2 us
    psum x1, waiting for transfers between devices, local(): lax.psum(d_normed.astype(jnp.bfloat16), 'tensor').astype(jnp.float32)  29.2 us
    psum x1, waiting for transfers between devices, local(): lax.psum(attn_part.astype(jnp.bfloat16), 'tensor').astype(jnp.float32)  26.3 us
    all_to_all x1, waiting for transfers between devices, local(): lax.all_to_all(d_expert_in.reshape(groups, CAP, model_width), 'dp', split...  24.8 us
    unnamed x106, local copies, waits for them, and re-layouts  23.8 us
  transfers between devices with their start and end apart: 10, of which 9 were waited for; matrix products, arithmetic and copies ran while one was open for 23% of the time, Pallas kernels for 0%

commit v1 on v0

--- a/solution.py
+++ b/solution.py
@@ -1,6 +1,10 @@
+import functools
+
 import jax
 import jax.numpy as jnp
 from jax import lax
+from jax.experimental import pallas as pl
+from jax.experimental.pallas import tpu as pltpu
 from jax.sharding import PartitionSpec as P
 
 HD = 64
@@ -279,6 +283,801 @@
     )
 
 
+VMEM_BYTES = 64000 * 1024
+FOLD = 96
+MESH = pl.DeviceIdType.MESH
+VM = pl.BlockSpec(memory_space=pltpu.VMEM)
+ANY = pl.BlockSpec(memory_space=pl.ANY)
+f32 = jnp.float32
+bf16 = jnp.bfloat16
+
+
+def round_up(value, unit):
+    return (value + unit - 1) // unit * unit
+
+
+def dot(a, b):
+    return jnp.dot(a, b, preferred_element_type=f32)
+
+
+def dot_nt(a, b):
+    return lax.dot_general(a, b, (((1,), (1,)), ((), ())), preferred_element_type=f32)
+
+
+def dot_tn(a, b):
+    return lax.dot_general(a, b, (((0,), (0,)), ((), ())), preferred_element_type=f32)
+
+
+def sigmoid(values):
+    return 0.5 * jnp.tanh(0.5 * values) + 0.5
+
+
+def swap_halves(values):
+    lane = lax.broadcasted_iota(jnp.int32, values.shape, 1)
+    ahead = pltpu.roll(values, values.shape[1] - HD // 2, 1)
+    behind = pltpu.roll(values, HD // 2, 1)
+    return jnp.where(lax.rem(lane, HD) < HD // 2, ahead, behind)
+
+
+def hello(groups):
+    me, t = lax.axis_index("dp"), lax.axis_index("tensor")
+    barrier = pltpu.get_barrier_semaphore()
+
+    def greet(k, carry):
+        pl.semaphore_signal(
+            barrier, inc=1, device_id=(lax.rem(me + k, groups), t), device_id_type=MESH
+        )
+        return carry
+
+    lax.fori_loop(1, groups, greet, 0)
+    pl.semaphore_signal(barrier, inc=1, device_id=(me, 1 - t), device_id_type=MESH)
+    pl.semaphore_wait(barrier, groups)
+
+
+def fill_bias(bias, segr, segc, rows):
+    step = FOLD
+
+    def body(i, carry):
+        at = pl.ds(pl.multiple_of(i * step, step), step)
+        row = lax.broadcasted_iota(jnp.int32, (step, rows), 0) + i * step
+        col = lax.broadcasted_iota(jnp.int32, (step, rows), 1)
+        own = segc[at, :]
+        other = segr[...]
+        ok = (col <= row) & ((other == 0) | (other == own))
+        bias[at, :] = jnp.where(ok, 0.0, -1000000000.0)
+        return carry
+
+    lax.fori_loop(0, rows // step, body, 0)
+
+
+def send(src, dst, ssem, rsem, to):
+    return pltpu.make_async_remote_copy(
+        src_ref=src, dst_ref=dst, send_sem=ssem, recv_sem=rsem, device_id=to, device_id_type=MESH
+    )
+
+
+def front_kernel(
+    G, tok, na, nf, cos, sin, segr, segc, rT, gT, wqkv, wo, cot, si, so, ei, eo,
+    qkv, lse, att_own, normed_a, resid, plan, gate, part, shp, dres, gnf, gsh, gein, geout,
+    bias, att, wo2, slot, drows, normed, rows, vsi, vso, vei, veo,
+    act_s, dgu_s, act_e, dgu_e, dnsh, dnsh_r, dxs, dxr, rets, ret, dnb, turned, tall, wide, pale,
+    s_x, r_x, s_c, r_c, s_r, r_r, s_f, r_f, s_dx, r_dx, s_ret, r_ret, lsem, osem,
+):
+    T, D = tok.shape
+    HL = wqkv.shape[2]
+    F = si.shape[2]
+    C = plan.shape[0] // G
+    half = D // 2
+    scale = HD ** (-0.5)
+    me, t = lax.axis_index("dp"), lax.axis_index("tensor")
+    mine = pl.ds(pl.multiple_of(t * half, 128), half)
+    theirs = pl.ds(pl.multiple_of((1 - t) * half, 128), half)
+    partner = (me, 1 - t)
+
+    loads = [
+        pltpu.make_async_copy(a, b, lsem.at[i])
+        for i, (a, b) in enumerate(((si, vsi), (so, vso), (ei, vei), (eo, veo)))
+    ]
+    for c in loads:
+        c.start()
+    hello(G)
+    wo_copy = send(wo, wo2, s_x.at[0], r_x.at[0], partner)
+    wo_copy.start()
+
+    names = lax.broadcasted_iota(jnp.int32, (EXPERTS, T), 0)
+    picks0, picks1 = rT[0:1, :] == names, rT[1:2, :] == names
+    member = jnp.where(picks0 | picks1, 1.0, 0.0)
+    upper = jnp.where(
+        lax.broadcasted_iota(jnp.int32, (T, T), 0) < lax.broadcasted_iota(jnp.int32, (T, T), 1),
+        1.0,
+        0.0,
+    ).astype(bf16)
+    slot[...] = jnp.where(member > 0.0, dot(member.astype(bf16), upper), -1.0)
+    gate[...] = jnp.where(picks0, gT[0:1, :], 0.0) + jnp.where(picks1, gT[1:2, :], 0.0)
+
+    def row_at(k):
+        return pl.ds(pl.multiple_of(k * C, C), C)
+
+    def cot_copy(k):
+        return send(
+            part.at[row_at(k)], drows.at[row_at(k)], s_c.at[k], r_c.at[k],
+            (lax.rem(me + k, G), t),
+        )
+
+    def cot_step(k, carry):
+        e = lax.rem(me + k, G)
+        at = pl.ds(pl.multiple_of(k * C, C), C)
+        place = lax.broadcasted_iota(jnp.int32, (C, T), 0).astype(f32)
+        hit = slot[pl.ds(e, 1), :] == place
+        picked = jnp.where(hit, 1.0, 0.0).astype(bf16)
+        plan[at, :] = picked
+        weight = jnp.sum(jnp.where(hit, gate[pl.ds(e, 1), :], 0.0), axis=1, keepdims=True)
+        grad = (dot(picked, cot[...]) * weight).astype(bf16)
+        part[at, :] = grad
+
+        @pl.when(k > 0)
+        def _():
+            cot_copy(k).start()
+
+        @pl.when(k == 0)
+        def _():
+            drows[at, :] = grad
+
+        return carry
+
+    lax.fori_loop(0, G, cot_step, 0)
+
+    fill_bias(bias, segr, segc, T)
+
+    def norm_step(i, carry):
+        at = pl.ds(pl.multiple_of(i * FOLD, FOLD), FOLD)
+        x = tok[at, :].astype(f32)
+        r = lax.rsqrt(jnp.mean(x * x, axis=1, keepdims=True) + epsilon)
+        normed_a[at, :] = (x * r * na[...]).astype(bf16)
+        return carry
+
+    lax.fori_loop(0, T // FOLD, norm_step, 0)
+
+    def project(s, turned):
+        full = dot(normed_a[...], wqkv[s])
+        for j in range(HL // 128):
+            x = full[:, j * 128 : (j + 1) * 128]
+            if turned:
+                x = x * cos[...] + swap_halves(x) * sin[...]
+            qkv[s, :, j * 128 : (j + 1) * 128] = x.astype(bf16)
+
+    project(0, True)
+    project(1, True)
+    project(2, False)
+    lane = lax.broadcasted_iota(jnp.int32, (T, 128), 1)
+
+    def att_copy(j):
+        at = pl.ds(pl.multiple_of(j * 128, 128), 128)
+        return send(att_own.at[:, at], att.at[:, at], s_x.at[1 + j], r_x.at[1 + j], partner)
+
+    lse[...] = jnp.zeros_like(lse)
+
+    def attend(j, carry):
+        at = pl.ds(pl.multiple_of(j * 128, 128), 128)
+        q, k, v = qkv[0, :, at], qkv[1, :, at], qkv[2, :, at]
+        outs = []
+        for i in range(2):
+            inside = (lane < HD) if i == 0 else (lane >= HD)
+            s = dot_nt(jnp.where(inside, q, jnp.zeros_like(q)), k) * scale + bias[...]
+            top = jnp.max(s, axis=1, keepdims=True)
+            e = jnp.exp(s - top)
+            total = jnp.sum(e, axis=1, keepdims=True)
+            p = (e * (1.0 / total)).astype(bf16)
+            lse[...] = jnp.where(lane == 2 * j + i, top + jnp.log(total), lse[...])
+            outs.append(dot(p, v))
+        att_own[:, at] = jnp.where(lane < HD, outs[0], outs[1]).astype(bf16)
+        att_copy(j).start()
+        return carry
+
+    lax.fori_loop(0, HL // 128, attend, 0)
+    wo_copy.wait()
+    own_out = dot(att_own[...], wo[...])
+    for j in range(HL // 128):
+        att_copy(j).wait()
+    resid[...] = tok[...].astype(f32) + own_out + dot(att[...], wo2[...])
+
+    def norm2_step(i, carry):
+        at = pl.ds(pl.multiple_of(i * FOLD, FOLD), FOLD)
+        x = resid[at, :]
+        r = lax.rsqrt(jnp.mean(x * x, axis=1, keepdims=True) + epsilon)
+        normed[at, :] = (x * r * nf[...]).astype(bf16)
+        return carry
+
+    lax.fori_loop(0, T // FOLD, norm2_step, 0)
+
+    def row_copy(k):
+        return send(
+            rets.at[row_at(k)], rows.at[row_at(k), mine], s_r.at[k], r_r.at[k], (lax.rem(me + k, G), t)
+        )
+
+    def row_pass(k):
+        return send(
+            rows.at[row_at(k), mine], rows.at[row_at(k), mine], s_f.at[k], r_f.at[k], partner
+        )
+
+    def row_step(k, carry):
+        values = dot(plan[row_at(k), :], normed[:, mine]).astype(bf16)
+        rets[row_at(k), :] = values
+
+        @pl.when(k > 0)
+        def _():
+            row_copy(k).start()
+
+        @pl.when(k == 0)
+        def _():
+            rows[row_at(k), mine] = values
+            row_pass(k).start()
+
+        return carry
+
+    lax.fori_loop(0, G, row_step, 0)
+
+    loads[0].wait()
+    loads[1].wait()
+    tile = 256
+
+    def hand_on(k):
+        row_copy(k).wait_recv()
+        row_pass(k).start()
+
+    def shared_step(u, carry):
+        at = pl.ds(pl.multiple_of(u * tile, tile), tile)
+        pre = dot(normed[...], vsi[0, :, at])
+        up = dot(normed[...], vsi[1, :, at])
+        d_act = dot_nt(cot[...], vso[at, :])
+        s = sigmoid(pre)
+        gs = pre * s
+        act_s[:, at] = (gs * up).astype(bf16)
+        dgu_s[0, :, at] = (d_act * up * (s + gs * (1.0 - s))).astype(bf16)
+        dgu_s[1, :, at] = (d_act * gs).astype(bf16)
+        return carry
+
+    lax.fori_loop(0, F // tile, shared_step, 0)
+    for k in range(1, 6):
+        hand_on(k)
+    dnsh[...] = (dot_nt(dgu_s[0], vsi[0]) + dot_nt(dgu_s[1], vsi[1])).astype(bf16)
+    dnsh_copy = send(dnsh.at[:, theirs], dnsh_r, s_x.at[4], r_x.at[4], partner)
+    for k in range(6, 9):
+        hand_on(k)
+    shp[...] = dot(act_s[...], vso[...]).astype(bf16)
+    for k in range(9, 11):
+        hand_on(k)
+
+    side = round_up(T, 128)
+    turned[:, 0:T] = normed[...].T
+    turned[:, side : side + T] = cot[...].T
+    tiles = F // tile
+
+    def gsh_copy(i):
+        at = pl.ds(pl.multiple_of(i * tile, tile), tile)
+        return pltpu.make_async_copy(pale.at[lax.rem(i, 2)], gsh.at[:, at], osem.at[lax.rem(i, 2)])
+
+    def gsh_step(i, carry):
+        @pl.when(i > 1)
+        def _():
+            gsh_copy(i - 2).wait()
+
+        u = lax.rem(i, tiles)
+        at = pl.ds(pl.multiple_of(u * tile, tile), tile)
+
+        @pl.when(i < 2 * tiles)
+        def _():
+            pale[lax.rem(i, 2)] = dot(turned[:, 0:T], dgu_s[i // tiles, :, at]).astype(bf16)
+
+        @pl.when(i >= 2 * tiles)
+        def _():
+            pale[lax.rem(i, 2)] = dot(turned[:, side : side + T], act_s[:, at]).astype(bf16)
+
+        gsh_copy(i).start()
+        return carry
+
+    lax.fori_loop(0, 3 * tiles, gsh_step, 0)
+    for k in range(11, G):
+        hand_on(k)
+    dnsh_copy.start()
+    gsh_copy(3 * tiles - 2).wait()
+    gsh_copy(3 * tiles - 1).wait()
+
+    loads[2].wait()
+    loads[3].wait()
+    per = 4
+    M = per * C
+
+    def dx_copy(c):
+        at = pl.ds(pl.multiple_of(c * M, M), M)
+        return send(dxs.at[at, theirs], dxr.at[at], s_dx.at[c], r_dx.at[c], partner)
+
+    def ret_copy(k):
+        return send(
+            rets.at[row_at(k)], ret.at[row_at(k)], s_ret.at[k], r_ret.at[k],
+            (lax.rem(me - k + G, G), t),
+        )
+
+    def expert_chunk(c):
+        for k in range(c * per, (c + 1) * per):
+            row_pass(k).wait_recv()
+            if k > 0:
+                cot_copy(k).wait_recv()
+        block = pl.ds(c * M, M)
+
+        def unit_step(u, carry):
+            at = pl.ds(pl.multiple_of(u * tile, tile), tile)
+            pre = dot(rows[block, :], vei[0, :, at])
+            up = dot(rows[block, :], vei[1, :, at])
+            d_act = dot_nt(drows[block, :], veo[at, :])
+            s = sigmoid(pre)
+            gs = pre * s
+            act_e[block, at] = (gs * up).astype(bf16)
+            dgu_e[0, block, at] = (d_act * up * (s + gs * (1.0 - s))).astype(bf16)
+            dgu_e[1, block, at] = (d_act * gs).astype(bf16)
+            return carry
+
+        lax.fori_loop(0, F // tile, unit_step, 0)
+        dx = dot_nt(dgu_e[0, block, :], vei[0]) + dot_nt(dgu_e[1, block, :], vei[1])
+        dxs[block, :] = dx.astype(bf16)
+        dx_copy(c).start()
+
+    for k in range(1, G):
+        row_copy(k).wait_send()
+
+    def return_chunk(c):
+        block = pl.ds(c * M, M)
+        dx_copy(c).wait_recv()
+        total = (dxs[block, mine].astype(f32) + dxr[block, :].astype(f32)).astype(bf16)
+        rets[block, :] = total
+        for k in range(c * per, (c + 1) * per):
+            if k > 0:
+                ret_copy(k).start()
+        if c == 0:
+            ret[0:C, :] = total[0:C, :]
+
+    chunks = G // per
+    for c in range(chunks):
+        expert_chunk(c)
+        if c > 0:
+            return_chunk(c - 1)
+    return_chunk(chunks - 1)
+
+    for k in range(1, G):
+        cot_copy(k).wait_send()
+
+    def part_step(c, carry):
+        block = pl.ds(pl.multiple_of(c * M, M), M)
+        part[block, :] = dot(act_e[block, :], veo[...]).astype(bf16)
+        return carry
+
+    lax.fori_loop(0, chunks, part_step, 0)
+    turned[...] = rows[...].T
+
+    def gein_copy(i):
+        at = pl.ds(pl.multiple_of(lax.rem(i, tiles) * tile, tile), tile)
+        return pltpu.make_async_copy(
+            tall.at[lax.rem(i, 2)], gein.at[i // tiles, :, at], osem.at[lax.rem(i, 2)]
+        )
+
+    def gein_step(i, carry):
+        @pl.when(i > 1)
+        def _():
+            gein_copy(i - 2).wait()
+
+        at = pl.ds(pl.multiple_of(lax.rem(i, tiles) * tile, tile), tile)
+        tall[lax.rem(i, 2)] = dot(turned[...], dgu_e[i // tiles, :, at])
+        gein_copy(i).start()
+        return carry
+
+    lax.fori_loop(0, 2 * tiles, gein_step, 0)
+
+    def geout_copy(i):
+        at = pl.ds(pl.multiple_of(i * tile, tile), tile)
+        return pltpu.make_async_copy(
+            wide.at[lax.rem(i, 2)], geout.at[at, :], osem.at[2 + lax.rem(i, 2)]
+        )
+
+    def geout_step(i, carry):
+        @pl.when(i > 1)
+        def _():
+            geout_copy(i - 2).wait()
+
+        at = pl.ds(pl.multiple_of(i * tile, tile), tile)
+        wide[lax.rem(i, 2)] = dot_tn(act_e[:, at], drows[...])
+        geout_copy(i).start()
+        return carry
+
+    lax.fori_loop(0, tiles, geout_step, 0)
+    gein_copy(2 * tiles - 2).wait()
+    gein_copy(2 * tiles - 1).wait()
+    geout_copy(tiles - 2).wait()
+    geout_copy(tiles - 1).wait()
+
+    dnsh_copy.wait()
+    total = dnsh[:, mine].astype(f32) + dnsh_r[...].astype(f32)
+    for c in range(chunks):
+        for k in range(c * per, (c + 1) * per):
+            if k > 0:
+                ret_copy(k).wait_recv()
+        block = pl.ds(c * M, M)
+        total = total + dot_tn(plan[block, :], ret[block, :])
+    dnb[:, mine] = total.astype(bf16)
+    dnb_copy = send(dnb.at[:, mine], dnb.at[:, mine], s_x.at[5], r_x.at[5], partner)
+    dnb_copy.start()
+    dnb_copy.wait()
+
+    def dres_step(i, carry):
+        at = pl.ds(pl.multiple_of(i * FOLD, FOLD), FOLD)
+        y = dnb[at, :].astype(f32)
+        x = resid[at, :]
+        r = lax.rsqrt(jnp.mean(x * x, axis=1, keepdims=True) + epsilon)
+        a = y * nf[...]
+        inner = jnp.mean(a * x, axis=1, keepdims=True)
+        xr = x * r
+        dres[at, :] = cot[at, :].astype(f32) + r * a - xr * (r * r * inner)
+        return carry + jnp.sum(y * xr, axis=0, keepdims=True)
+
+    gnf[...] = jnp.broadcast_to(
+        lax.fori_loop(0, T // FOLD, dres_step, jnp.zeros((1, D), f32)), gnf.shape
+    )
+    for k in range(G):
+        row_pass(k).wait_send()
+    for k in range(1, G):
+        ret_copy(k).wait_send()
+    for c in range(chunks):
+        dx_copy(c).wait_send()
+
+
+def back_kernel(
+    G, tok, na, cos, sin, segr, segc, wqkv, wo, qkv, lse, att_own, normed_a, resid, plan, gate,
+    part, shp, dres, gnf, gsh,
+    out, gtok, gw1, gw2,
+    bias, dresb, da, dqkv, turned, pay, partr, po, ro, shpr, gated, dna, dnar, gna, gnar, ob,
+    o1, a1, b1, c1, d1, o2, a2, b2, c2, d2,
+    s_x, r_x, s_p, r_p, s_ret, r_ret, s_w, r_w, lsem,
+):
+    T, D = tok.shape
+    HL = wqkv.shape[2]
+    C = plan.shape[0] // G
+    half = D // 2
+    share = D // G
+    scale = HD ** (-0.5)
+    zs = G // 4
+    me, t = lax.axis_index("dp"), lax.axis_index("tensor")
+    core, y, z = lax.rem(me, 2), lax.rem(me // 2, 2), me // 4
+    mine = pl.ds(pl.multiple_of(t * half, 128), half)
+    theirs = pl.ds(pl.multiple_of((1 - t) * half, 128), half)
+    partner = (me, 1 - t)
+    per = 4
+    M = per * C
+    chunks = G // per
+
+    def row_at(k):
+        return pl.ds(pl.multiple_of(k * C, C), C)
+
+    def fold_core(n, src, a):
+        return send(src.at[:, :, 1 - core], a, s_w.at[n, 0], r_w.at[n, 0], (me + 1 - 2 * core, t))
+
+    def fold_y(n, o, b):
+        return send(o.at[:, 1 - y], b, s_w.at[n, 1], r_w.at[n, 1], (me + 2 - 4 * y, t))
+
+    def fold_z(n, c, d, k):
+        to = lax.rem(z + k, zs)
+        return send(
+            c.at[to], d.at[k - 1], s_w.at[n, 1 + k], r_w.at[n, 1 + k],
+            (to * 4 + lax.rem(me, 4), t),
+        )
+
+    def add_core(own, o, a):
+        def body(i, carry):
+            u, v = i // 2, lax.rem(i, 2)
+            first = o[u, v] if own is None else own[u, v, core]
+            o[u, v] = (first.astype(f32) + a[u, v].astype(f32)).astype(bf16)
+            return carry
+
+        lax.fori_loop(0, 2 * zs, body, 0)
+
+    def add_y(o, b, c):
+        def body(i, carry):
+            c[i] = (o[i, y].astype(f32) + b[i].astype(f32)).astype(bf16)
+            return carry
+
+        lax.fori_loop(0, zs, body, 0)
+
+    def add_z(c, d, w):
+        total = c[z].astype(f32)
+        for k in range(1, zs):
+            total = total + d[k - 1].astype(f32)
+        w[...] = total
+
+    def part_copy(c):
+        block = pl.ds(c * M, M)
+        return send(part.at[block, theirs], partr.at[block], s_p.at[c], r_p.at[c], partner)
+
+    def ret_copy(k):
+        return send(
+            po.at[row_at(k)], ro.at[row_at(k)], s_ret.at[k], r_ret.at[k],
+            (lax.rem(me - k + G, G), t),
+        )
+
+    def return_chunk(c):
+        block = pl.ds(c * M, M)
+        part_copy(c).wait_recv()
+        total = (part[block, mine].astype(f32) + partr[block, :].astype(f32)).astype(bf16)
+        po[block, :] = total
+        for k in range(c * per, (c + 1) * per):
+            if k > 0:
+                ret_copy(k).start()
+        if c == 0:
+            ro[0:C, :] = total[0:C, :]
+
+    own1 = pltpu.make_async_copy(gsh.at[:, :, core], o1, lsem.at[0])
+    own1.start()
+    hello(G)
+    core1 = fold_core(0, gsh, a1)
+    core1.start()
+    for c in range(chunks):
+        part_copy(c).start()
+    shp_copy = send(shp.at[:, theirs], shpr, s_x.at[0], r_x.at[0], partner)
+    shp_copy.start()
+
+    fill_bias(bias, segr, segc, T)
+    dresb[...] = dres[...].astype(bf16)
+    da[...] = dot_nt(dresb[...], wo[...]).astype(bf16)
+    own1.wait()
+    core1.wait()
+    add_core(None, o1, a1)
+    y1 = fold_y(0, o1, b1)
+    y1.start()
+    lane = lax.broadcasted_iota(jnp.int32, (T, 128), 1)
+
+    def attend(j, carry):
+        at = pl.ds(pl.multiple_of(j * 128, 128), 128)
+        q, k, v, g = qkv[0, :, at], qkv[1, :, at], qkv[2, :, at], da[:, at]
+        none = jnp.zeros_like(q)
+        dq = dk = dv = jnp.zeros((T, 128), f32)
+        for i in range(2):
+            inside = (lane < HD) if i == 0 else (lane >= HD)
+            qi, ki, gi = jnp.where(inside, q, none), jnp.where(inside, k, none), jnp.where(inside, g, none)
+            total = jnp.sum(jnp.where(lane == 2 * j + i, lse[...], 0.0), axis=1, keepdims=True)
+            p = jnp.exp(dot_nt(qi, k) * scale + bias[...] - total)
+            dp = dot_nt(gi, v)
+            inner = jnp.sum(dp * p, axis=1, keepdims=True)
+            ds = (p * (dp - inner)).astype(bf16)
+            dv = dv + dot_tn(p.astype(bf16), gi)
+            dq = dq + dot(ds, ki)
+            dk = dk + dot_tn(ds, qi)
+        dq, dk = dq * scale, dk * scale
+        dqkv[0, :, at] = (dq * cos[...] - swap_halves(dq) * sin[...]).astype(bf16)
+        dqkv[1, :, at] = (dk * cos[...] - swap_halves(dk) * sin[...]).astype(bf16)
+        dqkv[2, :, at] = dv.astype(bf16)
+
+        @pl.when(j == 0)
+        def _():
+            y1.wait()
+            add_y(o1, b1, c1)
+            for s in range(1, zs):
+                fold_z(0, c1, d1, s).start()
+            return_chunk(0)
+            return_chunk(1)
+
+        @pl.when(j == 1)
+        def _():
+            return_chunk(2)
+
+        return carry
+
+    lax.fori_loop(0, HL // 128, attend, 0)
+    return_chunk(3)
+
+    dna[...] = (dot_nt(dqkv[0], wqkv[0]) + dot_nt(dqkv[1], wqkv[1]) + dot_nt(dqkv[2], wqkv[2])).astype(bf16)
+    dna_copy = send(dna, dnar, s_x.at[1], r_x.at[1], partner)
+    dna_copy.start()
+
+    def gain_step(i, carry):
+        at = pl.ds(pl.multiple_of(i * FOLD, FOLD), FOLD)
+        x = tok[at, :].astype(f32)
+        r = lax.rsqrt(jnp.mean(x * x, axis=1, keepdims=True) + epsilon)
+        return carry + jnp.sum(dna[at, :].astype(f32) * x * r, axis=0, keepdims=True)
+
+    gna[...] = jnp.broadcast_to(
+        lax.fori_loop(0, T // FOLD, gain_step, jnp.zeros((1, D), f32)), gna.shape
+    )
+    gna_copy = send(gna, gnar, s_x.at[3], r_x.at[3], partner)
+    gna_copy.start()
+
+    turned[...] = normed_a[...].T
+    for s in range(3):
+        pay[:, :, :, :, s * HL : (s + 1) * HL] = dot(turned[...], dqkv[s]).astype(bf16).reshape(zs, 2, 2, share, HL)
+    turned[...] = dresb[...].T
+    pay[:, :, :, :, 3 * HL : 4 * HL] = dot(turned[...], att_own[...]).astype(bf16).reshape(zs, 2, 2, share, HL)
+    gna_copy.wait()
+    row = lax.broadcasted_iota(jnp.int32, (128, D), 0)
+    gains = jnp.where(row == 0, gnf[0:1, :], jnp.where(row == 1, gna[0:1, :] + gnar[0:1, :], 0.0))
+    pay[:, :, :, :, 4 * HL :] = gains.T.astype(bf16).reshape(zs, 2, 2, share, 128)
+    core2 = fold_core(1, pay, a2)
+    core2.start()
+    for s in range(1, zs):
+        fold_z(0, c1, d1, s).wait()
+    add_z(c1, d1, gw1)
+    core2.wait()
+    add_core(pay, o2, a2)
+    y2 = fold_y(1, o2, b2)
+    y2.start()
+
+    shp_copy.wait()
+    mixed = shp[:, mine].astype(f32) + shpr[...].astype(f32)
+    for c in range(chunks):
+        for k in range(c * per, (c + 1) * per):
+            if k > 0:
+                ret_copy(k).wait_recv()
+            weights = gate[pl.ds(lax.rem(me + k, G), 1), :]
+            gated[(k - c * per) * C : (k - c * per + 1) * C, :] = (
+                plan[row_at(k), :].astype(f32) * weights
+            ).astype(bf16)
+        mixed = mixed + dot_tn(gated[...], ro[c * M : (c + 1) * M, :])
+    ob[:, mine] = (resid[:, mine] + mixed).astype(bf16)
+    out_copy = send(ob.at[:, mine], ob.at[:, mine], s_x.at[2], r_x.at[2], partner)
+    out_copy.start()
+    y2.wait()
+    add_y(o2, b2, c2)
+    for s in range(1, zs):
+        fold_z(1, c2, d2, s).start()
+
+    dna_copy.wait()
+
+    def last_step(i, carry):
+        at = pl.ds(pl.multiple_of(i * FOLD, FOLD), FOLD)
+        x = tok[at, :].astype(f32)
+        r = lax.rsqrt(jnp.mean(x * x, axis=1, keepdims=True) + epsilon)
+        a = (dna[at, :].astype(f32) + dnar[at, :].astype(f32)) * na[...]
+        inner = jnp.mean(a * x, axis=1, keepdims=True)
+        gtok[at, :] = (dres[at, :] + r * a - x * (r * r * r * inner)).astype(bf16)
+        return carry
+
+    lax.fori_loop(0, T // FOLD, last_step, 0)
+    out_copy.wait()
+    out[...] = ob[...]
+    for s in range(1, zs):
+        fold_z(1, c2, d2, s).wait()
+    add_z(c2, d2, gw2)
+    for c in range(chunks):
+        part_copy(c).wait_send()
+    for k in range(1, G):
+        ret_copy(k).wait_send()
+
+
+def fused(
+    tokens, cont_lengths, routes, route_gates, w_qkv, w_attn_out, norm_attn, norm_ffn,
+    shared_in, shared_out, expert_in, expert_out, cotangent,
+):
+    T, D = tokens.shape
+    G = lax.axis_size("dp")
+    HL, F, FX = w_qkv.shape[2], shared_in.shape[2], expert_in.shape[2]
+    C = round_up(CAP, 16)
+    S = G * C
+    half, share, zs = D // 2, D // G, G // 4
+    row_index = jnp.arange(T, dtype=jnp.int32)
+    ends = PROMPT + jnp.cumsum(cont_lengths[0], dtype=jnp.int32)
+    later = jnp.sum((row_index[:, None] >= ends[None, :]).astype(jnp.int32), axis=1)
+    segment = jnp.where(row_index < PROMPT, 0, 1 + later)
+    member = (segment[:, None] == jnp.arange(1, ends.shape[0] + 1, dtype=jnp.int32)[None, :])
+    offset = jnp.sum(member.astype(jnp.int32) * (ends - cont_lengths[0])[None, :], axis=1)
+    position = jnp.where(segment == 0, row_index, PROMPT + row_index - offset)
+    lane = jnp.arange(128, dtype=jnp.int32)
+    inv_freq = 10000.0 ** (-(lane % (HD // 2)).astype(f32) / (HD // 2))
+    angles = position.astype(f32)[:, None] * inv_freq[None, :]
+    cos = jnp.cos(angles)
+    sin = jnp.sin(angles) * jnp.where(lane % HD < HD // 2, -1.0, 1.0)[None, :]
+    segr, segc = segment[None, :], segment[:, None]
+    na, nf = norm_attn[None, :], norm_ffn[None, :]
+    rT, gT = routes.T, route_gates.T
+    shape = jax.ShapeDtypeStruct
+    dma = pltpu.SemaphoreType.DMA
+    tile = 256
+    front = pl.pallas_call(
+        functools.partial(front_kernel, G),
+        out_shape=(
+            shape((3, T, HL), bf16), shape((T, 128), f32), shape((T, HL), bf16),
+            shape((T, D), bf16), shape((T, D), f32), shape((S, T), bf16), shape((EXPERTS, T), f32),
+            shape((S, D), bf16), shape((T, D), bf16), shape((T, D), f32), shape((8, D), f32),
+            shape((D, 3 * F), bf16), shape((2, D, FX), f32), shape((FX, D), f32),
+        ),
+        in_specs=[VM] * 12 + [ANY] * 4,
+        out_specs=(VM,) * 11 + (ANY,) * 3,
+        scratch_shapes=[
+            pltpu.VMEM((T, T), f32),
+            pltpu.VMEM((T, HL), bf16),
+            pltpu.VMEM((HL, D), bf16),
+            pltpu.VMEM((EXPERTS, T), f32),
+            pltpu.VMEM((S, D), bf16),
+            pltpu.VMEM((T, D), bf16),
+            pltpu.VMEM((S, D), bf16),
+            pltpu.VMEM((2, D, F), bf16),
+            pltpu.VMEM((F, D), bf16),
+            pltpu.VMEM((2, D, FX), bf16),
+            pltpu.VMEM((FX, D), bf16),
+            pltpu.VMEM((T, F), bf16),
+            pltpu.VMEM((2, T, F), bf16),
+            pltpu.VMEM((S, FX), bf16),
+            pltpu.VMEM((2, S, FX), bf16),
+            pltpu.VMEM((T, D), bf16),
+            pltpu.VMEM((T, half), bf16),
+            pltpu.VMEM((S, D), bf16),
+            pltpu.VMEM((S, half), bf16),
+            pltpu.VMEM((S, half), bf16),
+            pltpu.VMEM((S, half), bf16),
+            pltpu.VMEM((T, D), bf16),
+            pltpu.VMEM((D, S), bf16),
+            pltpu.VMEM((2, D, tile), f32),
+            pltpu.VMEM((2, tile, D), f32),
+            pltpu.VMEM((2, D, tile), bf16),
+            dma((6,)), dma((6,)), dma((G,)), dma((G,)), dma((G,)), dma((G,)), dma((G,)), dma((G,)),
+            dma((4,)), dma((4,)), dma((G,)), dma((G,)), dma((4,)), dma((4,)),
+        ],
+        compiler_params=pltpu.CompilerParams(
+            collective_id=0, has_side_effects=True, vmem_limit_bytes=VMEM_BYTES
+        ),
+        name="front",
+    )(
+        tokens, na, nf, cos, sin, segr, segc, rT, gT, w_qkv, w_attn_out, cotangent,
+        shared_in, shared_out, expert_in, expert_out,
+    )
+    qkv, lse, att_own, normed_a, resid, plan, gate, part, shp, dres, gnf, gsh, gein, geout = front
+    W1, W2 = 3 * F, 4 * HL + 128
+    fold = [(zs, 2, share), (zs, 2, share), (zs, share), (zs, share), (zs - 1, share)]
+    out, gtok, gw1, gw2 = pl.pallas_call(
+        functools.partial(back_kernel, G),
+        out_shape=(
+            shape((T, D), bf16), shape((T, D), bf16), shape((share, W1), f32), shape((share, W2), f32),
+        ),
+        in_specs=[VM] * 19 + [ANY],
+        out_specs=(VM,) * 4,
+        scratch_shapes=[
+            pltpu.VMEM((T, T), f32),
+            pltpu.VMEM((T, D), bf16),
+            pltpu.VMEM((T, HL), bf16),
+            pltpu.VMEM((3, T, HL), bf16),
+            pltpu.VMEM((D, T), bf16),
+            pltpu.VMEM((zs, 2, 2, share, W2), bf16),
+            pltpu.VMEM((S, half), bf16),
+            pltpu.VMEM((S, half), bf16),
+            pltpu.VMEM((S, half), bf16),
+            pltpu.VMEM((T, half), bf16),
+            pltpu.VMEM((4 * C, T), bf16),
+            pltpu.VMEM((T, D), bf16),
+            pltpu.VMEM((T, D), bf16),
+            pltpu.VMEM((8, D), f32),
+            pltpu.VMEM((8, D), f32),
+            pltpu.VMEM((T, D), bf16),
+            *[pltpu.VMEM((*s, W1), bf16) for s in fold],
+            *[pltpu.VMEM((*s, W2), bf16) for s in fold],
+            dma((4,)), dma((4,)), dma((4,)), dma((4,)), dma((G,)), dma((G,)),
+            dma((2, 1 + zs)), dma((2, 1 + zs)), dma((1,)),
+        ],
+        compiler_params=pltpu.CompilerParams(
+            collective_id=1, has_side_effects=True, vmem_limit_bytes=VMEM_BYTES
+        ),
+        name="back",
+    )(
+        tokens, na, cos, sin, segr, segc, w_qkv, w_attn_out, qkv, lse, att_own, normed_a, resid,
+        plan, gate, part, shp, dres, gnf, gsh.reshape(zs, 2, 2, share, W1),
+    )
+    return (
+        out,
+        gtok,
+        gw2[:, : 3 * HL].reshape(share, 3, HL).transpose(1, 0, 2),
+        gw2[:, 3 * HL : 4 * HL].T,
+        gw2[:, 4 * HL + 1],
+        gw2[:, 4 * HL],
+        gw1[:, : 2 * F].reshape(share, 2, F).transpose(1, 0, 2),
+        gw1[:, 2 * F :].T,
+        gein,
+        geout,
+    )
+
+
 def solution(mesh):
     placed = (
         P("dp", None),
@@ -296,7 +1095,7 @@
         P("dp", None),
     )
     return jax.shard_map(
-        local,
+        fused if mesh.shape["dp"] == EXPERTS else local,
         mesh=mesh,
         in_specs=placed,
         out_specs=(

time: 863 us -> 314 us (0.36)
  waiting for transfers between devices: 429 us -> 0 us
  Pallas kernels: 0 us -> 284 us
  local copies, waits for them, and re-layouts: 149 us -> 21 us
  matrix products: 113 us -> 0 us
  other arithmetic: 65.4 us -> 5.02 us
  starting transfers between devices: 43.8 us -> 0 us
  blocking collectives: 36.2 us -> 0 us
  between operations: 16 us -> 0.72 us
    pallas_call x0 -> x2, Pallas kernels: none -> 284 us  [the longest x1 168 us: fused(): pl.pallas_call(functools.partial(front_kernel, G), out_shape=(shape((3, T...]
    unnamed x7 -> x0, waiting for transfers between devices: 162 us -> none
    reduce_scatter x2 -> x0, waiting for transfers between devices: 129 us -> none  [the longest x1 67.4 us: local(): lax.psum_scatter(g_shared_out, 'dp', scatter_dimension=1, tiled=True)]
    dot_general x24 -> x0, matrix products: 113 us -> none  [the longest x1 10.3 us: local(): jnp.einsum('rf,rd->fd', back_act, d_expert_rows, preferred_element_type=j...]
    all_to_all x4 -> x0, waiting for transfers between devices: 83 us -> none  [the longest x1 24.8 us: local(): lax.all_to_all(d_expert_in.reshape(groups, CAP, model_width), 'dp', split...]
    psum x3 -> x0, waiting for transfers between devices: 55.5 us -> none  [the longest x1 29.2 us: local(): lax.psum(d_normed.astype(jnp.bfloat16), 'tensor').astype(jnp.float32)]
    all_to_all x4 -> x0, starting transfers between devices: 42.9 us -> none  [the longest x1 12.5 us: local(): lax.all_to_all(send_grad, 'dp', split_axis=0, concat_axis=0, tiled=True)]
    gather x5 -> x0, local copies, waits for them, and re-layouts: 36.4 us -> none  [the longest x3 20.3 us: spread_rows(): jnp.take(padded, indices, axis=0).reshape(EXPERTS, 1, CAP, model_width)]
  transfers between devices with their start and end apart: 10 -> 0, of which waited for: 9 -> 0; matrix products, arithmetic and copies ran while one was open for 23% -> 0% of each run, Pallas kernels for 0% -> 0%
where the time goes in v1:
time: 314 us; the launch traced here: 311 us
  Pallas kernels  284 us (90%)
  local copies, waits for them, and re-layouts  21 us (7%)
  other arithmetic  5.02 us (2%)
    pallas_call x1, Pallas kernels, fused(): pl.pallas_call(functools.partial(front_kernel, G), out_shape=(shape((3, T...  168 us
    pallas_call x1, Pallas kernels, fused(): pl.pallas_call(functools.partial(back_kernel, G), out_shape=(shape((T, D)...  116 us
    unnamed x11, local copies, waits for them, and re-layouts  11 us

profile of v1, /device:TPU:0, one launch (start us, length us, event | category | flops | bytes accessed | tf_op | source)
XLA Modules:
  0.0 310.9 jit_solution(739471369409667421)
XLA Ops:
  0.6 0.8 reduce-window.4
  1.5 0.7 fusion.8
  2.1 1.3 broadcast_in_dim.32.na
  3.4 1.3 broadcast_in_dim.38.nf
  4.7 0.1 fusion.1
  4.8 0.1 fusion.2
  4.9 0.6 compare_select_fusion.segr
  5.5 0.8 reshape_select_fusion.segc
  6.3 1.9 fusion
  8.2 168.4 %front.1 = (bf16[3,576,384]{2,1,0:T(8,128)(2,1)}, f32[576,128]{1,0:T(8,128)}, bf16[576,384]{1,0:T(8,128)(2,1)}, bf16[576,768]{1,0:T(8,128)(2,1)}, f32[576,768]{1...) custom-call(bf16[576,768]{1,0:T(8,128)(2,1)} %tok.3, ...), custom_call_target="tpu_custom_call" | custom-call | tf_op jit(solution)/shard_map/front/pallas_call | solution.py:979
  176.7 115.7 %back.1 = (bf16[576,768]{1,0:T(8,128)(2,1)}, bf16[576,768]{1,0:T(8,128)(2,1)}, f32[48,3072]{1,0:T(8,128)}, f32[48,1664]{1,0:T(8,128)}) custom-call(bf16[576,768]{1,0:T(8,128)(2,1)} %tok.3, f32[1,768]{1,0:T(1,128)} %broadcast_in_dim.32.na, f32[576,128]{1,0:T(8,128)} %get-tuple-element.69.cos, f32[576,128]{1,0:T(8,128)} %get-tuple-element.68.sin, ...), custom_call_target="tpu_custom_call" | custom-call | tf_op jit(solution)/shard_map/back/pallas_call | solution.py:1030
  292.4 0.0 copy-start.2
  292.4 1.5 slice_reduce_fusion
  293.9 1.5 slice_bitcast_fusion.1
  295.4 0.9 slice.18
  296.4 0.1 reshape.132
  296.5 0.7 copy.30
  297.2 1.6 slice_bitcast_fusion
  298.8 1.0 slice.22
  299.8 0.8 copy.33
  300.6 0.9 copy.38
  301.5 0.9 copy.39
  302.4 6.8 %copy.40 = f32[2,768,1024]{2,1,0:T(8,128)} copy(f32[2,768,1024]{2,1,0:T(8,128)} %get-tuple-element.92) | data formatting | bytes 12582912
  309.2 1.7 copy.41
  (10 shorter events, 0.0 us)
Async XLA Ops:
  292.4 8.2 %copy-start.2 = (bf16[576,768]{1,0:T(8,128)(2,1)S(1)}, bf16[576,768]{1,0:T(8,128)(2,1)}, u32[]{:S(2)}) copy-start(bf16[576,768]{1,0:T(8,128)(2,1)} %get-tuple-element.84) | copy-start | bytes 2654212
  296.4 5.1 %copy-start.1 = (bf16[576,768]{1,0:T(8,128)(2,1)S(1)}, bf16[576,768]{1,0:T(8,128)(2,1)}, u32[]{:S(2)}) copy-start(bf16[576,768]{1,0:T(8,128)(2,1)} %get-tuple-element.85) | copy-start | bytes 2654212
  302.4 6.8 %copy-start = (f32[1024,768]{1,0:T(8,128)S(1)}, f32[1024,768]{1,0:T(8,128)}, u32[]{:S(2)}) copy-start(f32[1024,768]{1,0:T(8,128)} %get-tuple-element.93) | copy-start | bytes 9437188

commit v2 on v1

--- a/solution.py
+++ b/solution.py
@@ -1,4 +1,5 @@
 import functools
+import math
 
 import jax
 import jax.numpy as jnp
@@ -285,6 +286,7 @@
 
 VMEM_BYTES = 64000 * 1024
 FOLD = 96
+SPLIT = 7
 MESH = pl.DeviceIdType.MESH
 VM = pl.BlockSpec(memory_space=pltpu.VMEM)
 ANY = pl.BlockSpec(memory_space=pl.ANY)
@@ -334,17 +336,52 @@
     pl.semaphore_wait(barrier, groups)
 
 
-def fill_bias(bias, segr, segc, rows):
+def segment_of(index, lens):
+    segment = jnp.where(index < PROMPT, 0, 1)
+    end = PROMPT
+    for c in range(lens.shape[1]):
+        end = end + lens[0, c]
+        segment = segment + jnp.where(index >= end, 1, 0)
+    return segment
+
+
+def position_of(index, lens):
+    segment = segment_of(index, lens)
+    position, end = index, PROMPT
+    for c in range(lens.shape[1]):
+        position = jnp.where(segment == c + 1, PROMPT + index - end, position)
+        end = end + lens[0, c]
+    return position
+
+
+def fill_bias(bias, lens, rows):
     step = FOLD
 
     def body(i, carry):
         at = pl.ds(pl.multiple_of(i * step, step), step)
         row = lax.broadcasted_iota(jnp.int32, (step, rows), 0) + i * step
         col = lax.broadcasted_iota(jnp.int32, (step, rows), 1)
-        own = segc[at, :]
-        other = segr[...]
+        own = segment_of(lax.broadcasted_iota(jnp.int32, (step, 1), 0) + i * step, lens)
+        other = segment_of(lax.broadcasted_iota(jnp.int32, (1, rows), 1), lens)
         ok = (col <= row) & ((other == 0) | (other == own))
         bias[at, :] = jnp.where(ok, 0.0, -1000000000.0)
+        return carry
+
+    lax.fori_loop(0, rows // step, body, 0)
+
+
+def fill_angles(cos, sin, lens, rows):
+    step = FOLD
+
+    def body(i, carry):
+        at = pl.ds(pl.multiple_of(i * step, step), step)
+        lane = lax.broadcasted_iota(jnp.int32, (step, 128), 1)
+        row = lax.broadcasted_iota(jnp.int32, (step, 128), 0) + i * step
+        power = lax.rem(lane, HD // 2).astype(f32) * (-math.log(10000.0) / (HD // 2))
+        angle = position_of(row, lens).astype(f32) * jnp.exp(power)
+        cos[at, :] = jnp.cos(angle)
+        sine = jnp.sin(angle)
+        sin[at, :] = jnp.where(lax.rem(lane, HD) < HD // 2, -sine, sine)
         return carry
 
     lax.fori_loop(0, rows // step, body, 0)
@@ -357,11 +394,14 @@
 
 
 def front_kernel(
-    G, tok, na, nf, cos, sin, segr, segc, rT, gT, wqkv, wo, cot, si, so, ei, eo,
-    qkv, lse, att_own, normed_a, resid, plan, gate, part, shp, dres, gnf, gsh, gein, geout,
+    G, na, nf, lens, rT, gT, h_tok, h_wqkv, h_wo, h_cot, si, so, ei, eo,
+    h_qkv, h_lse, h_att, h_normed_a, h_resid, h_plan, h_gate, h_cos, h_sin, h_part, h_shp, h_dres, h_gnf,
+    gsh, gein, geout,
+    tok, wqkv, wo, cot, cos, sin,
+    qkv, lse, att_own, normed_a, resid, plan, gate, part, shp, dres, gnf,
     bias, att, wo2, slot, drows, normed, rows, vsi, vso, vei, veo,
     act_s, dgu_s, act_e, dgu_e, dnsh, dnsh_r, dxs, dxr, rets, ret, dnb, turned, tall, wide, pale,
-    s_x, r_x, s_c, r_c, s_r, r_r, s_f, r_f, s_dx, r_dx, s_ret, r_ret, lsem, osem,
+    s_x, r_x, s_c, r_c, s_cf, r_cf, s_r, r_r, s_f, r_f, s_dx, r_dx, s_ret, r_ret, lsem, osem, ksem,
 ):
     T, D = tok.shape
     HL = wqkv.shape[2]
@@ -374,15 +414,32 @@
     theirs = pl.ds(pl.multiple_of((1 - t) * half, 128), half)
     partner = (me, 1 - t)
 
+    core = lax.rem(me, 2)
     loads = [
         pltpu.make_async_copy(a, b, lsem.at[i])
-        for i, (a, b) in enumerate(((si, vsi), (so, vso), (ei, vei), (eo, veo)))
+        for i, (a, b) in enumerate(
+            ((h_cot, cot), (h_tok, tok), (h_wqkv, wqkv), (h_wo, wo), (si, vsi), (so, vso), (ei, vei), (eo, veo))
+        )
     ]
     for c in loads:
         c.start()
+    keeps = [
+        pltpu.make_async_copy(a, b, ksem.at[i])
+        for i, (a, b) in enumerate(
+            (
+                (qkv, h_qkv), (lse, h_lse), (att_own, h_att), (normed_a, h_normed_a), (resid, h_resid),
+                (plan, h_plan), (gate, h_gate), (cos, h_cos), (sin, h_sin), (part, h_part), (shp, h_shp),
+                (dres, h_dres), (gnf, h_gnf),
+            )
+        )
+    ]
     hello(G)
-    wo_copy = send(wo, wo2, s_x.at[0], r_x.at[0], partner)
+    part_wo = pl.ds(pl.multiple_of(core * (HL // 2), 16), HL // 2)
+    wo_copy = send(h_wo.at[part_wo], wo2.at[part_wo], s_x.at[0], r_x.at[0], partner)
     wo_copy.start()
+    wo_pass = send(
+        wo2.at[part_wo], wo2.at[part_wo], s_x.at[6], r_x.at[6], (me + 1 - 2 * core, t)
+    )
 
     names = lax.broadcasted_iota(jnp.int32, (EXPERTS, T), 0)
     picks0, picks1 = rT[0:1, :] == names, rT[1:2, :] == names
@@ -400,8 +457,18 @@
 
     def cot_copy(k):
         return send(
-            part.at[row_at(k)], drows.at[row_at(k)], s_c.at[k], r_c.at[k],
+            part.at[row_at(k)], drows.at[row_at(k)], s_c.at[k], r_c.at[k], (lax.rem(me + k, G), t)
+        )
+
+    def cot_half(k):
+        return send(
+            part.at[row_at(k), mine], drows.at[row_at(k), mine], s_c.at[k], r_c.at[k],
             (lax.rem(me + k, G), t),
+        )
+
+    def cot_pass(k):
+        return send(
+            drows.at[row_at(k), mine], drows.at[row_at(k), mine], s_cf.at[k], r_cf.at[k], partner
         )
 
     def cot_step(k, carry):
@@ -415,9 +482,13 @@
         grad = (dot(picked, cot[...]) * weight).astype(bf16)
         part[at, :] = grad
 
-        @pl.when(k > 0)
+        @pl.when(k > SPLIT)
         def _():
             cot_copy(k).start()
+
+        @pl.when((k > 0) & (k <= SPLIT))
+        def _():
+            cot_half(k).start()
 
         @pl.when(k == 0)
         def _():
@@ -425,18 +496,28 @@
 
         return carry
 
+    loads[0].wait()
     lax.fori_loop(0, G, cot_step, 0)
-
-    fill_bias(bias, segr, segc, T)
+    keeps[5].start()
+    keeps[6].start()
+
+    fill_angles(cos, sin, lens, T)
+    keeps[7].start()
+    keeps[8].start()
+    fill_bias(bias, lens, T)
+    loads[1].wait()
 
     def norm_step(i, carry):
         at = pl.ds(pl.multiple_of(i * FOLD, FOLD), FOLD)
         x = tok[at, :].astype(f32)
         r = lax.rsqrt(jnp.mean(x * x, axis=1, keepdims=True) + epsilon)
-        normed_a[at, :] = (x * r * na[...]).astype(bf16)
+        normed_a[at, :] = (x * r * na[...].reshape(1, D)).astype(bf16)
         return carry
 
     lax.fori_loop(0, T // FOLD, norm_step, 0)
+    keeps[3].start()
+    loads[2].wait()
+    loads[3].wait()
 
     def project(s, turned):
         full = dot(normed_a[...], wqkv[s])
@@ -449,6 +530,7 @@
     project(0, True)
     project(1, True)
     project(2, False)
+    keeps[0].start()
     lane = lax.broadcasted_iota(jnp.int32, (T, 128), 1)
 
     def att_copy(j):
@@ -474,21 +556,29 @@
         att_copy(j).start()
         return carry
 
+    wo_copy.wait()
+    wo_pass.start()
     lax.fori_loop(0, HL // 128, attend, 0)
-    wo_copy.wait()
+    keeps[1].start()
+    keeps[2].start()
     own_out = dot(att_own[...], wo[...])
+    wo_pass.wait()
     for j in range(HL // 128):
         att_copy(j).wait()
+    for k in range(1, SPLIT + 1):
+        cot_half(k).wait_recv()
+        cot_pass(k).start()
     resid[...] = tok[...].astype(f32) + own_out + dot(att[...], wo2[...])
 
     def norm2_step(i, carry):
         at = pl.ds(pl.multiple_of(i * FOLD, FOLD), FOLD)
         x = resid[at, :]
         r = lax.rsqrt(jnp.mean(x * x, axis=1, keepdims=True) + epsilon)
-        normed[at, :] = (x * r * nf[...]).astype(bf16)
+        normed[at, :] = (x * r * nf[...].reshape(1, D)).astype(bf16)
         return carry
 
     lax.fori_loop(0, T // FOLD, norm2_step, 0)
+    keeps[4].start()
 
     def row_copy(k):
         return send(
@@ -517,9 +607,10 @@
 
     lax.fori_loop(0, G, row_step, 0)
 
-    loads[0].wait()
-    loads[1].wait()
+    loads[4].wait()
+    loads[5].wait()
     tile = 256
+    tiles = F // tile
 
     def hand_on(k):
         row_copy(k).wait_recv()
@@ -537,21 +628,7 @@
         dgu_s[1, :, at] = (d_act * gs).astype(bf16)
         return carry
 
-    lax.fori_loop(0, F // tile, shared_step, 0)
-    for k in range(1, 6):
-        hand_on(k)
-    dnsh[...] = (dot_nt(dgu_s[0], vsi[0]) + dot_nt(dgu_s[1], vsi[1])).astype(bf16)
-    dnsh_copy = send(dnsh.at[:, theirs], dnsh_r, s_x.at[4], r_x.at[4], partner)
-    for k in range(6, 9):
-        hand_on(k)
-    shp[...] = dot(act_s[...], vso[...]).astype(bf16)
-    for k in range(9, 11):
-        hand_on(k)
-
     side = round_up(T, 128)
-    turned[:, 0:T] = normed[...].T
-    turned[:, side : side + T] = cot[...].T
-    tiles = F // tile
 
     def gsh_copy(i):
         at = pl.ds(pl.multiple_of(i * tile, tile), tile)
@@ -576,17 +653,9 @@
         gsh_copy(i).start()
         return carry
 
-    lax.fori_loop(0, 3 * tiles, gsh_step, 0)
-    for k in range(11, G):
-        hand_on(k)
-    dnsh_copy.start()
-    gsh_copy(3 * tiles - 2).wait()
-    gsh_copy(3 * tiles - 1).wait()
-
-    loads[2].wait()
-    loads[3].wait()
     per = 4
     M = per * C
+    chunks = G // per
 
     def dx_copy(c):
         at = pl.ds(pl.multiple_of(c * M, M), M)
@@ -601,8 +670,10 @@
     def expert_chunk(c):
         for k in range(c * per, (c + 1) * per):
             row_pass(k).wait_recv()
-            if k > 0:
+            if k > SPLIT:
                 cot_copy(k).wait_recv()
+            elif k > 0:
+                cot_pass(k).wait_recv()
         block = pl.ds(c * M, M)
 
         def unit_step(u, carry):
@@ -622,13 +693,13 @@
         dxs[block, :] = dx.astype(bf16)
         dx_copy(c).start()
 
-    for k in range(1, G):
-        row_copy(k).wait_send()
-
     def return_chunk(c):
         block = pl.ds(c * M, M)
         dx_copy(c).wait_recv()
         total = (dxs[block, mine].astype(f32) + dxr[block, :].astype(f32)).astype(bf16)
+        for k in range(c * per, (c + 1) * per):
+            if k > 0:
+                row_copy(k).wait_send()
         rets[block, :] = total
         for k in range(c * per, (c + 1) * per):
             if k > 0:
@@ -636,15 +707,40 @@
         if c == 0:
             ret[0:C, :] = total[0:C, :]
 
-    chunks = G // per
-    for c in range(chunks):
-        expert_chunk(c)
-        if c > 0:
-            return_chunk(c - 1)
-    return_chunk(chunks - 1)
+    lax.fori_loop(0, F // tile, shared_step, 0)
+    for k in range(1, 4):
+        hand_on(k)
+    dnsh[...] = (dot_nt(dgu_s[0], vsi[0]) + dot_nt(dgu_s[1], vsi[1])).astype(bf16)
+    dnsh_copy = send(dnsh.at[:, theirs], dnsh_r, s_x.at[4], r_x.at[4], partner)
+    loads[6].wait()
+    loads[7].wait()
+    for k in range(4, 6):
+        hand_on(k)
+    expert_chunk(0)
+    for k in range(6, 8):
+        hand_on(k)
+    shp[...] = dot(act_s[...], vso[...]).astype(bf16)
+    keeps[10].start()
+    turned[:, 0:T] = normed[...].T
+    turned[:, side : side + T] = cot[...].T
+    return_chunk(0)
+    expert_chunk(1)
+    for k in range(8, 12):
+        hand_on(k)
+    lax.fori_loop(0, 2 * tiles, gsh_step, 0)
+    return_chunk(1)
+    expert_chunk(2)
+    for k in range(12, G):
+        hand_on(k)
+    dnsh_copy.start()
+    lax.fori_loop(2 * tiles, 3 * tiles, gsh_step, 0)
+    return_chunk(2)
+    expert_chunk(3)
+    gsh_copy(3 * tiles - 2).wait()
+    gsh_copy(3 * tiles - 1).wait()
 
     for k in range(1, G):
-        cot_copy(k).wait_send()
+        (cot_copy(k) if k > SPLIT else cot_half(k)).wait_send()
 
     def part_step(c, carry):
         block = pl.ds(pl.multiple_of(c * M, M), M)
@@ -652,6 +748,8 @@
         return carry
 
     lax.fori_loop(0, chunks, part_step, 0)
+    keeps[9].start()
+    return_chunk(3)
     turned[...] = rows[...].T
 
     def gein_copy(i):
@@ -666,7 +764,7 @@
             gein_copy(i - 2).wait()
 
         at = pl.ds(pl.multiple_of(lax.rem(i, tiles) * tile, tile), tile)
-        tall[lax.rem(i, 2)] = dot(turned[...], dgu_e[i // tiles, :, at])
+        tall[lax.rem(i, 2)] = dot(turned[...], dgu_e[i // tiles, :, at]).astype(bf16)
         gein_copy(i).start()
         return carry
 
@@ -684,7 +782,7 @@
             geout_copy(i - 2).wait()
 
         at = pl.ds(pl.multiple_of(i * tile, tile), tile)
-        wide[lax.rem(i, 2)] = dot_tn(act_e[:, at], drows[...])
+        wide[lax.rem(i, 2)] = dot_tn(act_e[:, at], drows[...]).astype(bf16)
         geout_copy(i).start()
         return carry
 
@@ -712,7 +810,7 @@
         y = dnb[at, :].astype(f32)
         x = resid[at, :]
         r = lax.rsqrt(jnp.mean(x * x, axis=1, keepdims=True) + epsilon)
-        a = y * nf[...]
+        a = y * nf[...].reshape(1, D)
         inner = jnp.mean(a * x, axis=1, keepdims=True)
         xr = x * r
         dres[at, :] = cot[at, :].astype(f32) + r * a - xr * (r * r * inner)
@@ -721,18 +819,25 @@
     gnf[...] = jnp.broadcast_to(
         lax.fori_loop(0, T // FOLD, dres_step, jnp.zeros((1, D), f32)), gnf.shape
     )
+    keeps[11].start()
+    keeps[12].start()
     for k in range(G):
         row_pass(k).wait_send()
+    for k in range(1, SPLIT + 1):
+        cot_pass(k).wait_send()
     for k in range(1, G):
         ret_copy(k).wait_send()
     for c in range(chunks):
         dx_copy(c).wait_send()
+    for c in keeps:
+        c.wait()
 
 
 def back_kernel(
-    G, tok, na, cos, sin, segr, segc, wqkv, wo, qkv, lse, att_own, normed_a, resid, plan, gate,
-    part, shp, dres, gnf, gsh,
+    G, na, lens, h_tok, h_wqkv, h_wo, h_qkv, h_lse, h_att, h_normed_a, h_resid, h_plan, h_gate,
+    h_cos, h_sin, h_part, h_shp, h_dres, h_gnf, gsh,
     out, gtok, gw1, gw2,
+    tok, wqkv, wo, qkv, lse, att_own, normed_a, resid, plan, gate, cos, sin, part, shp, dres, gnf,
     bias, dresb, da, dqkv, turned, pay, partr, po, ro, shpr, gated, dna, dnar, gna, gnar, ob,
     o1, a1, b1, c1, d1, o2, a2, b2, c2, d2,
     s_x, r_x, s_p, r_p, s_ret, r_ret, s_w, r_w, lsem,
@@ -759,13 +864,15 @@
     def fold_core(n, src, a):
         return send(src.at[:, :, 1 - core], a, s_w.at[n, 0], r_w.at[n, 0], (me + 1 - 2 * core, t))
 
-    def fold_y(n, o, b):
-        return send(o.at[:, 1 - y], b, s_w.at[n, 1], r_w.at[n, 1], (me + 2 - 4 * y, t))
-
-    def fold_z(n, c, d, k):
+    def fold_y(n, o, b, cols):
+        return send(
+            o.at[:, 1 - y, :, cols], b.at[:, :, cols], s_w.at[n, 1], r_w.at[n, 1], (me + 2 - 4 * y, t)
+        )
+
+    def fold_z(n, c, d, cols, k):
         to = lax.rem(z + k, zs)
         return send(
-            c.at[to], d.at[k - 1], s_w.at[n, 1 + k], r_w.at[n, 1 + k],
+            c.at[to, :, cols], d.at[k - 1, :, cols], s_w.at[n, 1 + k], r_w.at[n, 1 + k],
             (to * 4 + lax.rem(me, 4), t),
         )
 
@@ -778,22 +885,22 @@
 
         lax.fori_loop(0, 2 * zs, body, 0)
 
-    def add_y(o, b, c):
+    def add_y(o, b, c, cols):
         def body(i, carry):
-            c[i] = (o[i, y].astype(f32) + b[i].astype(f32)).astype(bf16)
+            c[i, :, cols] = (o[i, y, :, cols].astype(f32) + b[i, :, cols].astype(f32)).astype(bf16)
             return carry
 
         lax.fori_loop(0, zs, body, 0)
 
-    def add_z(c, d, w):
-        total = c[z].astype(f32)
+    def add_z(c, d, w, cols):
+        total = c[z, :, cols].astype(f32)
         for k in range(1, zs):
-            total = total + d[k - 1].astype(f32)
-        w[...] = total
+            total = total + d[k - 1, :, cols].astype(f32)
+        w[:, cols] = total
 
     def part_copy(c):
         block = pl.ds(c * M, M)
-        return send(part.at[block, theirs], partr.at[block], s_p.at[c], r_p.at[c], partner)
+        return send(h_part.at[block, theirs], partr.at[block], s_p.at[c], r_p.at[c], partner)
 
     def ret_copy(k):
         return send(
@@ -804,7 +911,7 @@
     def return_chunk(c):
         block = pl.ds(c * M, M)
         part_copy(c).wait_recv()
-        total = (part[block, mine].astype(f32) + partr[block, :].astype(f32)).astype(bf16)
+        total = (part[block, :].astype(f32) + partr[block, :].astype(f32)).astype(bf16)
         po[block, :] = total
         for k in range(c * per, (c + 1) * per):
             if k > 0:
@@ -812,24 +919,36 @@
         if c == 0:
             ro[0:C, :] = total[0:C, :]
 
-    own1 = pltpu.make_async_copy(gsh.at[:, :, core], o1, lsem.at[0])
-    own1.start()
+    pairs = (
+        (h_dres, dres), (h_wo, wo), (h_qkv, qkv), (h_lse, lse), (h_cos, cos), (h_sin, sin),
+        (gsh.at[:, :, core], o1), (h_part.at[:, mine], part), (h_wqkv, wqkv), (h_tok, tok),
+        (h_normed_a, normed_a), (h_att, att_own), (h_gnf, gnf), (h_shp.at[:, mine], shp),
+        (h_plan, plan), (h_gate, gate), (h_resid.at[:, mine], resid),
+    )
+    loads = [pltpu.make_async_copy(a, b, lsem.at[i]) for i, (a, b) in enumerate(pairs)]
+    for c in loads:
+        c.start()
     hello(G)
     core1 = fold_core(0, gsh, a1)
     core1.start()
     for c in range(chunks):
         part_copy(c).start()
-    shp_copy = send(shp.at[:, theirs], shpr, s_x.at[0], r_x.at[0], partner)
-    shp_copy.start()
-
-    fill_bias(bias, segr, segc, T)
+
+    fill_bias(bias, lens, T)
+    loads[0].wait()
+    loads[1].wait()
     dresb[...] = dres[...].astype(bf16)
     da[...] = dot_nt(dresb[...], wo[...]).astype(bf16)
-    own1.wait()
+    loads[6].wait()
     core1.wait()
     add_core(None, o1, a1)
-    y1 = fold_y(0, o1, b1)
-    y1.start()
+    W1 = gw1.shape[1]
+    halves = [slice(i * (W1 // 2), (i + 1) * (W1 // 2)) for i in range(2)]
+    ys = [fold_y(i, o1, b1, halves[i]) for i in range(2)]
+    for c in ys:
+        c.start()
+    for i in range(2, 6):
+        loads[i].wait()
     lane = lax.broadcasted_iota(jnp.int32, (T, 128), 1)
 
     def attend(j, carry):
@@ -853,27 +972,27 @@
         dqkv[1, :, at] = (dk * cos[...] - swap_halves(dk) * sin[...]).astype(bf16)
         dqkv[2, :, at] = dv.astype(bf16)
 
-        @pl.when(j == 0)
-        def _():
-            y1.wait()
-            add_y(o1, b1, c1)
-            for s in range(1, zs):
-                fold_z(0, c1, d1, s).start()
-            return_chunk(0)
-            return_chunk(1)
-
-        @pl.when(j == 1)
-        def _():
-            return_chunk(2)
-
         return carry
 
     lax.fori_loop(0, HL // 128, attend, 0)
-    return_chunk(3)
+    loads[7].wait()
+    loads[8].wait()
 
     dna[...] = (dot_nt(dqkv[0], wqkv[0]) + dot_nt(dqkv[1], wqkv[1]) + dot_nt(dqkv[2], wqkv[2])).astype(bf16)
     dna_copy = send(dna, dnar, s_x.at[1], r_x.at[1], partner)
+    return_chunk(0)
+    return_chunk(1)
     dna_copy.start()
+    shp_copy = send(h_shp.at[:, theirs], shpr, s_x.at[0], r_x.at[0], partner)
+    shp_copy.start()
+    for i in range(9, 13):
+        loads[i].wait()
+
+    def fold_on(i):
+        ys[i].wait()
+        add_y(o1, b1, c1, halves[i])
+        for s in range(1, zs):
+            fold_z(i, c1, d1, halves[i], s).start()
 
     def gain_step(i, carry):
         at = pl.ds(pl.multiple_of(i * FOLD, FOLD), FOLD)
@@ -886,28 +1005,32 @@
     )
     gna_copy = send(gna, gnar, s_x.at[3], r_x.at[3], partner)
     gna_copy.start()
+    return_chunk(2)
 
     turned[...] = normed_a[...].T
     for s in range(3):
         pay[:, :, :, :, s * HL : (s + 1) * HL] = dot(turned[...], dqkv[s]).astype(bf16).reshape(zs, 2, 2, share, HL)
+    fold_on(0)
+    return_chunk(3)
     turned[...] = dresb[...].T
     pay[:, :, :, :, 3 * HL : 4 * HL] = dot(turned[...], att_own[...]).astype(bf16).reshape(zs, 2, 2, share, HL)
     gna_copy.wait()
     row = lax.broadcasted_iota(jnp.int32, (128, D), 0)
     gains = jnp.where(row == 0, gnf[0:1, :], jnp.where(row == 1, gna[0:1, :] + gnar[0:1, :], 0.0))
     pay[:, :, :, :, 4 * HL :] = gains.T.astype(bf16).reshape(zs, 2, 2, share, 128)
-    core2 = fold_core(1, pay, a2)
+    core2 = fold_core(2, pay, a2)
     core2.start()
-    for s in range(1, zs):
-        fold_z(0, c1, d1, s).wait()
-    add_z(c1, d1, gw1)
+    fold_on(1)
     core2.wait()
     add_core(pay, o2, a2)
-    y2 = fold_y(1, o2, b2)
+    every = slice(0, gw2.shape[1])
+    y2 = fold_y(2, o2, b2, every)
     y2.start()
 
+    for i in range(13, 17):
+        loads[i].wait()
     shp_copy.wait()
-    mixed = shp[:, mine].astype(f32) + shpr[...].astype(f32)
+    mixed = shp[...].astype(f32) + shpr[...].astype(f32)
     for c in range(chunks):
         for k in range(c * per, (c + 1) * per):
             if k > 0:
@@ -917,13 +1040,17 @@
                 plan[row_at(k), :].astype(f32) * weights
             ).astype(bf16)
         mixed = mixed + dot_tn(gated[...], ro[c * M : (c + 1) * M, :])
-    ob[:, mine] = (resid[:, mine] + mixed).astype(bf16)
+    ob[:, mine] = (resid[...] + mixed).astype(bf16)
     out_copy = send(ob.at[:, mine], ob.at[:, mine], s_x.at[2], r_x.at[2], partner)
     out_copy.start()
     y2.wait()
-    add_y(o2, b2, c2)
+    add_y(o2, b2, c2, every)
     for s in range(1, zs):
-        fold_z(1, c2, d2, s).start()
+        fold_z(2, c2, d2, every, s).start()
+    for i in range(2):
+        for s in range(1, zs):
+            fold_z(i, c1, d1, halves[i], s).wait()
+        add_z(c1, d1, gw1, halves[i])
 
     dna_copy.wait()
 
@@ -931,7 +1058,7 @@
         at = pl.ds(pl.multiple_of(i * FOLD, FOLD), FOLD)
         x = tok[at, :].astype(f32)
         r = lax.rsqrt(jnp.mean(x * x, axis=1, keepdims=True) + epsilon)
-        a = (dna[at, :].astype(f32) + dnar[at, :].astype(f32)) * na[...]
+        a = (dna[at, :].astype(f32) + dnar[at, :].astype(f32)) * na[...].reshape(1, D)
         inner = jnp.mean(a * x, axis=1, keepdims=True)
         gtok[at, :] = (dres[at, :] + r * a - x * (r * r * r * inner)).astype(bf16)
         return carry
@@ -940,12 +1067,34 @@
     out_copy.wait()
     out[...] = ob[...]
     for s in range(1, zs):
-        fold_z(1, c2, d2, s).wait()
-    add_z(c2, d2, gw2)
+        fold_z(2, c2, d2, every, s).wait()
+    add_z(c2, d2, gw2, every)
     for c in range(chunks):
         part_copy(c).wait_send()
     for k in range(1, G):
         ret_copy(k).wait_send()
+
+
+def finish_kernel(
+    HL, F, h_out, h_gtok, h_gw1, h_gw2, h_gein, h_geout,
+    out, gtok, gqkv, gao, gna, gnf, gsi, gso, gein, geout,
+):
+    out[...] = h_out[...]
+    gtok[...] = h_gtok[...]
+    gein[...] = h_gein[...].astype(f32)
+    geout[...] = h_geout[...].astype(f32)
+
+    @pl.when(pl.program_id(0) == 0)
+    def _():
+        for s in range(3):
+            gqkv[s] = h_gw2[:, s * HL : (s + 1) * HL]
+        gao[...] = h_gw2[:, 3 * HL : 4 * HL].T
+        gains = h_gw2[:, 4 * HL :].T
+        gnf[...] = gains[0:1, :]
+        gna[...] = gains[1:2, :]
+        for s in range(2):
+            gsi[s] = h_gw1[:, s * F : (s + 1) * F]
+        gso[...] = h_gw1[:, 2 * F :].T
 
 
 def fused(
@@ -958,35 +1107,35 @@
     C = round_up(CAP, 16)
     S = G * C
     half, share, zs = D // 2, D // G, G // 4
-    row_index = jnp.arange(T, dtype=jnp.int32)
-    ends = PROMPT + jnp.cumsum(cont_lengths[0], dtype=jnp.int32)
-    later = jnp.sum((row_index[:, None] >= ends[None, :]).astype(jnp.int32), axis=1)
-    segment = jnp.where(row_index < PROMPT, 0, 1 + later)
-    member = (segment[:, None] == jnp.arange(1, ends.shape[0] + 1, dtype=jnp.int32)[None, :])
-    offset = jnp.sum(member.astype(jnp.int32) * (ends - cont_lengths[0])[None, :], axis=1)
-    position = jnp.where(segment == 0, row_index, PROMPT + row_index - offset)
-    lane = jnp.arange(128, dtype=jnp.int32)
-    inv_freq = 10000.0 ** (-(lane % (HD // 2)).astype(f32) / (HD // 2))
-    angles = position.astype(f32)[:, None] * inv_freq[None, :]
-    cos = jnp.cos(angles)
-    sin = jnp.sin(angles) * jnp.where(lane % HD < HD // 2, -1.0, 1.0)[None, :]
-    segr, segc = segment[None, :], segment[:, None]
-    na, nf = norm_attn[None, :], norm_ffn[None, :]
-    rT, gT = routes.T, route_gates.T
+    W1, W2 = 3 * F, 4 * HL + 128
     shape = jax.ShapeDtypeStruct
     dma = pltpu.SemaphoreType.DMA
+    SM = pl.BlockSpec(memory_space=pltpu.SMEM)
     tile = 256
+    kept = {
+        "qkv": ((3, T, HL), bf16), "lse": ((T, 128), f32), "att": ((T, HL), bf16), "normed_a": ((T, D), bf16),
+        "resid": ((T, D), f32), "plan": ((S, T), bf16), "gate": ((EXPERTS, T), f32), "cos": ((T, 128), f32),
+        "sin": ((T, 128), f32), "part": ((S, D), bf16), "shp": ((T, D), bf16), "dres": ((T, D), f32),
+        "gnf": ((8, D), f32),
+    }
+
+    def keep(*names):
+        return [pltpu.VMEM(*kept[name]) for name in names]
+
     front = pl.pallas_call(
         functools.partial(front_kernel, G),
         out_shape=(
-            shape((3, T, HL), bf16), shape((T, 128), f32), shape((T, HL), bf16),
-            shape((T, D), bf16), shape((T, D), f32), shape((S, T), bf16), shape((EXPERTS, T), f32),
-            shape((S, D), bf16), shape((T, D), bf16), shape((T, D), f32), shape((8, D), f32),
-            shape((D, 3 * F), bf16), shape((2, D, FX), f32), shape((FX, D), f32),
+            *[shape(*k) for k in kept.values()],
+            shape((D, W1), bf16), shape((2, D, FX), bf16), shape((FX, D), bf16),
         ),
-        in_specs=[VM] * 12 + [ANY] * 4,
-        out_specs=(VM,) * 11 + (ANY,) * 3,
+        in_specs=[VM] * 2 + [SM] + [VM] * 2 + [ANY] * 8,
+        out_specs=(ANY,) * (len(kept) + 3),
         scratch_shapes=[
+            pltpu.VMEM((T, D), bf16),
+            pltpu.VMEM((3, D, HL), bf16),
+            pltpu.VMEM((HL, D), bf16),
+            pltpu.VMEM((T, D), bf16),
+            *keep("cos", "sin", "qkv", "lse", "att", "normed_a", "resid", "plan", "gate", "part", "shp", "dres", "gnf"),
             pltpu.VMEM((T, T), f32),
             pltpu.VMEM((T, HL), bf16),
             pltpu.VMEM((HL, D), bf16),
@@ -1010,31 +1159,39 @@
             pltpu.VMEM((S, half), bf16),
             pltpu.VMEM((T, D), bf16),
             pltpu.VMEM((D, S), bf16),
-            pltpu.VMEM((2, D, tile), f32),
-            pltpu.VMEM((2, tile, D), f32),
             pltpu.VMEM((2, D, tile), bf16),
-            dma((6,)), dma((6,)), dma((G,)), dma((G,)), dma((G,)), dma((G,)), dma((G,)), dma((G,)),
-            dma((4,)), dma((4,)), dma((G,)), dma((G,)), dma((4,)), dma((4,)),
+            pltpu.VMEM((2, tile, D), bf16),
+            pltpu.VMEM((2, D, tile), bf16),
+            dma((7,)), dma((7,)), *[dma((G,))] * 8,
+            dma((4,)), dma((4,)), dma((G,)), dma((G,)), dma((8,)), dma((4,)), dma((len(kept),)),
         ],
         compiler_params=pltpu.CompilerParams(
             collective_id=0, has_side_effects=True, vmem_limit_bytes=VMEM_BYTES
         ),
         name="front",
     )(
-        tokens, na, nf, cos, sin, segr, segc, rT, gT, w_qkv, w_attn_out, cotangent,
+        norm_attn, norm_ffn, cont_lengths, routes.T, route_gates.T, tokens, w_qkv, w_attn_out, cotangent,
         shared_in, shared_out, expert_in, expert_out,
     )
-    qkv, lse, att_own, normed_a, resid, plan, gate, part, shp, dres, gnf, gsh, gein, geout = front
-    W1, W2 = 3 * F, 4 * HL + 128
+    kept_out, (gsh, gein, geout) = front[: len(kept)], front[len(kept) :]
     fold = [(zs, 2, share), (zs, 2, share), (zs, share), (zs, share), (zs - 1, share)]
-    out, gtok, gw1, gw2 = pl.pallas_call(
+    raw = pl.pallas_call(
         functools.partial(back_kernel, G),
         out_shape=(
             shape((T, D), bf16), shape((T, D), bf16), shape((share, W1), f32), shape((share, W2), f32),
         ),
-        in_specs=[VM] * 19 + [ANY],
+        in_specs=[VM, SM] + [ANY] * (4 + len(kept)),
         out_specs=(VM,) * 4,
         scratch_shapes=[
+            pltpu.VMEM((T, D), bf16),
+            pltpu.VMEM((3, D, HL), bf16),
+            pltpu.VMEM((HL, D), bf16),
+            *keep("qkv", "lse", "att", "normed_a"),
+            pltpu.VMEM((T, half), f32),
+            *keep("plan", "gate", "cos", "sin"),
+            pltpu.VMEM((S, half), bf16),
+            pltpu.VMEM((T, half), bf16),
+            *keep("dres", "gnf"),
             pltpu.VMEM((T, T), f32),
             pltpu.VMEM((T, D), bf16),
             pltpu.VMEM((T, HL), bf16),
@@ -1054,28 +1211,43 @@
             *[pltpu.VMEM((*s, W1), bf16) for s in fold],
             *[pltpu.VMEM((*s, W2), bf16) for s in fold],
             dma((4,)), dma((4,)), dma((4,)), dma((4,)), dma((G,)), dma((G,)),
-            dma((2, 1 + zs)), dma((2, 1 + zs)), dma((1,)),
+            dma((3, 1 + zs)), dma((3, 1 + zs)), dma((17,)),
         ],
         compiler_params=pltpu.CompilerParams(
             collective_id=1, has_side_effects=True, vmem_limit_bytes=VMEM_BYTES
         ),
         name="back",
     )(
-        tokens, na, cos, sin, segr, segc, w_qkv, w_attn_out, qkv, lse, att_own, normed_a, resid,
-        plan, gate, part, shp, dres, gnf, gsh.reshape(zs, 2, 2, share, W1),
-    )
-    return (
-        out,
-        gtok,
-        gw2[:, : 3 * HL].reshape(share, 3, HL).transpose(1, 0, 2),
-        gw2[:, 3 * HL : 4 * HL].T,
-        gw2[:, 4 * HL + 1],
-        gw2[:, 4 * HL],
-        gw1[:, : 2 * F].reshape(share, 2, F).transpose(1, 0, 2),
-        gw1[:, 2 * F :].T,
-        gein,
-        geout,
-    )
+        norm_attn, cont_lengths, tokens, w_qkv, w_attn_out, *kept_out, gsh.reshape(zs, 2, 2, share, W1),
+    )
+    steps = 4
+
+    def rows_of(*dims):
+        return pl.BlockSpec(dims, lambda i: (0,) * (len(dims) - 2) + (i, 0))
+
+    def whole(*dims):
+        return pl.BlockSpec(dims, lambda i: (0,) * len(dims))
+
+    results = ((3, share, HL), (HL, share), (1, share), (1, share), (2, share, F), (F, share))
+    out, gtok, gqkv, gao, gna, gnf, gsi, gso, gein, geout = pl.pallas_call(
+        functools.partial(finish_kernel, HL, F),
+        grid=(steps,),
+        out_shape=(
+            shape((T, D), bf16), shape((T, D), bf16), *[shape(r, f32) for r in results],
+            shape((2, D, FX), f32), shape((FX, D), f32),
+        ),
+        in_specs=[
+            rows_of(T // steps, D), rows_of(T // steps, D), whole(share, W1), whole(share, W2),
+            rows_of(2, D // steps, FX), rows_of(FX // steps, D),
+        ],
+        out_specs=(
+            rows_of(T // steps, D), rows_of(T // steps, D), *[whole(*r) for r in results],
+            rows_of(2, D // steps, FX), rows_of(FX // steps, D),
+        ),
+        compiler_params=pltpu.CompilerParams(vmem_limit_bytes=VMEM_BYTES),
+        name="finish",
+    )(*raw, gein, geout)
+    return (out, gtok, gqkv, gao, gna[0], gnf[0], gsi, gso, gein, geout)
 
 
 def solution(mesh):

time: 314 us -> 275 us (0.88)
  local copies, waits for them, and re-layouts: 21 us -> 3.57 us
  Pallas kernels: 284 us -> 270 us
  other arithmetic: 5.02 us -> 0 us
    unnamed x11 -> x2, local copies, waits for them, and re-layouts: 11 us -> 3.57 us
    pallas_call x1, Pallas kernels: 116 us -> 108 us  [fused(): pl.pallas_call(functools.partial(back_kernel, G), out_shape=(shape((T, D)...]
    pallas_call x1 -> x2, Pallas kernels: 168 us -> 162 us  [the longest x1 153 us: fused(): pl.pallas_call(functools.partial(front_kernel, G), out_shape=(*[shape(*k)...]
    slice x3 -> x0, local copies, waits for them, and re-layouts: 3.51 us -> none  [the longest x1 1.53 us: fused(): gw2[:, 4 * HL]]
where the time goes in v2:
time: 275 us; the launch traced here: 274 us
  Pallas kernels  270 us (98%)
  local copies, waits for them, and re-layouts  3.57 us (1%)
    pallas_call x1, Pallas kernels, fused(): pl.pallas_call(functools.partial(front_kernel, G), out_shape=(*[shape(*k)...  153 us
    pallas_call x1, Pallas kernels, fused(): pl.pallas_call(functools.partial(back_kernel, G), out_shape=(shape((T, D)...  108 us
    pallas_call x1, Pallas kernels, fused(): pl.pallas_call(functools.partial(finish_kernel, HL, F), grid=(steps,), ou...  8.35 us

profile of v2, /device:TPU:0, one launch (start us, length us, event | category | flops | bytes accessed | tf_op | source)
XLA Modules:
  0.0 274.2 jit_solution(1393167282635847238)
XLA Ops:
  0.6 153.1 %front.1 = (bf16[3,576,384]{2,1,0:T(8,128)(2,1)}, f32[576,128]{1,0:T(8,128)}, bf16[576,384]{1,0:T(8,128)(2,1)}, bf16[576,768]{1,0:T(8,128)(2,1)}, f32[576,768]{1...) custom-call(f32[768]{0:T(1024)} %na.3, f32[768]{0:T(1024)} %nf.1, ...), custom_call_target="tpu_custom_call" | custom-call | tf_op jit(solution)/shard_map/front/pallas_call | solution.py:1125
  153.8 108.5 %back.1 = (bf16[576,768]{1,0:T(8,128)(2,1)}, bf16[576,768]{1,0:T(8,128)(2,1)}, f32[48,3072]{1,0:T(8,128)}, f32[48,1664]{1,0:T(8,128)}) custom-call(f32[768]{0:T(1024)} %na.3, s32[1,2]{1,0:T(1,128)} %lens.3, bf16[576,768]{1,0:T(8,128)(2,1)} %h_tok.3, bf16[3,768,384]{2,1,0:T(8,128)(2,1)} %h_wqkv.3, bf16[384,768]{1,0:T(8,128)(2,1)} %h_wo.3, ...), custom_call_target="tpu_custom_call" | custom-call | tf_op jit(solution)/shard_map/back/pallas_call | solution.py:1178
  262.3 8.4 %finish.1 = (bf16[576,768]{1,0:T(8,128)(2,1)}, bf16[576,768]{1,0:T(8,128)(2,1)}, f32[3,48,384]{2,1,0:T(8,128)}, f32[384,48]{1,0:T(8,128)}, f32[1,48]{1,0:T(1,128...) custom-call(bf16[576,768]{1,0:T(8,128)(2,1)} %get-tuple-element.54.h, ...), custom_call_target="tpu_custom_call" | custom-call | tf_op jit(solution)/shard_map/finish/pallas_call | solution.py:1232
  270.6 1.7 copy.23
  272.3 1.9 copy.24

commit v3 on v0

--- a/solution.py
+++ b/solution.py
@@ -1,6 +1,11 @@
+import functools
+import math
+
 import jax
 import jax.numpy as jnp
 from jax import lax
+from jax.experimental import pallas as pl
+from jax.experimental.pallas import tpu as pltpu
 from jax.sharding import PartitionSpec as P
 
 HD = 64
@@ -279,6 +284,895 @@
     )
 
 
+VMEM_BYTES = 64000 * 1024
+FOLD = 96
+SPLIT = 7
+EARLY = 2
+MESH = pl.DeviceIdType.MESH
+VM = pl.BlockSpec(memory_space=pltpu.VMEM)
+ANY = pl.BlockSpec(memory_space=pl.ANY)
+f32 = jnp.float32
+bf16 = jnp.bfloat16
+
+
+def round_up(value, unit):
+    return (value + unit - 1) // unit * unit
+
+
+def dot(a, b):
+    return jnp.dot(a, b, preferred_element_type=f32)
+
+
+def dot_nt(a, b):
+    return lax.dot_general(a, b, (((1,), (1,)), ((), ())), preferred_element_type=f32)
+
+
+def dot_tn(a, b):
+    return lax.dot_general(a, b, (((0,), (0,)), ((), ())), preferred_element_type=f32)
+
+
+def sigmoid(values):
+    return 0.5 * jnp.tanh(0.5 * values) + 0.5
+
+
+def swap_halves(values):
+    lane = lax.broadcasted_iota(jnp.int32, values.shape, 1)
+    ahead = pltpu.roll(values, values.shape[1] - HD // 2, 1)
+    behind = pltpu.roll(values, HD // 2, 1)
+    return jnp.where(lax.rem(lane, HD) < HD // 2, ahead, behind)
+
+
+def hello(groups):
+    me, t = lax.axis_index("dp"), lax.axis_index("tensor")
+    barrier = pltpu.get_barrier_semaphore()
+
+    def greet(k, carry):
+        pl.semaphore_signal(
+            barrier, inc=1, device_id=(lax.rem(me + k, groups), t), device_id_type=MESH
+        )
+        return carry
+
+    lax.fori_loop(1, groups, greet, 0)
+    pl.semaphore_signal(barrier, inc=1, device_id=(me, 1 - t), device_id_type=MESH)
+    pl.semaphore_wait(barrier, groups)
+
+
+def segment_of(index, lens):
+    segment = jnp.where(index < PROMPT, 0, 1)
+    end = PROMPT
+    for c in range(lens.shape[1]):
+        end = end + lens[0, c]
+        segment = segment + jnp.where(index >= end, 1, 0)
+    return segment
+
+
+def position_of(index, lens):
+    segment = segment_of(index, lens)
+    position, end = index, PROMPT
+    for c in range(lens.shape[1]):
+        position = jnp.where(segment == c + 1, PROMPT + index - end, position)
+        end = end + lens[0, c]
+    return position
+
+
+def fill_bias(bias, lens, rows):
+    step = FOLD
+
+    def body(i, carry):
+        at = pl.ds(pl.multiple_of(i * step, step), step)
+        row = lax.broadcasted_iota(jnp.int32, (step, rows), 0) + i * step
+        col = lax.broadcasted_iota(jnp.int32, (step, rows), 1)
+        own = segment_of(lax.broadcasted_iota(jnp.int32, (step, 1), 0) + i * step, lens)
+        other = segment_of(lax.broadcasted_iota(jnp.int32, (1, rows), 1), lens)
+        ok = (col <= row) & ((other == 0) | (other == own))
+        bias[at, :] = jnp.where(ok, 0.0, -1000000000.0)
+        return carry
+
+    lax.fori_loop(0, rows // step, body, 0)
+
+
+def fill_angles(cos, sin, lens, rows):
+    step = FOLD
+
+    def body(i, carry):
+        at = pl.ds(pl.multiple_of(i * step, step), step)
+        lane = lax.broadcasted_iota(jnp.int32, (step, 128), 1)
+        row = lax.broadcasted_iota(jnp.int32, (step, 128), 0) + i * step
+        power = lax.rem(lane, HD // 2).astype(f32) * (-math.log(10000.0) / (HD // 2))
+        angle = position_of(row, lens).astype(f32) * jnp.exp(power)
+        cos[at, :] = jnp.cos(angle)
+        sine = jnp.sin(angle)
+        sin[at, :] = jnp.where(lax.rem(lane, HD) < HD // 2, -sine, sine)
+        return carry
+
+    lax.fori_loop(0, rows // step, body, 0)
+
+
+def send(src, dst, ssem, rsem, to):
+    return pltpu.make_async_remote_copy(
+        src_ref=src, dst_ref=dst, send_sem=ssem, recv_sem=rsem, device_id=to, device_id_type=MESH
+    )
+
+
+def layer_kernel(
+    G, na, nf, lens, rT, gT, h_tok, h_wqkv, h_wo, h_cot, si, so, ei, eo,
+    h_out, h_gtok, h_gw1, h_gw2, gein, geout,
+    tok, wqkv, wo, cot, cos, sin, qkv, lse, att_own, normed_a, resid, plan, gate, slot, bias, att, wo2,
+    csend, drows, rows, rets, ret, dxr, dnsh, dnsh_r, dnb, shp, partr, ro, shpr, gna, gnar,
+    a1, b1, d1, a2, b2, d2,
+    s_x, r_x, s_c, r_c, s_cf, r_cf, s_r, r_r, s_f, r_f, s_dx, r_dx, s_ret, r_ret, s_p, r_p, s_po, r_po,
+    s_k, r_k, s_y, r_y, s_z, r_z, lsem, osem,
+):
+    T, D = tok.shape
+    HL = wqkv.shape[2]
+    F = si.shape[2]
+    S = plan.shape[0]
+    C = S // G
+    half, share, zs = D // 2, D // G, G // 4
+    W2 = a2.shape[3]
+    scale = HD ** (-0.5)
+    me, t = lax.axis_index("dp"), lax.axis_index("tensor")
+    core, y, z = lax.rem(me, 2), lax.rem(me // 2, 2), me // 4
+    mine = pl.ds(pl.multiple_of(t * half, 128), half)
+    theirs = pl.ds(pl.multiple_of((1 - t) * half, 128), half)
+    partner = (me, 1 - t)
+    sibling = (me + 1 - 2 * core, t)
+    neighbour = (me + 2 - 4 * y, t)
+    per, tile = 4, 256
+    M, chunks, tiles = per * C, G // per, F // tile
+
+    loads = [
+        pltpu.make_async_copy(a, b, lsem.at[i])
+        for i, (a, b) in enumerate(((h_cot, cot), (h_tok, tok), (h_wqkv, wqkv), (h_wo, wo)))
+    ]
+    for c in loads:
+        c.start()
+    hello(G)
+    part_wo = pl.ds(pl.multiple_of(core * (HL // 2), 16), HL // 2)
+    wo_copy = send(h_wo.at[part_wo], wo2.at[part_wo], s_x.at[0], r_x.at[0], partner)
+    wo_copy.start()
+    wo_pass = send(wo2.at[part_wo], wo2.at[part_wo], s_x.at[6], r_x.at[6], sibling)
+
+    def row_at(k):
+        return pl.ds(pl.multiple_of(k * C, C), C)
+
+    def chunk_at(c):
+        return pl.ds(c * M, M)
+
+    names = lax.broadcasted_iota(jnp.int32, (EXPERTS, T), 0)
+    picks0, picks1 = rT[0:1, :] == names, rT[1:2, :] == names
+    member = jnp.where(picks0 | picks1, 1.0, 0.0)
+    upper = jnp.where(
+        lax.broadcasted_iota(jnp.int32, (T, T), 0) < lax.broadcasted_iota(jnp.int32, (T, T), 1),
+        1.0,
+        0.0,
+    ).astype(bf16)
+    slot[...] = jnp.where(member > 0.0, dot(member.astype(bf16), upper), -1.0)
+    gate[...] = jnp.where(picks0, gT[0:1, :], 0.0) + jnp.where(picks1, gT[1:2, :], 0.0)
+
+    def cot_copy(k):
+        return send(
+            csend.at[row_at(k)], drows.at[row_at(k)], s_c.at[k], r_c.at[k], (lax.rem(me + k, G), t)
+        )
+
+    def cot_half(k):
+        return send(
+            csend.at[row_at(k), mine], drows.at[row_at(k), mine], s_c.at[k], r_c.at[k],
+            (lax.rem(me + k, G), t),
+        )
+
+    def cot_pass(k):
+        return send(
+            drows.at[row_at(k), mine], drows.at[row_at(k), mine], s_cf.at[k], r_cf.at[k], partner
+        )
+
+    def cot_step(k, carry):
+        e = lax.rem(me + k, G)
+        at = row_at(k)
+        place = lax.broadcasted_iota(jnp.int32, (C, T), 0).astype(f32)
+        hit = slot[pl.ds(e, 1), :] == place
+        picked = jnp.where(hit, 1.0, 0.0).astype(bf16)
+        plan[at, :] = picked
+        weight = jnp.sum(jnp.where(hit, gate[pl.ds(e, 1), :], 0.0), axis=1, keepdims=True)
+        grad = (dot(picked, cot[...]) * weight).astype(bf16)
+        csend[at, :] = grad
+
+        @pl.when(k > SPLIT)
+        def _():
+            cot_copy(k).start()
+
+        @pl.when((k > 0) & (k <= SPLIT))
+        def _():
+            cot_half(k).start()
+
+        @pl.when(k == 0)
+        def _():
+            drows[at, :] = grad
+
+        return carry
+
+    loads[0].wait()
+    lax.fori_loop(0, G, cot_step, 0)
+
+    fill_angles(cos, sin, lens, T)
+    fill_bias(bias, lens, T)
+    loads[1].wait()
+
+    def norm_step(i, carry):
+        at = pl.ds(pl.multiple_of(i * FOLD, FOLD), FOLD)
+        x = tok[at, :].astype(f32)
+        r = lax.rsqrt(jnp.mean(x * x, axis=1, keepdims=True) + epsilon)
+        normed_a[at, :] = (x * r * na[...].reshape(1, D)).astype(bf16)
+        return carry
+
+    lax.fori_loop(0, T // FOLD, norm_step, 0)
+    loads[2].wait()
+    loads[3].wait()
+
+    def project(s, turned):
+        full = dot(normed_a[...], wqkv[s])
+        for j in range(HL // 128):
+            x = full[:, j * 128 : (j + 1) * 128]
+            if turned:
+                x = x * cos[...] + swap_halves(x) * sin[...]
+            qkv[s, :, j * 128 : (j + 1) * 128] = x.astype(bf16)
+
+    project(0, True)
+    project(1, True)
+    project(2, False)
+    lane = lax.broadcasted_iota(jnp.int32, (T, 128), 1)
+
+    def att_copy(j):
+        at = pl.ds(pl.multiple_of(j * 128, 128), 128)
+        return send(att_own.at[:, at], att.at[:, at], s_x.at[1 + j], r_x.at[1 + j], partner)
+
+    lse[...] = jnp.zeros_like(lse)
+
+    def attend(j, carry):
+        at = pl.ds(pl.multiple_of(j * 128, 128), 128)
+        q, k, v = qkv[0, :, at], qkv[1, :, at], qkv[2, :, at]
+        outs = []
+        for i in range(2):
+            inside = (lane < HD) if i == 0 else (lane >= HD)
+            s = dot_nt(jnp.where(inside, q, jnp.zeros_like(q)), k) * scale + bias[...]
+            top = jnp.max(s, axis=1, keepdims=True)
+            e = jnp.exp(s - top)
+            total = jnp.sum(e, axis=1, keepdims=True)
+            p = (e * (1.0 / total)).astype(bf16)
+            lse[...] = jnp.where(lane == 2 * j + i, top + jnp.log(total), lse[...])
+            outs.append(dot(p, v))
+        att_own[:, at] = jnp.where(lane < HD, outs[0], outs[1]).astype(bf16)
+        att_copy(j).start()
+        return carry
+
+    wo_copy.wait()
+    wo_pass.start()
+    lax.fori_loop(0, HL // 128, attend, 0)
+    own_out = dot(att_own[...], wo[...])
+    wo_pass.wait()
+    for j in range(HL // 128):
+        att_copy(j).wait()
+    for k in range(1, SPLIT + 1):
+        cot_half(k).wait_recv()
+        cot_pass(k).start()
+    resid[...] = tok[...].astype(f32) + own_out + dot(att[...], wo2[...])
+
+    def row_copy(k):
+        return send(
+            rets.at[row_at(k)], rows.at[row_at(k), mine], s_r.at[k], r_r.at[k], (lax.rem(me + k, G), t)
+        )
+
+    def row_pass(k):
+        return send(
+            rows.at[row_at(k), mine], rows.at[row_at(k), mine], s_f.at[k], r_f.at[k], partner
+        )
+
+    def hand_on(k):
+        row_copy(k).wait_recv()
+        row_pass(k).start()
+
+    def dx_copy(c):
+        return send(csend.at[chunk_at(c), theirs], dxr.at[chunk_at(c)], s_dx.at[c], r_dx.at[c], partner)
+
+    def ret_copy(k):
+        return send(
+            rets.at[row_at(k)], ret.at[row_at(k)], s_ret.at[k], r_ret.at[k], (lax.rem(me - k + G, G), t)
+        )
+
+    def return_chunk(c):
+        dx_copy(c).wait_recv()
+        total = (csend[chunk_at(c), mine].astype(f32) + dxr[chunk_at(c), :].astype(f32)).astype(bf16)
+        for k in range(c * per, (c + 1) * per):
+            if k > 0:
+                row_copy(k).wait_send()
+        rets[chunk_at(c), :] = total
+        for k in range(c * per, (c + 1) * per):
+            if k > 0:
+                ret_copy(k).start()
+        if c == 0:
+            ret[0:C, :] = total[0:C, :]
+
+    def part_copy(c):
+        return send(csend.at[chunk_at(c), theirs], partr.at[chunk_at(c)], s_p.at[c], r_p.at[c], partner)
+
+    def po_copy(k):
+        return send(
+            rets.at[row_at(k)], ro.at[row_at(k)], s_po.at[k], r_po.at[k], (lax.rem(me - k + G, G), t)
+        )
+
+    def return_part(c):
+        part_copy(c).wait_recv()
+        total = (csend[chunk_at(c), mine].astype(f32) + partr[chunk_at(c), :].astype(f32)).astype(bf16)
+        for k in range(c * per, (c + 1) * per):
+            if k > 0:
+                ret_copy(k).wait_send()
+        rets[chunk_at(c), :] = total
+        for k in range(c * per, (c + 1) * per):
+            if k > 0:
+                po_copy(k).start()
+        if c == 0:
+            ro[0:C, :] = total[0:C, :]
+
+    dnsh_copy = send(dnsh.at[:, theirs], dnsh_r, s_x.at[4], r_x.at[4], partner)
+    shp_copy = send(shp.at[:, theirs], shpr, s_x.at[7], r_x.at[7], partner)
+
+    def columns(p):
+        return slice(p * F, (p + 1) * F) if p < 3 else slice(0, W2)
+
+    def fold_bufs(p):
+        return (a1, b1, d1) if p < 3 else (a2, b2, d2)
+
+    def fold_y(p):
+        a, b, d = fold_bufs(p)
+        return send(
+            a.at[:, 1 - y, :, columns(p)], b.at[:, :, columns(p)], s_y.at[p], r_y.at[p], neighbour
+        )
+
+    def fold_z(p, k):
+        a, b, d = fold_bufs(p)
+        to = lax.rem(z + k, zs)
+        return send(
+            b.at[to, :, columns(p)], d.at[k - 1, :, columns(p)], s_z.at[p, k - 1], r_z.at[p, k - 1],
+            (to * 4 + lax.rem(me, 4), t),
+        )
+
+    def fold_on(p):
+        a, b, d = fold_bufs(p)
+        fold_y(p).wait()
+
+        def body(i, carry):
+            b[i, :, columns(p)] = (
+                b[i, :, columns(p)].astype(f32) + a[i, y, :, columns(p)].astype(f32)
+            ).astype(bf16)
+            return carry
+
+        lax.fori_loop(0, zs, body, 0)
+        for k in range(1, zs):
+            fold_z(p, k).start()
+
+    def fold_end(p, w):
+        a, b, d = fold_bufs(p)
+        total = b[z, :, columns(p)].astype(f32)
+        for k in range(1, zs):
+            fold_z(p, k).wait()
+            total = total + d[k - 1, :, columns(p)].astype(f32)
+        w[:, columns(p)] = total
+
+    def experts(vsi, vso, vei, veo, act, dgu, normed, tall, wide):
+        weights = [
+            pltpu.make_async_copy(a, b, lsem.at[4 + i])
+            for i, (a, b) in enumerate(((si, vsi), (so, vso), (ei, vei), (eo, veo)))
+        ]
+        for c in weights:
+            c.start()
+
+        def norm2_step(i, carry):
+            at = pl.ds(pl.multiple_of(i * FOLD, FOLD), FOLD)
+            x = resid[at, :]
+            r = lax.rsqrt(jnp.mean(x * x, axis=1, keepdims=True) + epsilon)
+            normed[at, :] = (x * r * nf[...].reshape(1, D)).astype(bf16)
+            return carry
+
+        lax.fori_loop(0, T // FOLD, norm2_step, 0)
+
+        def row_step(k, carry):
+            values = dot(plan[row_at(k), :], normed[:, mine]).astype(bf16)
+            rets[row_at(k), :] = values
+
+            @pl.when(k > 0)
+            def _():
+                row_copy(k).start()
+
+            @pl.when(k == 0)
+            def _():
+                rows[row_at(k), mine] = values
+                row_pass(k).start()
+
+            return carry
+
+        lax.fori_loop(0, G, row_step, 0)
+
+        mid = slice(S - T, S)
+
+        def shared_step(u, carry):
+            at = pl.ds(pl.multiple_of(u * tile, tile), tile)
+            pre = dot(normed[...], vsi[0, :, at])
+            up = dot(normed[...], vsi[1, :, at])
+            d_act = dot_nt(cot[...], vso[at, :])
+            s = sigmoid(pre)
+            gs = pre * s
+            act[mid, at] = (gs * up).astype(bf16)
+            dgu[0, mid, at] = (d_act * up * (s + gs * (1.0 - s))).astype(bf16)
+            dgu[1, mid, at] = (d_act * gs).astype(bf16)
+            return carry
+
+        def tile_at(i):
+            return pl.ds(pl.multiple_of(i * tile, tile), tile)
+
+        def fold_core(i):
+            return send(
+                tall.at[lax.rem(i, 2), :, :, 1 - core], a1.at[:, :, :, tile_at(i)], s_k.at[i], r_k.at[i],
+                sibling,
+            )
+
+        def core_end(i):
+            fold_core(i).wait()
+
+            def body(n, carry):
+                u, v = n // 2, lax.rem(n, 2)
+                a1[u, v, :, tile_at(i)] = (
+                    a1[u, v, :, tile_at(i)].astype(f32) + tall[lax.rem(i, 2), u, v, core].astype(f32)
+                ).astype(bf16)
+                return carry
+
+            lax.fori_loop(0, 2 * zs, body, 0)
+
+        def shared_grads(p):
+            def body(i, carry):
+                at = tile_at(i - p * tiles)
+                if p < 2:
+                    grad = dot(vsi[0, :, 0:T], dgu[p, mid, at])
+                else:
+                    grad = dot(vsi[1, :, 0:T], act[mid, at])
+                tall[lax.rem(i, 2)] = grad.astype(bf16).reshape(tall.shape[1:])
+                fold_core(i).start()
+
+                @pl.when(i > p * tiles)
+                def _():
+                    core_end(i - 1)
+
+                return carry
+
+            lax.fori_loop(p * tiles, (p + 1) * tiles, body, 0)
+            core_end((p + 1) * tiles - 1)
+            fold_y(p).start()
+
+        def expert_chunk(c):
+            for k in range(c * per, (c + 1) * per):
+                row_pass(k).wait_recv()
+                if k > SPLIT:
+                    cot_copy(k).wait_recv()
+                elif k > 0:
+                    cot_pass(k).wait_recv()
+            block = chunk_at(c)
+
+            def unit_step(u, carry):
+                at = pl.ds(pl.multiple_of(u * tile, tile), tile)
+                pre = dot(rows[block, :], vei[0, :, at])
+                up = dot(rows[block, :], vei[1, :, at])
+                d_act = dot_nt(drows[block, :], veo[at, :])
+                s = sigmoid(pre)
+                gs = pre * s
+                act[block, at] = (gs * up).astype(bf16)
+                dgu[0, block, at] = (d_act * up * (s + gs * (1.0 - s))).astype(bf16)
+                dgu[1, block, at] = (d_act * gs).astype(bf16)
+                return carry
+
+            lax.fori_loop(0, tiles, unit_step, 0)
+            dx = dot_nt(dgu[0, block, :], vei[0]) + dot_nt(dgu[1, block, :], vei[1])
+            for k in range(c * per, (c + 1) * per):
+                if k > SPLIT:
+                    cot_copy(k).wait_send()
+                elif k > 0:
+                    cot_half(k).wait_send()
+            csend[block, :] = dx.astype(bf16)
+            dx_copy(c).start()
+
+        weights[0].wait()
+        weights[1].wait()
+        lax.fori_loop(0, tiles, shared_step, 0)
+        for k in range(1, 4):
+            hand_on(k)
+        dnsh[...] = (dot_nt(dgu[0, mid, :], vsi[0]) + dot_nt(dgu[1, mid, :], vsi[1])).astype(bf16)
+        dnsh_copy.start()
+        weights[2].wait()
+        weights[3].wait()
+        for k in range(4, 6):
+            hand_on(k)
+        vsi[0, :, 0:T] = normed[...].T
+        vsi[1, :, 0:T] = cot[...].T
+        expert_chunk(0)
+        for k in range(6, 8):
+            hand_on(k)
+        shp[...] = dot(act[mid, :], vso[...]).astype(bf16)
+        shared_grads(0)
+        return_chunk(0)
+        expert_chunk(1)
+        for k in range(8, 12):
+            hand_on(k)
+        shared_grads(1)
+        shared_grads(2)
+        return_chunk(1)
+        expert_chunk(2)
+        for k in range(12, G):
+            hand_on(k)
+        return_chunk(2)
+        expert_chunk(3)
+
+        def part_chunk(c):
+            dx_copy(c).wait_send()
+            csend[chunk_at(c), :] = dot(act[chunk_at(c), :], veo[...]).astype(bf16)
+
+        for c in range(chunks - 1):
+            part_chunk(c)
+        return_chunk(3)
+        for c in range(EARLY):
+            part_copy(c).start()
+        part_chunk(3)
+        sides = [slice(0, S // 2), slice(S // 2, S)]
+        for n in range(2):
+            vsi[n, :, 0 : S // 2] = rows[sides[n], :].T
+
+        def gein_copy(i):
+            return pltpu.make_async_copy(
+                tall.at[lax.rem(i, 2)], gein.at[i // tiles, :, :, :, :, tile_at(lax.rem(i, tiles))],
+                osem.at[lax.rem(i, 2)],
+            )
+
+        def gein_step(i, carry):
+            @pl.when(i > 1)
+            def _():
+                gein_copy(i - 2).wait()
+
+            at = tile_at(lax.rem(i, tiles))
+            grad = dot(vsi[0, :, 0 : S // 2], dgu[i // tiles, sides[0], at])
+            grad = grad + dot(vsi[1, :, 0 : S // 2], dgu[i // tiles, sides[1], at])
+            tall[lax.rem(i, 2)] = grad.astype(bf16).reshape(tall.shape[1:])
+            gein_copy(i).start()
+            return carry
+
+        lax.fori_loop(0, 2 * tiles, gein_step, 0)
+        for p in range(3):
+            fold_on(p)
+
+        def geout_copy(i):
+            return pltpu.make_async_copy(
+                wide.at[lax.rem(i, 2)], geout.at[tile_at(i), :], osem.at[2 + lax.rem(i, 2)]
+            )
+
+        def geout_step(i, carry):
+            @pl.when(i > 1)
+            def _():
+                geout_copy(i - 2).wait()
+
+            wide[lax.rem(i, 2)] = dot_tn(act[:, tile_at(i)], drows[...]).astype(bf16)
+            geout_copy(i).start()
+            return carry
+
+        lax.fori_loop(0, tiles, geout_step, 0)
+        for k in range(G):
+            row_pass(k).wait_send()
+        for k in range(1, SPLIT + 1):
+            cot_pass(k).wait_send()
+        gein_copy(2 * tiles - 2).wait()
+        gein_copy(2 * tiles - 1).wait()
+        geout_copy(tiles - 2).wait()
+        geout_copy(tiles - 1).wait()
+
+    pl.run_scoped(
+        experts,
+        pltpu.VMEM((2, D, F), bf16),
+        pltpu.VMEM((F, D), bf16),
+        pltpu.VMEM((2, D, F), bf16),
+        pltpu.VMEM((F, D), bf16),
+        pltpu.VMEM((S, F), bf16),
+        pltpu.VMEM((2, S, F), bf16),
+        pltpu.VMEM((T, D), bf16),
+        pltpu.VMEM((2, zs, 2, 2, share, tile), bf16),
+        pltpu.VMEM((2, tile, D), bf16),
+    )
+
+    dnsh_copy.wait()
+    total = dnsh[:, mine].astype(f32) + dnsh_r[...].astype(f32)
+    for c in range(chunks):
+        for k in range(c * per, (c + 1) * per):
+            if k > 0:
+                ret_copy(k).wait_recv()
+        total = total + dot_tn(plan[chunk_at(c), :], ret[chunk_at(c), :])
+    dnb[:, mine] = total.astype(bf16)
+    dnb_copy = send(dnb.at[:, mine], dnb.at[:, mine], s_x.at[5], r_x.at[5], partner)
+    dnb_copy.start()
+
+    dnar, ob = drows.at[0:T], rows.at[0:T]
+    out_copy = send(ob.at[:, mine], ob.at[:, mine], s_x.at[8], r_x.at[8], partner)
+    gna_copy = send(gna, gnar, s_x.at[9], r_x.at[9], partner)
+
+    def attention_back(dres, dresb, da, dqkv, turned, pay, gated, dna, gtok, w1, w2):
+        dna_copy = send(dna, dnar, s_x.at[10], r_x.at[10], partner)
+        for c in range(min(2, EARLY)):
+            return_part(c)
+        dnb_copy.wait()
+        for c in range(EARLY, chunks):
+            part_copy(c).start()
+
+        def dres_step(i, carry):
+            at = pl.ds(pl.multiple_of(i * FOLD, FOLD), FOLD)
+            y_ = dnb[at, :].astype(f32)
+            x = resid[at, :]
+            r = lax.rsqrt(jnp.mean(x * x, axis=1, keepdims=True) + epsilon)
+            a = y_ * nf[...].reshape(1, D)
+            inner = jnp.mean(a * x, axis=1, keepdims=True)
+            xr = x * r
+            value = cot[at, :].astype(f32) + r * a - xr * (r * r * inner)
+            dres[at, :] = value
+            dresb[at, :] = value.astype(bf16)
+            return carry + jnp.sum(y_ * xr, axis=0, keepdims=True)
+
+        gnf = lax.fori_loop(0, T // FOLD, dres_step, jnp.zeros((1, D), f32))
+        da[...] = dot_nt(dresb[...], wo[...]).astype(bf16)
+
+        def attend_back(j, carry):
+            at = pl.ds(pl.multiple_of(j * 128, 128), 128)
+            q, k, v, g = qkv[0, :, at], qkv[1, :, at], qkv[2, :, at], da[:, at]
+            none = jnp.zeros_like(q)
+            dq = dk = dv = jnp.zeros((T, 128), f32)
+            for i in range(2):
+                inside = (lane < HD) if i == 0 else (lane >= HD)
+                qi, ki, gi = (jnp.where(inside, x, none) for x in (q, k, g))
+                total = jnp.sum(jnp.where(lane == 2 * j + i, lse[...], 0.0), axis=1, keepdims=True)
+                p = jnp.exp(dot_nt(qi, k) * scale + bias[...] - total)
+                dp = dot_nt(gi, v)
+                inner = jnp.sum(dp * p, axis=1, keepdims=True)
+                ds = (p * (dp - inner)).astype(bf16)
+                dv = dv + dot_tn(p.astype(bf16), gi)
+                dq = dq + dot(ds, ki)
+                dk = dk + dot_tn(ds, qi)
+            dq, dk = dq * scale, dk * scale
+            dqkv[0, :, at] = (dq * cos[...] - swap_halves(dq) * sin[...]).astype(bf16)
+            dqkv[1, :, at] = (dk * cos[...] - swap_halves(dk) * sin[...]).astype(bf16)
+            dqkv[2, :, at] = dv.astype(bf16)
+            return carry
+
+        lax.fori_loop(0, HL // 128, attend_back, 0)
+
+        dna[...] = (
+            dot_nt(dqkv[0], wqkv[0]) + dot_nt(dqkv[1], wqkv[1]) + dot_nt(dqkv[2], wqkv[2])
+        ).astype(bf16)
+        dna_copy.start()
+        shp_copy.start()
+
+        def gain_step(i, carry):
+            at = pl.ds(pl.multiple_of(i * FOLD, FOLD), FOLD)
+            x = tok[at, :].astype(f32)
+            r = lax.rsqrt(jnp.mean(x * x, axis=1, keepdims=True) + epsilon)
+            return carry + jnp.sum(dna[at, :].astype(f32) * x * r, axis=0, keepdims=True)
+
+        gna[...] = jnp.broadcast_to(
+            lax.fori_loop(0, T // FOLD, gain_step, jnp.zeros((1, D), f32)), gna.shape
+        )
+        gna_copy.start()
+        for c in range(min(2, EARLY), chunks):
+            return_part(c)
+
+        turned[...] = normed_a[...].T
+        for s in range(3):
+            pay[:, :, :, :, s * HL : (s + 1) * HL] = (
+                dot(turned[...], dqkv[s]).astype(bf16).reshape(zs, 2, 2, share, HL)
+            )
+        turned[...] = dresb[...].T
+        pay[:, :, :, :, 3 * HL : 4 * HL] = (
+            dot(turned[...], att_own[...]).astype(bf16).reshape(zs, 2, 2, share, HL)
+        )
+        gna_copy.wait()
+        row = lax.broadcasted_iota(jnp.int32, (128, D), 0)
+        gains = jnp.where(row == 0, gnf, jnp.where(row == 1, gna[0:1, :] + gnar[0:1, :], 0.0))
+        pay[:, :, :, :, 4 * HL :] = gains.T.astype(bf16).reshape(zs, 2, 2, share, 128)
+        core_copy = send(pay.at[:, :, 1 - core], a2, s_x.at[11], r_x.at[11], sibling)
+        core_copy.start()
+        core_copy.wait()
+
+        def body(n, carry):
+            u, v = n // 2, lax.rem(n, 2)
+            a2[u, v] = (a2[u, v].astype(f32) + pay[u, v, core].astype(f32)).astype(bf16)
+            return carry
+
+        lax.fori_loop(0, 2 * zs, body, 0)
+        fold_y(3).start()
+        for p in range(3):
+            fold_end(p, w1)
+        fold_on(3)
+
+        shp_copy.wait()
+        mixed = shp[:, mine].astype(f32) + shpr[...].astype(f32)
+        for c in range(chunks):
+            for k in range(c * per, (c + 1) * per):
+                if k > 0:
+                    po_copy(k).wait_recv()
+                weights = gate[pl.ds(lax.rem(me + k, G), 1), :]
+                gated[(k - c * per) * C : (k - c * per + 1) * C, :] = (
+                    plan[row_at(k), :].astype(f32) * weights
+                ).astype(bf16)
+            mixed = mixed + dot_tn(gated[...], ro[chunk_at(c), :])
+        ob[:, mine] = (resid[:, mine] + mixed).astype(bf16)
+        out_copy.start()
+        dna_copy.wait()
+
+        def last_step(i, carry):
+            at = pl.ds(pl.multiple_of(i * FOLD, FOLD), FOLD)
+            x = tok[at, :].astype(f32)
+            r = lax.rsqrt(jnp.mean(x * x, axis=1, keepdims=True) + epsilon)
+            a = (dna[at, :].astype(f32) + dnar[at, :].astype(f32)) * na[...].reshape(1, D)
+            inner = jnp.mean(a * x, axis=1, keepdims=True)
+            gtok[at, :] = (dres[at, :] + r * a - x * (r * r * r * inner)).astype(bf16)
+            return carry
+
+        lax.fori_loop(0, T // FOLD, last_step, 0)
+        fold_end(3, w2)
+        ends = [
+            pltpu.make_async_copy(a, b, osem.at[i])
+            for i, (a, b) in enumerate(((gtok, h_gtok), (w1, h_gw1), (w2, h_gw2), (ob, h_out)))
+        ]
+        for c in ends[:3]:
+            c.start()
+        out_copy.wait()
+        ends[3].start()
+        for c in ends:
+            c.wait()
+
+    pl.run_scoped(
+        attention_back,
+        pltpu.VMEM((T, D), f32),
+        pltpu.VMEM((T, D), bf16),
+        pltpu.VMEM((T, HL), bf16),
+        pltpu.VMEM((3, T, HL), bf16),
+        pltpu.VMEM((D, T), bf16),
+        pltpu.VMEM((zs, 2, 2, share, W2), bf16),
+        pltpu.VMEM((M, T), bf16),
+        pltpu.VMEM((T, D), bf16),
+        pltpu.VMEM((T, D), bf16),
+        pltpu.VMEM((share, 3 * F), f32),
+        pltpu.VMEM((share, W2), f32),
+    )
+    for c in range(chunks):
+        part_copy(c).wait_send()
+    for k in range(1, G):
+        po_copy(k).wait_send()
+
+
+def finish_kernel(
+    HL, F, h_out, h_gtok, h_gw1, h_gw2, h_gein, h_geout,
+    out, gtok, gqkv, gao, gna, gnf, gsi, gso, gein, geout,
+):
+    out[...] = h_out[...]
+    gtok[...] = h_gtok[...]
+    gein[...] = h_gein[...].astype(f32)
+    geout[...] = h_geout[...].astype(f32)
+
+    @pl.when(pl.program_id(0) == 0)
+    def _():
+        for s in range(3):
+            gqkv[s] = h_gw2[:, s * HL : (s + 1) * HL]
+        gao[...] = h_gw2[:, 3 * HL : 4 * HL].T
+        gains = h_gw2[:, 4 * HL :].T
+        gnf[...] = gains[0:1, :]
+        gna[...] = gains[1:2, :]
+        for s in range(2):
+            gsi[s] = h_gw1[:, s * F : (s + 1) * F]
+        gso[...] = h_gw1[:, 2 * F :].T
+
+
+def fused(
+    tokens, cont_lengths, routes, route_gates, w_qkv, w_attn_out, norm_attn, norm_ffn,
+    shared_in, shared_out, expert_in, expert_out, cotangent,
+):
+    T, D = tokens.shape
+    G = lax.axis_size("dp")
+    HL, F = w_qkv.shape[2], shared_in.shape[2]
+    C = round_up(CAP, 16)
+    S = G * C
+    half, share, zs = D // 2, D // G, G // 4
+    W1, W2 = 3 * F, 4 * HL + 128
+    shape = jax.ShapeDtypeStruct
+    dma = pltpu.SemaphoreType.DMA
+    SM = pl.BlockSpec(memory_space=pltpu.SMEM)
+    out, gtok, gw1, gw2, gein, geout = pl.pallas_call(
+        functools.partial(layer_kernel, G),
+        out_shape=(
+            shape((T, D), bf16), shape((T, D), bf16), shape((share, W1), f32), shape((share, W2), f32),
+            shape((2, zs, 2, 2, share, F), bf16), shape((F, D), bf16),
+        ),
+        in_specs=[VM] * 2 + [SM] + [VM] * 2 + [ANY] * 8,
+        out_specs=(ANY,) * 6,
+        scratch_shapes=[
+            pltpu.VMEM((T, D), bf16),
+            pltpu.VMEM((3, D, HL), bf16),
+            pltpu.VMEM((HL, D), bf16),
+            pltpu.VMEM((T, D), bf16),
+            pltpu.VMEM((T, 128), f32),
+            pltpu.VMEM((T, 128), f32),
+            pltpu.VMEM((3, T, HL), bf16),
+            pltpu.VMEM((T, 128), f32),
+            pltpu.VMEM((T, HL), bf16),
+            pltpu.VMEM((T, D), bf16),
+            pltpu.VMEM((T, D), f32),
+            pltpu.VMEM((S, T), bf16),
+            pltpu.VMEM((EXPERTS, T), f32),
+            pltpu.VMEM((EXPERTS, T), f32),
+            pltpu.VMEM((T, T), f32),
+            pltpu.VMEM((T, HL), bf16),
+            pltpu.VMEM((HL, D), bf16),
+            pltpu.VMEM((S, D), bf16),
+            pltpu.VMEM((S, D), bf16),
+            pltpu.VMEM((S, D), bf16),
+            pltpu.VMEM((S, half), bf16),
+            pltpu.VMEM((S, half), bf16),
+            pltpu.VMEM((S, half), bf16),
+            pltpu.VMEM((T, D), bf16),
+            pltpu.VMEM((T, half), bf16),
+            pltpu.VMEM((T, D), bf16),
+            pltpu.VMEM((T, D), bf16),
+            pltpu.VMEM((S, half), bf16),
+            pltpu.VMEM((S, half), bf16),
+            pltpu.VMEM((T, half), bf16),
+            pltpu.VMEM((8, D), f32),
+            pltpu.VMEM((8, D), f32),
+            *[
+                pltpu.VMEM((*dims, share, width), bf16)
+                for width in (W1, W2)
+                for dims in ((zs, 2), (zs,), (zs - 1,))
+            ],
+            dma((12,)), dma((12,)), *[dma((G,))] * 8, dma((4,)), dma((4,)), dma((G,)), dma((G,)),
+            dma((4,)), dma((4,)), dma((G,)), dma((G,)), dma((12,)), dma((12,)), dma((4,)), dma((4,)),
+            dma((4, zs - 1)), dma((4, zs - 1)), dma((8,)), dma((4,)),
+        ],
+        compiler_params=pltpu.CompilerParams(
+            collective_id=0, has_side_effects=True, vmem_limit_bytes=VMEM_BYTES
+        ),
+        name="layer",
+    )(
+        norm_attn, norm_ffn, cont_lengths, routes.T, route_gates.T, tokens, w_qkv, w_attn_out, cotangent,
+        shared_in, shared_out, expert_in, expert_out,
+    )
+    steps = 4
+
+    def rows_of(*dims):
+        return pl.BlockSpec(dims, lambda i: (0,) * (len(dims) - 2) + (i, 0))
+
+    def whole(*dims):
+        return pl.BlockSpec(dims, lambda i: (0,) * len(dims))
+
+    results = ((3, share, HL), (HL, share), (1, share), (1, share), (2, share, F), (F, share))
+    out, gtok, gqkv, gao, gna, gnf, gsi, gso, gein, geout = pl.pallas_call(
+        functools.partial(finish_kernel, HL, F),
+        grid=(steps,),
+        out_shape=(
+            shape((T, D), bf16), shape((T, D), bf16), *[shape(r, f32) for r in results],
+            shape((2, D, F), f32), shape((F, D), f32),
+        ),
+        in_specs=[
+            rows_of(T // steps, D), rows_of(T // steps, D), whole(share, W1), whole(share, W2),
+            rows_of(2, D // steps, F), rows_of(F // steps, D),
+        ],
+        out_specs=(
+            rows_of(T // steps, D), rows_of(T // steps, D), *[whole(*r) for r in results],
+            rows_of(2, D // steps, F), rows_of(F // steps, D),
+        ),
+        compiler_params=pltpu.CompilerParams(vmem_limit_bytes=VMEM_BYTES),
+        name="finish",
+    )(out, gtok, gw1, gw2, gein.reshape(2, D, F), geout)
+    return (out, gtok, gqkv, gao, gna[0], gnf[0], gsi, gso, gein, geout)
+
+
 def solution(mesh):
     placed = (
         P("dp", None),
@@ -296,7 +1190,7 @@
         P("dp", None),
     )
     return jax.shard_map(
-        local,
+        fused if mesh.shape["dp"] == EXPERTS else local,
         mesh=mesh,
         in_specs=placed,
         out_specs=(

time: 863 us -> 246 us (0.29)
  waiting for transfers between devices: 429 us -> 0 us
  Pallas kernels: 0 us -> 238 us
  local copies, waits for them, and re-layouts: 149 us -> 3.57 us
  matrix products: 113 us -> 0 us
  other arithmetic: 65.4 us -> 0 us
  starting transfers between devices: 43.8 us -> 0 us
  blocking collectives: 36.2 us -> 0 us
  between operations: 16 us -> 0.66 us
    pallas_call x0 -> x2, Pallas kernels: none -> 238 us  [the longest x1 229 us: fused(): pl.pallas_call(functools.partial(layer_kernel, G), out_shape=(shape((T, D...]
    unnamed x7 -> x0, waiting for transfers between devices: 162 us -> none
    reduce_scatter x2 -> x0, waiting for transfers between devices: 129 us -> none  [the longest x1 67.4 us: local(): lax.psum_scatter(g_shared_out, 'dp', scatter_dimension=1, tiled=True)]
    dot_general x24 -> x0, matrix products: 113 us -> none  [the longest x1 10.3 us: local(): jnp.einsum('rf,rd->fd', back_act, d_expert_rows, preferred_element_type=j...]
    all_to_all x4 -> x0, waiting for transfers between devices: 83 us -> none  [the longest x1 24.8 us: local(): lax.all_to_all(d_expert_in.reshape(groups, CAP, model_width), 'dp', split...]
    psum x3 -> x0, waiting for transfers between devices: 55.5 us -> none  [the longest x1 29.2 us: local(): lax.psum(d_normed.astype(jnp.bfloat16), 'tensor').astype(jnp.float32)]
    all_to_all x4 -> x0, starting transfers between devices: 42.9 us -> none  [the longest x1 12.5 us: local(): lax.all_to_all(send_grad, 'dp', split_axis=0, concat_axis=0, tiled=True)]
    gather x5 -> x0, local copies, waits for them, and re-layouts: 36.4 us -> none  [the longest x3 20.3 us: spread_rows(): jnp.take(padded, indices, axis=0).reshape(EXPERTS, 1, CAP, model_width)]
  transfers between devices with their start and end apart: 10 -> 0, of which waited for: 9 -> 0; matrix products, arithmetic and copies ran while one was open for 23% -> 0% of each run, Pallas kernels for 0% -> 0%
where the time goes in v3:
time: 246 us; the launch traced here: 242 us
  Pallas kernels  238 us (97%)
  local copies, waits for them, and re-layouts  3.57 us (1%)
    pallas_call x1, Pallas kernels, fused(): pl.pallas_call(functools.partial(layer_kernel, G), out_shape=(shape((T, D...  229 us
    pallas_call x1, Pallas kernels, fused(): pl.pallas_call(functools.partial(finish_kernel, HL, F), grid=(steps,), ou...  8.35 us

profile of v3, /device:TPU:0, one launch (start us, length us, event | category | flops | bytes accessed | tf_op | source)
XLA Modules:
  0.0 242.0 jit_solution(7423661309852951817)
XLA Ops:
  0.6 229.5 %layer.1 = (bf16[576,768]{1,0:T(8,128)(2,1)}, bf16[576,768]{1,0:T(8,128)(2,1)}, f32[48,3072]{1,0:T(8,128)}, f32[48,1664]{1,0:T(8,128)}, bf16[2,4,2,2,48,1024]{5,...) custom-call(f32[768]{0:T(1024)} %na.1, f32[768]{0:T(1024)} %nf.1, s32[1,2]{1,0:T(1,128)} %lens.1, s32[2,576]{1,0:T(2,128)} %bitcast.6, ...), custom_call_target="tpu_custom_call" | custom-call | tf_op jit(solution)/shard_map/layer/pallas_call | solution.py:1088
  230.1 8.4 %finish.1 = (bf16[576,768]{1,0:T(8,128)(2,1)}, bf16[576,768]{1,0:T(8,128)(2,1)}, f32[3,48,384]{2,1,0:T(8,128)}, f32[384,48]{1,0:T(8,128)}, f32[1,48]{1,0:T(1,128...) custom-call(bf16[576,768]{1,0:T(8,128)(2,1)} %get-tuple-element.26.h, ...), custom_call_target="tpu_custom_call" | custom-call | tf_op jit(solution)/shard_map/finish/pallas_call | solution.py:1155
  238.5 1.7 copy.23
  240.2 1.9 copy.24

commit v4 on v3

--- a/solution.py
+++ b/solution.py
@@ -287,7 +287,6 @@
 VMEM_BYTES = 64000 * 1024
 FOLD = 96
 SPLIT = 7
-EARLY = 2
 MESH = pl.DeviceIdType.MESH
 VM = pl.BlockSpec(memory_space=pltpu.VMEM)
 ANY = pl.BlockSpec(memory_space=pl.ANY)
@@ -466,6 +465,10 @@
             drows.at[row_at(k), mine], drows.at[row_at(k), mine], s_cf.at[k], r_cf.at[k], partner
         )
 
+    def cot_hand_on(k):
+        cot_half(k).wait_recv()
+        cot_pass(k).start()
+
     def cot_step(k, carry):
         e = lax.rem(me + k, G)
         at = row_at(k)
@@ -496,6 +499,7 @@
 
     fill_angles(cos, sin, lens, T)
     fill_bias(bias, lens, T)
+    cot_hand_on(1)
     loads[1].wait()
 
     def norm_step(i, carry):
@@ -506,6 +510,7 @@
         return carry
 
     lax.fori_loop(0, T // FOLD, norm_step, 0)
+    cot_hand_on(2)
     loads[2].wait()
     loads[3].wait()
 
@@ -520,6 +525,7 @@
     project(0, True)
     project(1, True)
     project(2, False)
+    cot_hand_on(3)
     lane = lax.broadcasted_iota(jnp.int32, (T, 128), 1)
 
     def att_copy(j):
@@ -552,9 +558,8 @@
     wo_pass.wait()
     for j in range(HL // 128):
         att_copy(j).wait()
-    for k in range(1, SPLIT + 1):
-        cot_half(k).wait_recv()
-        cot_pass(k).start()
+    for k in range(4, SPLIT + 1):
+        cot_hand_on(k)
     resid[...] = tok[...].astype(f32) + own_out + dot(att[...], wo2[...])
 
     def row_copy(k):
@@ -613,11 +618,15 @@
         if c == 0:
             ro[0:C, :] = total[0:C, :]
 
+    dnar, ob = rows.at[0:T], rows.at[T : 2 * T]
+    out_copy = send(ob.at[:, mine], ob.at[:, mine], s_x.at[8], r_x.at[8], partner)
+    gna_copy = send(gna, gnar, s_x.at[9], r_x.at[9], partner)
+    dnb_copy = send(dnb.at[:, mine], dnb.at[:, mine], s_x.at[5], r_x.at[5], partner)
     dnsh_copy = send(dnsh.at[:, theirs], dnsh_r, s_x.at[4], r_x.at[4], partner)
     shp_copy = send(shp.at[:, theirs], shpr, s_x.at[7], r_x.at[7], partner)
 
     def columns(p):
-        return slice(p * F, (p + 1) * F) if p < 3 else slice(0, W2)
+        return slice(p * F, (p + 1) * F) if p < 3 else (slice(0, HL), slice(HL, W2))[p - 3]
 
     def fold_bufs(p):
         return (a1, b1, d1) if p < 3 else (a2, b2, d2)
@@ -787,27 +796,29 @@
         dnsh_copy.start()
         weights[2].wait()
         weights[3].wait()
-        for k in range(4, 6):
-            hand_on(k)
         vsi[0, :, 0:T] = normed[...].T
         vsi[1, :, 0:T] = cot[...].T
-        expert_chunk(0)
-        for k in range(6, 8):
-            hand_on(k)
         shp[...] = dot(act[mid, :], vso[...]).astype(bf16)
         shared_grads(0)
+        for k in range(4, 8):
+            hand_on(k)
+        expert_chunk(0)
+        shared_grads(1)
+        for k in range(8, 10):
+            hand_on(k)
+        expert_chunk(1)
         return_chunk(0)
-        expert_chunk(1)
-        for k in range(8, 12):
+        for k in range(10, 12):
             hand_on(k)
-        shared_grads(1)
         shared_grads(2)
+        for k in range(12, 14):
+            hand_on(k)
+        expert_chunk(2)
         return_chunk(1)
-        expert_chunk(2)
-        for k in range(12, G):
+        for k in range(14, G):
             hand_on(k)
+        expert_chunk(3)
         return_chunk(2)
-        expert_chunk(3)
 
         def part_chunk(c):
             dx_copy(c).wait_send()
@@ -816,8 +827,8 @@
         for c in range(chunks - 1):
             part_chunk(c)
         return_chunk(3)
-        for c in range(EARLY):
-            part_copy(c).start()
+        part_copy(0).start()
+        part_copy(1).start()
         part_chunk(3)
         sides = [slice(0, S // 2), slice(S // 2, S)]
         for n in range(2):
@@ -841,9 +852,26 @@
             gein_copy(i).start()
             return carry
 
-        lax.fori_loop(0, 2 * tiles, gein_step, 0)
+        first = 2
+        lax.fori_loop(0, first, gein_step, 0)
+        for k in range(G):
+            row_pass(k).wait_send()
+
+        dnsh_copy.wait()
+        total = dnsh[:, mine].astype(f32) + dnsh_r[...].astype(f32)
+        for c in range(chunks):
+            for k in range(c * per, (c + 1) * per):
+                if k > 0:
+                    ret_copy(k).wait_recv()
+            total = total + dot_tn(plan[chunk_at(c), :], ret[chunk_at(c), :])
+        dnb[:, mine] = total.astype(bf16)
+        dnb_copy.start()
+        part_copy(2).start()
         for p in range(3):
             fold_on(p)
+        lax.fori_loop(first, 2 * tiles, gein_step, 0)
+        return_part(0)
+        return_part(1)
 
         def geout_copy(i):
             return pltpu.make_async_copy(
@@ -860,10 +888,6 @@
             return carry
 
         lax.fori_loop(0, tiles, geout_step, 0)
-        for k in range(G):
-            row_pass(k).wait_send()
-        for k in range(1, SPLIT + 1):
-            cot_pass(k).wait_send()
         gein_copy(2 * tiles - 2).wait()
         gein_copy(2 * tiles - 1).wait()
         geout_copy(tiles - 2).wait()
@@ -882,28 +906,12 @@
         pltpu.VMEM((2, tile, D), bf16),
     )
 
-    dnsh_copy.wait()
-    total = dnsh[:, mine].astype(f32) + dnsh_r[...].astype(f32)
-    for c in range(chunks):
-        for k in range(c * per, (c + 1) * per):
-            if k > 0:
-                ret_copy(k).wait_recv()
-        total = total + dot_tn(plan[chunk_at(c), :], ret[chunk_at(c), :])
-    dnb[:, mine] = total.astype(bf16)
-    dnb_copy = send(dnb.at[:, mine], dnb.at[:, mine], s_x.at[5], r_x.at[5], partner)
-    dnb_copy.start()
-
-    dnar, ob = drows.at[0:T], rows.at[0:T]
-    out_copy = send(ob.at[:, mine], ob.at[:, mine], s_x.at[8], r_x.at[8], partner)
-    gna_copy = send(gna, gnar, s_x.at[9], r_x.at[9], partner)
-
-    def attention_back(dres, dresb, da, dqkv, turned, pay, gated, dna, gtok, w1, w2):
+    def attention_back(dres, dresb, da, dqkv, turned, turned2, pay, gated, dna, gtok, w1, w2):
         dna_copy = send(dna, dnar, s_x.at[10], r_x.at[10], partner)
-        for c in range(min(2, EARLY)):
-            return_part(c)
+        turned[...] = normed_a[...].T
         dnb_copy.wait()
-        for c in range(EARLY, chunks):
-            part_copy(c).start()
+        part_copy(3).start()
+        shp_copy.start()
 
         def dres_step(i, carry):
             at = pl.ds(pl.multiple_of(i * FOLD, FOLD), FOLD)
@@ -920,6 +928,29 @@
 
         gnf = lax.fori_loop(0, T // FOLD, dres_step, jnp.zeros((1, D), f32))
         da[...] = dot_nt(dresb[...], wo[...]).astype(bf16)
+        turned2[...] = dresb[...].T
+        pay[:, :, :, :, 0:HL] = dot(turned2[...], att_own[...]).astype(bf16).reshape(zs, 2, 2, share, HL)
+
+        def pay_core(p):
+            return send(
+                pay.at[:, :, 1 - core, :, columns(p)], a2.at[:, :, :, columns(p)], s_x.at[8 + p], r_x.at[8 + p],
+                sibling,
+            )
+
+        def pay_on(p):
+            pay_core(p).wait()
+
+            def body(n, carry):
+                u, v = n // 2, lax.rem(n, 2)
+                a2[u, v, :, columns(p)] = (
+                    a2[u, v, :, columns(p)].astype(f32) + pay[u, v, core, :, columns(p)].astype(f32)
+                ).astype(bf16)
+                return carry
+
+            lax.fori_loop(0, 2 * zs, body, 0)
+            fold_y(p).start()
+
+        pay_core(3).start()
 
         def attend_back(j, carry):
             at = pl.ds(pl.multiple_of(j * 128, 128), 128)
@@ -944,12 +975,11 @@
             return carry
 
         lax.fori_loop(0, HL // 128, attend_back, 0)
+        pay_on(3)
 
         dna[...] = (
             dot_nt(dqkv[0], wqkv[0]) + dot_nt(dqkv[1], wqkv[1]) + dot_nt(dqkv[2], wqkv[2])
         ).astype(bf16)
-        dna_copy.start()
-        shp_copy.start()
 
         def gain_step(i, carry):
             at = pl.ds(pl.multiple_of(i * FOLD, FOLD), FOLD)
@@ -961,36 +991,23 @@
             lax.fori_loop(0, T // FOLD, gain_step, jnp.zeros((1, D), f32)), gna.shape
         )
         gna_copy.start()
-        for c in range(min(2, EARLY), chunks):
-            return_part(c)
-
-        turned[...] = normed_a[...].T
+        dna_copy.start()
+        return_part(2)
+        return_part(3)
         for s in range(3):
-            pay[:, :, :, :, s * HL : (s + 1) * HL] = (
+            pay[:, :, :, :, (s + 1) * HL : (s + 2) * HL] = (
                 dot(turned[...], dqkv[s]).astype(bf16).reshape(zs, 2, 2, share, HL)
             )
-        turned[...] = dresb[...].T
-        pay[:, :, :, :, 3 * HL : 4 * HL] = (
-            dot(turned[...], att_own[...]).astype(bf16).reshape(zs, 2, 2, share, HL)
-        )
         gna_copy.wait()
         row = lax.broadcasted_iota(jnp.int32, (128, D), 0)
         gains = jnp.where(row == 0, gnf, jnp.where(row == 1, gna[0:1, :] + gnar[0:1, :], 0.0))
         pay[:, :, :, :, 4 * HL :] = gains.T.astype(bf16).reshape(zs, 2, 2, share, 128)
-        core_copy = send(pay.at[:, :, 1 - core], a2, s_x.at[11], r_x.at[11], sibling)
-        core_copy.start()
-        core_copy.wait()
-
-        def body(n, carry):
-            u, v = n // 2, lax.rem(n, 2)
-            a2[u, v] = (a2[u, v].astype(f32) + pay[u, v, core].astype(f32)).astype(bf16)
-            return carry
-
-        lax.fori_loop(0, 2 * zs, body, 0)
-        fold_y(3).start()
+        pay_core(4).start()
+        fold_on(3)
+        pay_on(4)
         for p in range(3):
             fold_end(p, w1)
-        fold_on(3)
+        fold_on(4)
 
         shp_copy.wait()
         mixed = shp[:, mine].astype(f32) + shpr[...].astype(f32)
@@ -1018,6 +1035,7 @@
 
         lax.fori_loop(0, T // FOLD, last_step, 0)
         fold_end(3, w2)
+        fold_end(4, w2)
         ends = [
             pltpu.make_async_copy(a, b, osem.at[i])
             for i, (a, b) in enumerate(((gtok, h_gtok), (w1, h_gw1), (w2, h_gw2), (ob, h_out)))
@@ -1036,6 +1054,7 @@
         pltpu.VMEM((T, HL), bf16),
         pltpu.VMEM((3, T, HL), bf16),
         pltpu.VMEM((D, T), bf16),
+        pltpu.VMEM((D, T), bf16),
         pltpu.VMEM((zs, 2, 2, share, W2), bf16),
         pltpu.VMEM((M, T), bf16),
         pltpu.VMEM((T, D), bf16),
@@ -1043,6 +1062,8 @@
         pltpu.VMEM((share, 3 * F), f32),
         pltpu.VMEM((share, W2), f32),
     )
+    for k in range(1, SPLIT + 1):
+        cot_pass(k).wait_send()
     for c in range(chunks):
         part_copy(c).wait_send()
     for k in range(1, G):
@@ -1061,14 +1082,14 @@
     @pl.when(pl.program_id(0) == 0)
     def _():
         for s in range(3):
-            gqkv[s] = h_gw2[:, s * HL : (s + 1) * HL]
-        gao[...] = h_gw2[:, 3 * HL : 4 * HL].T
+            gqkv[s] = h_gw2[:, (s + 1) * HL : (s + 2) * HL]
+        gao[...] = h_gw2[:, 0:HL]
         gains = h_gw2[:, 4 * HL :].T
         gnf[...] = gains[0:1, :]
         gna[...] = gains[1:2, :]
         for s in range(2):
             gsi[s] = h_gw1[:, s * F : (s + 1) * F]
-        gso[...] = h_gw1[:, 2 * F :].T
+        gso[...] = h_gw1[:, 2 * F :]
 
 
 def fused(
@@ -1131,9 +1152,9 @@
                 for width in (W1, W2)
                 for dims in ((zs, 2), (zs,), (zs - 1,))
             ],
-            dma((12,)), dma((12,)), *[dma((G,))] * 8, dma((4,)), dma((4,)), dma((G,)), dma((G,)),
-            dma((4,)), dma((4,)), dma((G,)), dma((G,)), dma((12,)), dma((12,)), dma((4,)), dma((4,)),
-            dma((4, zs - 1)), dma((4, zs - 1)), dma((8,)), dma((4,)),
+            dma((13,)), dma((13,)), *[dma((G,))] * 8, dma((4,)), dma((4,)), dma((G,)), dma((G,)),
+            dma((4,)), dma((4,)), dma((G,)), dma((G,)), dma((12,)), dma((12,)), dma((5,)), dma((5,)),
+            dma((5, zs - 1)), dma((5, zs - 1)), dma((8,)), dma((4,)),
         ],
         compiler_params=pltpu.CompilerParams(
             collective_id=0, has_side_effects=True, vmem_limit_bytes=VMEM_BYTES
@@ -1151,7 +1172,7 @@
     def whole(*dims):
         return pl.BlockSpec(dims, lambda i: (0,) * len(dims))
 
-    results = ((3, share, HL), (HL, share), (1, share), (1, share), (2, share, F), (F, share))
+    results = ((3, share, HL), (share, HL), (1, share), (1, share), (2, share, F), (share, F))
     out, gtok, gqkv, gao, gna, gnf, gsi, gso, gein, geout = pl.pallas_call(
         functools.partial(finish_kernel, HL, F),
         grid=(steps,),
@@ -1170,7 +1191,7 @@
         compiler_params=pltpu.CompilerParams(vmem_limit_bytes=VMEM_BYTES),
         name="finish",
     )(out, gtok, gw1, gw2, gein.reshape(2, D, F), geout)
-    return (out, gtok, gqkv, gao, gna[0], gnf[0], gsi, gso, gein, geout)
+    return (out, gtok, gqkv, gao.T, gna[0], gnf[0], gsi, gso.T, gein, geout)
 
 
 def solution(mesh):

time: 246 us -> 215 us (0.87); the launches traced: 242 us -> 214 us
  Pallas kernels: 238 us -> 214 us
  local copies, waits for them, and re-layouts: 3.57 us -> 0 us
    pallas_call x1, Pallas kernels: 229 us -> 205 us  [fused(): pl.pallas_call(functools.partial(layer_kernel, G), out_shape=(shape((T, D...]
    unnamed x2 -> x0, local copies, waits for them, and re-layouts: 3.57 us -> none
where the time goes in v4:
time: 215 us; the launch traced here: 214 us
  Pallas kernels  214 us (100%)
    pallas_call x1, Pallas kernels, fused(): pl.pallas_call(functools.partial(layer_kernel, G), out_shape=(shape((T, D...  205 us
    pallas_call x1, Pallas kernels, fused(): pl.pallas_call(functools.partial(finish_kernel, HL, F), grid=(steps,), ou...  8.23 us

profile of v4, /device:TPU:0, one launch (start us, length us, event | category | flops | bytes accessed | tf_op | source)
XLA Modules:
  0.0 214.4 jit_solution(12331869295344465289)
XLA Ops:
  0.6 205.3 %layer.1 = (bf16[576,768]{1,0:T(8,128)(2,1)}, bf16[576,768]{1,0:T(8,128)(2,1)}, f32[48,3072]{1,0:T(8,128)}, f32[48,1664]{1,0:T(8,128)}, bf16[2,4,2,2,48,1024]{5,...) custom-call(f32[768]{0:T(1024)} %na.1, f32[768]{0:T(1024)} %nf.1, s32[1,2]{1,0:T(1,128)} %lens.1, s32[2,576]{1,0:T(2,128)} %bitcast.8, ...), custom_call_target="tpu_custom_call" | custom-call | tf_op jit(solution)/shard_map/layer/pallas_call | solution.py:1109
  205.9 8.2 %finish.1 = (bf16[576,768]{1,0:T(8,128)(2,1)}, bf16[576,768]{1,0:T(8,128)(2,1)}, f32[3,48,384]{2,1,0:T(8,128)}, f32[48,384]{1,0:T(8,128)}, f32[1,48]{1,0:T(1,128...) custom-call(bf16[576,768]{1,0:T(8,128)(2,1)} %get-tuple-element.26.h, ...), custom_call_target="tpu_custom_call" | custom-call | tf_op jit(solution)/shard_map/finish/pallas_call | solution.py:1176

commit v5 on v4

--- a/solution.py
+++ b/solution.py
@@ -286,7 +286,6 @@
 
 VMEM_BYTES = 64000 * 1024
 FOLD = 96
-SPLIT = 7
 MESH = pl.DeviceIdType.MESH
 VM = pl.BlockSpec(memory_space=pltpu.VMEM)
 ANY = pl.BlockSpec(memory_space=pl.ANY)
@@ -397,7 +396,7 @@
     G, na, nf, lens, rT, gT, h_tok, h_wqkv, h_wo, h_cot, si, so, ei, eo,
     h_out, h_gtok, h_gw1, h_gw2, gein, geout,
     tok, wqkv, wo, cot, cos, sin, qkv, lse, att_own, normed_a, resid, plan, gate, slot, bias, att, wo2,
-    csend, drows, rows, rets, ret, dxr, dnsh, dnsh_r, dnb, shp, partr, ro, shpr, gna, gnar,
+    csend, drows, rows, near_send, rets, near_ret, ret, dxr, dnsh, dnsh_r, dnb, shp, partr, near_ro, ro, shpr, gna, gnar,
     a1, b1, d1, a2, b2, d2,
     s_x, r_x, s_c, r_c, s_cf, r_cf, s_r, r_r, s_f, r_f, s_dx, r_dx, s_ret, r_ret, s_p, r_p, s_po, r_po,
     s_k, r_k, s_y, r_y, s_z, r_z, lsem, osem,
@@ -438,6 +437,28 @@
     def chunk_at(c):
         return pl.ds(c * M, M)
 
+    near = G // 2
+
+    def peer(k):
+        to, weight = me, 1
+        while weight < G:
+            bit = lax.rem(k // weight, 2)
+            to = to + weight * bit * (1 - 2 * lax.rem(me // weight, 2))
+            weight = weight * 2
+        return to
+
+    def far_at(k):
+        return pl.ds(pl.multiple_of((k - per) * C, C), C)
+
+    def out_at(k):
+        return pl.ds(pl.multiple_of((k - near) * C, C), C)
+
+    def far_chunk(c):
+        return pl.ds((c - 1) * M, M)
+
+    def out_chunk(c):
+        return pl.ds((c - near // per) * M, M)
+
     names = lax.broadcasted_iota(jnp.int32, (EXPERTS, T), 0)
     picks0, picks1 = rT[0:1, :] == names, rT[1:2, :] == names
     member = jnp.where(picks0 | picks1, 1.0, 0.0)
@@ -450,14 +471,11 @@
     gate[...] = jnp.where(picks0, gT[0:1, :], 0.0) + jnp.where(picks1, gT[1:2, :], 0.0)
 
     def cot_copy(k):
-        return send(
-            csend.at[row_at(k)], drows.at[row_at(k)], s_c.at[k], r_c.at[k], (lax.rem(me + k, G), t)
-        )
+        return send(csend.at[row_at(k)], drows.at[row_at(k)], s_c.at[k], r_c.at[k], (peer(k), t))
 
     def cot_half(k):
         return send(
-            csend.at[row_at(k), mine], drows.at[row_at(k), mine], s_c.at[k], r_c.at[k],
-            (lax.rem(me + k, G), t),
+            csend.at[row_at(k), mine], drows.at[row_at(k), mine], s_c.at[k], r_c.at[k], (peer(k), t)
         )
 
     def cot_pass(k):
@@ -469,8 +487,9 @@
         cot_half(k).wait_recv()
         cot_pass(k).start()
 
-    def cot_step(k, carry):
-        e = lax.rem(me + k, G)
+    def cot_step(i, carry):
+        k = G - 1 - i
+        e = peer(k)
         at = row_at(k)
         place = lax.broadcasted_iota(jnp.int32, (C, T), 0).astype(f32)
         hit = slot[pl.ds(e, 1), :] == place
@@ -480,13 +499,13 @@
         grad = (dot(picked, cot[...]) * weight).astype(bf16)
         csend[at, :] = grad
 
-        @pl.when(k > SPLIT)
+        @pl.when(k >= near)
+        def _():
+            cot_half(k).start()
+
+        @pl.when((k > 0) & (k < near))
         def _():
             cot_copy(k).start()
-
-        @pl.when((k > 0) & (k <= SPLIT))
-        def _():
-            cot_half(k).start()
 
         @pl.when(k == 0)
         def _():
@@ -499,7 +518,7 @@
 
     fill_angles(cos, sin, lens, T)
     fill_bias(bias, lens, T)
-    cot_hand_on(1)
+    cot_hand_on(G - 1)
     loads[1].wait()
 
     def norm_step(i, carry):
@@ -510,7 +529,7 @@
         return carry
 
     lax.fori_loop(0, T // FOLD, norm_step, 0)
-    cot_hand_on(2)
+    cot_hand_on(G - 2)
     loads[2].wait()
     loads[3].wait()
 
@@ -525,7 +544,7 @@
     project(0, True)
     project(1, True)
     project(2, False)
-    cot_hand_on(3)
+    cot_hand_on(G - 3)
     lane = lax.broadcasted_iota(jnp.int32, (T, 128), 1)
 
     def att_copy(j):
@@ -558,14 +577,15 @@
     wo_pass.wait()
     for j in range(HL // 128):
         att_copy(j).wait()
-    for k in range(4, SPLIT + 1):
+    for k in range(G - 4, near - 1, -1):
         cot_hand_on(k)
     resid[...] = tok[...].astype(f32) + own_out + dot(att[...], wo2[...])
 
     def row_copy(k):
-        return send(
-            rets.at[row_at(k)], rows.at[row_at(k), mine], s_r.at[k], r_r.at[k], (lax.rem(me + k, G), t)
-        )
+        return send(near_send.at[row_at(k)], rows.at[row_at(k)], s_r.at[k], r_r.at[k], (peer(k), t))
+
+    def row_half(k):
+        return send(rets.at[far_at(k)], rows.at[row_at(k), mine], s_r.at[k], r_r.at[k], (peer(k), t))
 
     def row_pass(k):
         return send(
@@ -573,50 +593,45 @@
         )
 
     def hand_on(k):
-        row_copy(k).wait_recv()
+        row_half(k).wait_recv()
         row_pass(k).start()
 
     def dx_copy(c):
-        return send(csend.at[chunk_at(c), theirs], dxr.at[chunk_at(c)], s_dx.at[c], r_dx.at[c], partner)
+        return send(csend.at[chunk_at(c), theirs], dxr.at[far_chunk(c)], s_dx.at[c], r_dx.at[c], partner)
 
     def ret_copy(k):
-        return send(
-            rets.at[row_at(k)], ret.at[row_at(k)], s_ret.at[k], r_ret.at[k], (lax.rem(me - k + G, G), t)
-        )
+        return send(csend.at[row_at(k)], near_ret.at[row_at(k)], s_ret.at[k], r_ret.at[k], (peer(k), t))
+
+    def ret_half(k):
+        return send(rets.at[far_at(k)], ret.at[far_at(k)], s_ret.at[k], r_ret.at[k], (peer(k), t))
 
     def return_chunk(c):
         dx_copy(c).wait_recv()
-        total = (csend[chunk_at(c), mine].astype(f32) + dxr[chunk_at(c), :].astype(f32)).astype(bf16)
+        total = (csend[chunk_at(c), mine].astype(f32) + dxr[far_chunk(c), :].astype(f32)).astype(bf16)
         for k in range(c * per, (c + 1) * per):
-            if k > 0:
-                row_copy(k).wait_send()
-        rets[chunk_at(c), :] = total
+            if k >= near:
+                row_half(k).wait_send()
+        rets[far_chunk(c), :] = total
         for k in range(c * per, (c + 1) * per):
-            if k > 0:
-                ret_copy(k).start()
-        if c == 0:
-            ret[0:C, :] = total[0:C, :]
+            ret_half(k).start()
 
     def part_copy(c):
-        return send(csend.at[chunk_at(c), theirs], partr.at[chunk_at(c)], s_p.at[c], r_p.at[c], partner)
+        return send(csend.at[chunk_at(c), theirs], partr.at[out_chunk(c)], s_p.at[c], r_p.at[c], partner)
 
     def po_copy(k):
-        return send(
-            rets.at[row_at(k)], ro.at[row_at(k)], s_po.at[k], r_po.at[k], (lax.rem(me - k + G, G), t)
-        )
+        return send(csend.at[row_at(k)], near_ro.at[row_at(k)], s_po.at[k], r_po.at[k], (peer(k), t))
+
+    def po_half(k):
+        return send(rets.at[far_at(k)], ro.at[out_at(k)], s_po.at[k], r_po.at[k], (peer(k), t))
 
     def return_part(c):
         part_copy(c).wait_recv()
-        total = (csend[chunk_at(c), mine].astype(f32) + partr[chunk_at(c), :].astype(f32)).astype(bf16)
+        total = (csend[chunk_at(c), mine].astype(f32) + partr[out_chunk(c), :].astype(f32)).astype(bf16)
         for k in range(c * per, (c + 1) * per):
-            if k > 0:
-                ret_copy(k).wait_send()
-        rets[chunk_at(c), :] = total
+            ret_half(k).wait_send()
+        rets[far_chunk(c), :] = total
         for k in range(c * per, (c + 1) * per):
-            if k > 0:
-                po_copy(k).start()
-        if c == 0:
-            ro[0:C, :] = total[0:C, :]
+            po_half(k).start()
 
     dnar, ob = rows.at[0:T], rows.at[T : 2 * T]
     out_copy = send(ob.at[:, mine], ob.at[:, mine], s_x.at[8], r_x.at[8], partner)
@@ -684,24 +699,30 @@
 
         lax.fori_loop(0, T // FOLD, norm2_step, 0)
 
-        def row_step(k, carry):
-            values = dot(plan[row_at(k), :], normed[:, mine]).astype(bf16)
-            rets[row_at(k), :] = values
+        def near_step(k, carry):
+            values = dot(plan[row_at(k), :], normed[...]).astype(bf16)
 
             @pl.when(k > 0)
             def _():
+                near_send[row_at(k), :] = values
                 row_copy(k).start()
 
             @pl.when(k == 0)
             def _():
-                rows[row_at(k), mine] = values
-                row_pass(k).start()
+                rows[row_at(k), :] = values
 
             return carry
 
-        lax.fori_loop(0, G, row_step, 0)
-
-        mid = slice(S - T, S)
+        def far_step(i, carry):
+            k = G - 1 - i
+            rets[far_at(k), :] = dot(plan[row_at(k), :], normed[:, mine]).astype(bf16)
+            row_half(k).start()
+            return carry
+
+        lax.fori_loop(0, G - near, far_step, 0)
+        lax.fori_loop(0, near, near_step, 0)
+
+        mid = slice(M, M + T)
 
         def shared_step(u, carry):
             at = pl.ds(pl.multiple_of(u * tile, tile), tile)
@@ -758,11 +779,12 @@
 
         def expert_chunk(c):
             for k in range(c * per, (c + 1) * per):
-                row_pass(k).wait_recv()
-                if k > SPLIT:
+                if k >= near:
+                    row_pass(k).wait_recv()
+                    cot_pass(k).wait_recv()
+                elif k > 0:
+                    row_copy(k).wait_recv()
                     cot_copy(k).wait_recv()
-                elif k > 0:
-                    cot_pass(k).wait_recv()
             block = chunk_at(c)
 
             def unit_step(u, carry):
@@ -780,56 +802,67 @@
             lax.fori_loop(0, tiles, unit_step, 0)
             dx = dot_nt(dgu[0, block, :], vei[0]) + dot_nt(dgu[1, block, :], vei[1])
             for k in range(c * per, (c + 1) * per):
-                if k > SPLIT:
+                if k >= near:
+                    cot_half(k).wait_send()
+                elif k > 0:
                     cot_copy(k).wait_send()
-                elif k > 0:
-                    cot_half(k).wait_send()
             csend[block, :] = dx.astype(bf16)
-            dx_copy(c).start()
+            if c > 0:
+                dx_copy(c).start()
+                return
+            for k in range(c * per, (c + 1) * per):
+                if k > 0:
+                    ret_copy(k).start()
+                else:
+                    near_ret[0:C, :] = csend[0:C, :]
 
         weights[0].wait()
         weights[1].wait()
         lax.fori_loop(0, tiles, shared_step, 0)
-        for k in range(1, 4):
-            hand_on(k)
         dnsh[...] = (dot_nt(dgu[0, mid, :], vsi[0]) + dot_nt(dgu[1, mid, :], vsi[1])).astype(bf16)
-        dnsh_copy.start()
         weights[2].wait()
         weights[3].wait()
         vsi[0, :, 0:T] = normed[...].T
         vsi[1, :, 0:T] = cot[...].T
         shp[...] = dot(act[mid, :], vso[...]).astype(bf16)
+        expert_chunk(0)
+        for k in range(G - 1, G - 5, -1):
+            hand_on(k)
         shared_grads(0)
-        for k in range(4, 8):
+        expert_chunk(3)
+        for k in range(G - 5, G - 7, -1):
             hand_on(k)
-        expert_chunk(0)
         shared_grads(1)
-        for k in range(8, 10):
-            hand_on(k)
-        expert_chunk(1)
-        return_chunk(0)
-        for k in range(10, 12):
+        for k in range(G - 7, near - 1, -1):
             hand_on(k)
         shared_grads(2)
-        for k in range(12, 14):
-            hand_on(k)
+        return_chunk(3)
+
         expert_chunk(2)
+        expert_chunk(1)
+        for k in range(1, per):
+            ret_copy(k).wait_recv()
+        dnsh[...] = (dnsh[...].astype(f32) + dot_tn(plan[0:M, :], near_ret[...])).astype(bf16)
+        dnsh_copy.start()
+        return_chunk(2)
+
+        def part_chunk(c):
+            if c > 0:
+                dx_copy(c).wait_send()
+            else:
+                for k in range(1, per):
+                    ret_copy(k).wait_send()
+            csend[chunk_at(c), :] = dot(act[chunk_at(c), :], veo[...]).astype(bf16)
+
+        part_chunk(0)
+        near_ro[0:C, :] = csend[0:C, :]
+        part_chunk(3)
         return_chunk(1)
-        for k in range(14, G):
-            hand_on(k)
-        expert_chunk(3)
-        return_chunk(2)
-
-        def part_chunk(c):
-            dx_copy(c).wait_send()
-            csend[chunk_at(c), :] = dot(act[chunk_at(c), :], veo[...]).astype(bf16)
-
-        for c in range(chunks - 1):
-            part_chunk(c)
-        return_chunk(3)
-        part_copy(0).start()
-        part_copy(1).start()
-        part_chunk(3)
+        part_copy(3).start()
+        part_chunk(2)
+        part_chunk(1)
+        for k in range(1, near):
+            po_copy(k).start()
         sides = [slice(0, S // 2), slice(S // 2, S)]
         for n in range(2):
             vsi[n, :, 0 : S // 2] = rows[sides[n], :].T
@@ -854,24 +887,21 @@
 
         first = 2
         lax.fori_loop(0, first, gein_step, 0)
-        for k in range(G):
+        for k in range(near, G):
             row_pass(k).wait_send()
 
         dnsh_copy.wait()
         total = dnsh[:, mine].astype(f32) + dnsh_r[...].astype(f32)
-        for c in range(chunks):
-            for k in range(c * per, (c + 1) * per):
-                if k > 0:
-                    ret_copy(k).wait_recv()
-            total = total + dot_tn(plan[chunk_at(c), :], ret[chunk_at(c), :])
+        for k in range(per, G):
+            ret_half(k).wait_recv()
+        total = total + dot_tn(plan[M:S, :], ret[...])
         dnb[:, mine] = total.astype(bf16)
         dnb_copy.start()
         part_copy(2).start()
         for p in range(3):
             fold_on(p)
         lax.fori_loop(first, 2 * tiles, gein_step, 0)
-        return_part(0)
-        return_part(1)
+        return_part(3)
 
         def geout_copy(i):
             return pltpu.make_async_copy(
@@ -910,8 +940,13 @@
         dna_copy = send(dna, dnar, s_x.at[10], r_x.at[10], partner)
         turned[...] = normed_a[...].T
         dnb_copy.wait()
-        part_copy(3).start()
-        shp_copy.start()
+
+        def gated_rows(c):
+            for k in range(c * per, (c + 1) * per):
+                gated[(k - c * per) * C : (k - c * per + 1) * C, :] = (
+                    plan[row_at(k), :].astype(f32) * gate[pl.ds(peer(k), 1), :]
+                ).astype(bf16)
+            return gated[...]
 
         def dres_step(i, carry):
             at = pl.ds(pl.multiple_of(i * FOLD, FOLD), FOLD)
@@ -993,7 +1028,13 @@
         gna_copy.start()
         dna_copy.start()
         return_part(2)
-        return_part(3)
+        mixed = shp[...].astype(f32)
+        for c in range(near // per):
+            for k in range(max(1, c * per), (c + 1) * per):
+                po_copy(k).wait_recv()
+            mixed = mixed + dot_tn(gated_rows(c), near_ro[chunk_at(c), :])
+        shp[...] = mixed.astype(bf16)
+        shp_copy.start()
         for s in range(3):
             pay[:, :, :, :, (s + 1) * HL : (s + 2) * HL] = (
                 dot(turned[...], dqkv[s]).astype(bf16).reshape(zs, 2, 2, share, HL)
@@ -1011,15 +1052,10 @@
 
         shp_copy.wait()
         mixed = shp[:, mine].astype(f32) + shpr[...].astype(f32)
-        for c in range(chunks):
+        for c in range(near // per, chunks):
             for k in range(c * per, (c + 1) * per):
-                if k > 0:
-                    po_copy(k).wait_recv()
-                weights = gate[pl.ds(lax.rem(me + k, G), 1), :]
-                gated[(k - c * per) * C : (k - c * per + 1) * C, :] = (
-                    plan[row_at(k), :].astype(f32) * weights
-                ).astype(bf16)
-            mixed = mixed + dot_tn(gated[...], ro[chunk_at(c), :])
+                po_half(k).wait_recv()
+            mixed = mixed + dot_tn(gated_rows(c), ro[out_chunk(c), :])
         ob[:, mine] = (resid[:, mine] + mixed).astype(bf16)
         out_copy.start()
         dna_copy.wait()
@@ -1062,12 +1098,16 @@
         pltpu.VMEM((share, 3 * F), f32),
         pltpu.VMEM((share, W2), f32),
     )
-    for k in range(1, SPLIT + 1):
+    for k in range(near, G):
         cot_pass(k).wait_send()
-    for c in range(chunks):
+        po_half(k).wait_send()
+    for k in range(1, near):
+        row_copy(k).wait_send()
+        po_copy(k).wait_send()
+    for k in range(per, near):
+        ret_half(k).wait_send()
+    for c in range(near // per, chunks):
         part_copy(c).wait_send()
-    for k in range(1, G):
-        po_copy(k).wait_send()
 
 
 def finish_kernel(
@@ -1135,15 +1175,18 @@
             pltpu.VMEM((S, D), bf16),
             pltpu.VMEM((S, D), bf16),
             pltpu.VMEM((S, D), bf16),
-            pltpu.VMEM((S, half), bf16),
-            pltpu.VMEM((S, half), bf16),
-            pltpu.VMEM((S, half), bf16),
+            pltpu.VMEM((S // 2, D), bf16),
+            pltpu.VMEM((S - 4 * C, half), bf16),
+            pltpu.VMEM((4 * C, D), bf16),
+            pltpu.VMEM((S - 4 * C, half), bf16),
+            pltpu.VMEM((S - 4 * C, half), bf16),
             pltpu.VMEM((T, D), bf16),
             pltpu.VMEM((T, half), bf16),
             pltpu.VMEM((T, D), bf16),
             pltpu.VMEM((T, D), bf16),
-            pltpu.VMEM((S, half), bf16),
-            pltpu.VMEM((S, half), bf16),
+            pltpu.VMEM((S // 2, half), bf16),
+            pltpu.VMEM((S // 2, D), bf16),
+            pltpu.VMEM((S // 2, half), bf16),
             pltpu.VMEM((T, half), bf16),
             pltpu.VMEM((8, D), f32),
             pltpu.VMEM((8, D), f32),

time: 215 us -> 208 us (0.967)
  Pallas kernels: 214 us -> 206 us
    pallas_call x1, Pallas kernels: 205 us -> 198 us  [fused(): pl.pallas_call(functools.partial(layer_kernel, G), out_shape=(shape((T, D...]
where the time goes in v5:
time: 208 us; the launch traced here: 207 us
  Pallas kernels  206 us (99%)
    pallas_call x1, Pallas kernels, fused(): pl.pallas_call(functools.partial(layer_kernel, G), out_shape=(shape((T, D...  198 us
    pallas_call x1, Pallas kernels, fused(): pl.pallas_call(functools.partial(finish_kernel, HL, F), grid=(steps,), ou...  8.23 us

profile of v5, /device:TPU:0, one launch (start us, length us, event | category | flops | bytes accessed | tf_op | source)
XLA Modules:
  0.0 207.1 jit_solution(13994343212139795838)
XLA Ops:
  0.6 198.1 %layer.1 = (bf16[576,768]{1,0:T(8,128)(2,1)}, bf16[576,768]{1,0:T(8,128)(2,1)}, f32[48,3072]{1,0:T(8,128)}, f32[48,1664]{1,0:T(8,128)}, bf16[2,4,2,2,48,1024]{5,...) custom-call(f32[768]{0:T(1024)} %na.1, f32[768]{0:T(1024)} %nf.1, s32[1,2]{1,0:T(1,128)} %lens.1, s32[2,576]{1,0:T(2,128)} %bitcast.8, ...), custom_call_target="tpu_custom_call" | custom-call | tf_op jit(solution)/shard_map/layer/pallas_call | solution.py:1149
  198.7 8.2 %finish.1 = (bf16[576,768]{1,0:T(8,128)(2,1)}, bf16[576,768]{1,0:T(8,128)(2,1)}, f32[3,48,384]{2,1,0:T(8,128)}, f32[48,384]{1,0:T(8,128)}, f32[1,48]{1,0:T(1,128...) custom-call(bf16[576,768]{1,0:T(8,128)(2,1)} %get-tuple-element.26.h, ...), custom_call_target="tpu_custom_call" | custom-call | tf_op jit(solution)/shard_map/finish/pallas_call | solution.py:1219

commit v6 on v5

--- a/solution.py
+++ b/solution.py
@@ -286,6 +286,8 @@
 
 VMEM_BYTES = 64000 * 1024
 FOLD = 96
+NEAR = 8
+WHOLE = 4
 MESH = pl.DeviceIdType.MESH
 VM = pl.BlockSpec(memory_space=pltpu.VMEM)
 ANY = pl.BlockSpec(memory_space=pl.ANY)
@@ -437,7 +439,8 @@
     def chunk_at(c):
         return pl.ds(c * M, M)
 
-    near = G // 2
+    near = NEAR
+    whole = WHOLE
 
     def peer(k):
         to, weight = me, 1
@@ -451,13 +454,13 @@
         return pl.ds(pl.multiple_of((k - per) * C, C), C)
 
     def out_at(k):
-        return pl.ds(pl.multiple_of((k - near) * C, C), C)
+        return pl.ds(pl.multiple_of((k - whole) * C, C), C)
 
     def far_chunk(c):
         return pl.ds((c - 1) * M, M)
 
     def out_chunk(c):
-        return pl.ds((c - near // per) * M, M)
+        return pl.ds((c - whole // per) * M, M)
 
     names = lax.broadcasted_iota(jnp.int32, (EXPERTS, T), 0)
     picks0, picks1 = rT[0:1, :] == names, rT[1:2, :] == names
@@ -518,7 +521,6 @@
 
     fill_angles(cos, sin, lens, T)
     fill_bias(bias, lens, T)
-    cot_hand_on(G - 1)
     loads[1].wait()
 
     def norm_step(i, carry):
@@ -529,7 +531,6 @@
         return carry
 
     lax.fori_loop(0, T // FOLD, norm_step, 0)
-    cot_hand_on(G - 2)
     loads[2].wait()
     loads[3].wait()
 
@@ -544,7 +545,6 @@
     project(0, True)
     project(1, True)
     project(2, False)
-    cot_hand_on(G - 3)
     lane = lax.broadcasted_iota(jnp.int32, (T, 128), 1)
 
     def att_copy(j):
@@ -577,8 +577,6 @@
     wo_pass.wait()
     for j in range(HL // 128):
         att_copy(j).wait()
-    for k in range(G - 4, near - 1, -1):
-        cot_hand_on(k)
     resid[...] = tok[...].astype(f32) + own_out + dot(att[...], wo2[...])
 
     def row_copy(k):
@@ -721,6 +719,8 @@
 
         lax.fori_loop(0, G - near, far_step, 0)
         lax.fori_loop(0, near, near_step, 0)
+        for k in range(G - 1, near - 1, -1):
+            cot_hand_on(k)
 
         mid = slice(M, M + T)
 
@@ -861,7 +861,7 @@
         part_copy(3).start()
         part_chunk(2)
         part_chunk(1)
-        for k in range(1, near):
+        for k in range(1, whole):
             po_copy(k).start()
         sides = [slice(0, S // 2), slice(S // 2, S)]
         for n in range(2):
@@ -898,6 +898,8 @@
         dnb[:, mine] = total.astype(bf16)
         dnb_copy.start()
         part_copy(2).start()
+        if whole == per:
+            part_copy(1).start()
         for p in range(3):
             fold_on(p)
         lax.fori_loop(first, 2 * tiles, gein_step, 0)
@@ -1028,8 +1030,10 @@
         gna_copy.start()
         dna_copy.start()
         return_part(2)
+        if whole == per:
+            return_part(1)
         mixed = shp[...].astype(f32)
-        for c in range(near // per):
+        for c in range(whole // per):
             for k in range(max(1, c * per), (c + 1) * per):
                 po_copy(k).wait_recv()
             mixed = mixed + dot_tn(gated_rows(c), near_ro[chunk_at(c), :])
@@ -1052,7 +1056,7 @@
 
         shp_copy.wait()
         mixed = shp[:, mine].astype(f32) + shpr[...].astype(f32)
-        for c in range(near // per, chunks):
+        for c in range(whole // per, chunks):
             for k in range(c * per, (c + 1) * per):
                 po_half(k).wait_recv()
             mixed = mixed + dot_tn(gated_rows(c), ro[out_chunk(c), :])
@@ -1100,13 +1104,15 @@
     )
     for k in range(near, G):
         cot_pass(k).wait_send()
+    for k in range(whole, G):
         po_half(k).wait_send()
     for k in range(1, near):
         row_copy(k).wait_send()
+    for k in range(1, whole):
         po_copy(k).wait_send()
-    for k in range(per, near):
+    for k in range(per, whole):
         ret_half(k).wait_send()
-    for c in range(near // per, chunks):
+    for c in range(whole // per, chunks):
         part_copy(c).wait_send()
 
 
@@ -1175,7 +1181,7 @@
             pltpu.VMEM((S, D), bf16),
             pltpu.VMEM((S, D), bf16),
             pltpu.VMEM((S, D), bf16),
-            pltpu.VMEM((S // 2, D), bf16),
+            pltpu.VMEM((NEAR * C, D), bf16),
             pltpu.VMEM((S - 4 * C, half), bf16),
             pltpu.VMEM((4 * C, D), bf16),
             pltpu.VMEM((S - 4 * C, half), bf16),
@@ -1184,9 +1190,9 @@
             pltpu.VMEM((T, half), bf16),
             pltpu.VMEM((T, D), bf16),
             pltpu.VMEM((T, D), bf16),
-            pltpu.VMEM((S // 2, half), bf16),
-            pltpu.VMEM((S // 2, D), bf16),
-            pltpu.VMEM((S // 2, half), bf16),
+            pltpu.VMEM((S - WHOLE * C, half), bf16),
+            pltpu.VMEM((WHOLE * C, D), bf16),
+            pltpu.VMEM((S - WHOLE * C, half), bf16),
             pltpu.VMEM((T, half), bf16),
             pltpu.VMEM((8, D), f32),
             pltpu.VMEM((8, D), f32),
@@ -1207,7 +1213,7 @@
         norm_attn, norm_ffn, cont_lengths, routes.T, route_gates.T, tokens, w_qkv, w_attn_out, cotangent,
         shared_in, shared_out, expert_in, expert_out,
     )
-    steps = 4
+    steps = 2
 
     def rows_of(*dims):
         return pl.BlockSpec(dims, lambda i: (0,) * (len(dims) - 2) + (i, 0))

time: 208 us -> 190 us (0.913)
  Pallas kernels: 206 us -> 189 us
    pallas_call x1, Pallas kernels: 198 us -> 182 us  [fused(): pl.pallas_call(functools.partial(layer_kernel, G), out_shape=(shape((T, D...]
where the time goes in v6:
time: 190 us
  Pallas kernels  189 us (99%)
    pallas_call x1, Pallas kernels, fused(): pl.pallas_call(functools.partial(layer_kernel, G), out_shape=(shape((T, D...  182 us
    pallas_call x1, Pallas kernels, fused(): pl.pallas_call(functools.partial(finish_kernel, HL, F), grid=(steps,), ou...  7.07 us

profile of v6, /device:TPU:0, one launch (start us, length us, event | category | flops | bytes accessed | tf_op | source)
XLA Modules:
  0.0 189.5 jit_solution(8826041294160640909)
XLA Ops:
  0.6 181.6 %layer.1 = (bf16[576,768]{1,0:T(8,128)(2,1)}, bf16[576,768]{1,0:T(8,128)(2,1)}, f32[48,3072]{1,0:T(8,128)}, f32[48,1664]{1,0:T(8,128)}, bf16[2,4,2,2,48,1024]{5,...) custom-call(f32[768]{0:T(1024)} %na.1, f32[768]{0:T(1024)} %nf.1, s32[1,2]{1,0:T(1,128)} %lens.1, s32[2,576]{1,0:T(2,128)} %bitcast.8, ...), custom_call_target="tpu_custom_call" | custom-call | tf_op jit(solution)/shard_map/layer/pallas_call | solution.py:1155
  182.3 7.1 %finish.1 = (bf16[576,768]{1,0:T(8,128)(2,1)}, bf16[576,768]{1,0:T(8,128)(2,1)}, f32[3,48,384]{2,1,0:T(8,128)}, f32[48,384]{1,0:T(8,128)}, f32[1,48]{1,0:T(1,128...) custom-call(bf16[576,768]{1,0:T(8,128)(2,1)} %get-tuple-element.26.h, ...), custom_call_target="tpu_custom_call" | custom-call | tf_op jit(solution)/shard_map/finish/pallas_call | solution.py:1225

commit v7 on v6

--- a/solution.py
+++ b/solution.py
@@ -719,7 +719,7 @@
 
         lax.fori_loop(0, G - near, far_step, 0)
         lax.fori_loop(0, near, near_step, 0)
-        for k in range(G - 1, near - 1, -1):
+        for k in range(G - 1, G - 5, -1):
             cot_hand_on(k)
 
         mid = slice(M, M + T)
@@ -819,6 +819,8 @@
         weights[0].wait()
         weights[1].wait()
         lax.fori_loop(0, tiles, shared_step, 0)
+        for k in range(G - 5, near - 1, -1):
+            cot_hand_on(k)
         dnsh[...] = (dot_nt(dgu[0, mid, :], vsi[0]) + dot_nt(dgu[1, mid, :], vsi[1])).astype(bf16)
         weights[2].wait()
         weights[3].wait()

time: 190 us -> 190 us (level)
  no operation moved by 1% of the time
where the time goes in v7:
time: 190 us
  Pallas kernels  189 us (99%)
    pallas_call x1, Pallas kernels, fused(): pl.pallas_call(functools.partial(layer_kernel, G), out_shape=(shape((T, D...  182 us
    pallas_call x1, Pallas kernels, fused(): pl.pallas_call(functools.partial(finish_kernel, HL, F), grid=(steps,), ou...  7.07 us

profile of v7, /device:TPU:0, one launch (start us, length us, event | category | flops | bytes accessed | tf_op | source)
XLA Modules:
  0.0 189.5 jit_solution(4981395350276832657)
XLA Ops:
  0.6 181.6 %layer.1 = (bf16[576,768]{1,0:T(8,128)(2,1)}, bf16[576,768]{1,0:T(8,128)(2,1)}, f32[48,3072]{1,0:T(8,128)}, f32[48,1664]{1,0:T(8,128)}, bf16[2,4,2,2,48,1024]{5,...) custom-call(f32[768]{0:T(1024)} %na.1, f32[768]{0:T(1024)} %nf.1, s32[1,2]{1,0:T(1,128)} %lens.1, s32[2,576]{1,0:T(2,128)} %bitcast.8, ...), custom_call_target="tpu_custom_call" | custom-call | tf_op jit(solution)/shard_map/layer/pallas_call | solution.py:1157
  182.3 7.1 %finish.1 = (bf16[576,768]{1,0:T(8,128)(2,1)}, bf16[576,768]{1,0:T(8,128)(2,1)}, f32[3,48,384]{2,1,0:T(8,128)}, f32[48,384]{1,0:T(8,128)}, f32[1,48]{1,0:T(1,128...) custom-call(bf16[576,768]{1,0:T(8,128)(2,1)} %get-tuple-element.26.h, ...), custom_call_target="tpu_custom_call" | custom-call | tf_op jit(solution)/shard_map/finish/pallas_call | solution.py:1227
